TPU v7x, 32 devices: a whole 2x2x4 slice. The times are simulated.
32 devices in a mesh: section: 4 (over y, x), batch: 8 (over z, core).
Axes of the slice: x: 2, y: 2, z: 4, core: 2. Of those that a mesh axis runs over, the one named last changes fastest.
Arguments:
- images: bfloat16 [4, 2048, 512], P(None, 'batch'), may hold values from -6 to 6
- crop_big: int32 [4, 8], P(None, 'batch'), may hold values from 0 to 2
- w_point: float32 [4, 512, 512], P('section', 'batch')
- w_spatial: float32 [4, 9, 512, 512], P('section', None, 'batch')
- norm_params: float32 [4, 4, 512], P('section'), as said below
- mom_point: float32 [4, 512, 512], P('section', 'batch'), may hold values from -0.078125 to 0.078125
- mom_spatial: float32 [4, 9, 512, 512], P('section', None, 'batch'), may hold values from -0.02734375 to 0.02734375
- mom_norm: float32 [4, 4, 512], P('section'), may hold values from -0.4375 to 0.4375
- out_grad: bfloat16 [4, 2048, 512], P(None, 'batch'), may hold values from -6 to 6
Outputs:
- features: float32 [4, 2048, 512], P('section', 'batch')
- in_grad: float32 [4, 2048, 512], P('section', 'batch')
- new_point: float32 [4, 512, 512], P('section', 'batch')
- new_spatial: float32 [4, 9, 512, 512], P('section', None, 'batch')
- new_norm: float32 [4, 4, 512], P('section')
- new_mom_point: float32 [4, 512, 512], P('section', 'batch')
- new_mom_spatial: float32 [4, 9, 512, 512], P('section', None, 'batch')
- new_mom_norm: float32 [4, 4, 512], P('section')
Inputs may be any that keep to these rules, and one draw needn't show every extreme that they name: `crop_big`: each value is the number of big crops at the head of one device's 256 rows of one micro-batch; small crops fill the rows after them as described. `norm_params`: rows 0 and 2 are gains, rows 1 and 3 shifts.
All inputs are finite; a program needn't handle non-finite values.
Results may differ from a plain program's by a relative error of at most 0.02.
Values may be sent and summed in bfloat16 or wider, within the bound.
A program may use at most 256 MiB of HBM per device.

v0:
```python
import jax
import jax.numpy as jnp
from jax import lax
from jax.sharding import PartitionSpec as P

BIG_SIDE = 7
SMALL_SIDE = 3
WARMUP = 20
STEP = 9


EPS = 1e-05
EPS_NORM = 1e-06
BASE_RATE = 6.0
MOMENTUM = 0.9
TRUST_COEF = 0.1


def from_behind(block, axis, distance):
    devices = range(lax.axis_size(axis))
    route = [(i - distance, i) for i in devices if i - distance in devices]
    return lax.ppermute(block, axis, route)


def crop_table(big_count, total_rows):
    places = jnp.arange(total_rows, dtype=jnp.int32)
    big_area = BIG_SIDE * BIG_SIDE
    small_area = SMALL_SIDE * SMALL_SIDE
    big_rows = big_count * big_area
    small_rows = (total_rows - big_rows) // small_area * small_area
    in_big = places < big_rows
    offsets = places - big_rows
    sides = jnp.where(in_big, BIG_SIDE, SMALL_SIDE)
    within = jnp.where(in_big, places % big_area, offsets % small_area)
    starts = places - within
    valid_rows = places < big_rows + small_rows
    row_pos = within // sides
    col_pos = within % sides
    indices = []
    masks = []
    for row_step in (-1, 0, 1):
        for col_step in (-1, 0, 1):
            new_row = row_pos + row_step
            new_col = col_pos + col_step
            inside = (
                valid_rows & (new_row >= 0) & (new_row < sides) & (new_col >= 0) & (new_col < sides)
            )
            indices.append(jnp.where(inside, starts + new_row * sides + new_col, places))
            masks.append(inside)
    return (
        jnp.stack(indices, 1),
        jnp.stack(masks, 1).astype(jnp.float32),
        valid_rows.astype(jnp.float32),
    )


def mish(values):
    return values * jnp.tanh(jax.nn.softplus(values))


def mish_parts(values):
    tangent = jnp.tanh(jax.nn.softplus(values))
    slope = tangent + values * jax.nn.sigmoid(values) * (1.0 - tangent * tangent)
    return (values * tangent, slope)


def mish_slope(values):
    tangent = jnp.tanh(jax.nn.softplus(values))
    return tangent + values * jax.nn.sigmoid(values) * (1.0 - tangent * tangent)


def batch_moments(proj, valid_rows):
    weighted = valid_rows[:, None] * proj
    summed, squared, row_count = lax.psum(
        (jnp.sum(weighted, 0), jnp.sum(weighted * proj, 0), jnp.sum(valid_rows)), "batch"
    )
    center = summed / row_count
    inv_std = lax.rsqrt(squared / row_count - center * center + EPS)
    return (center, inv_std, row_count)


def spatial_apply(source, tap_index, tap_mask, weights):
    stacked = source[tap_index] * tap_mask[:, :, None].astype(source.dtype)
    result = lax.dot_general(
        stacked, weights, (((1, 2), (0, 1)), ((), ())), preferred_element_type=jnp.float32
    )
    return (result, stacked)


def forward_block(hidden, point_low, spatial_low, affine, tap_index, tap_mask, valid_rows):
    proj_one = jnp.dot(hidden.astype(jnp.bfloat16), point_low, preferred_element_type=jnp.float32)
    center_one, inv_one, row_count = batch_moments(proj_one, valid_rows)
    mixed_one = mish(affine[0] * ((proj_one - center_one) * inv_one) + affine[1])
    proj_two, stacked = spatial_apply(
        mixed_one.astype(jnp.bfloat16), tap_index, tap_mask, spatial_low
    )
    center_two, inv_two, count_two = batch_moments(proj_two, valid_rows)
    mixed_two = mish(affine[2] * ((proj_two - center_two) * inv_two) + affine[3])
    moments = jnp.stack([center_one, inv_one, center_two, inv_two])
    return (hidden + valid_rows[:, None] * mixed_two, moments, row_count)


def norm_back(d_value, normed, inv_std, gain, valid_rows, row_count):
    first_sum, second_sum = lax.psum((jnp.sum(d_value, 0), jnp.sum(d_value * normed, 0)), "batch")
    d_proj = (
        gain
        * inv_std
        * (d_value - valid_rows[:, None] * (first_sum + normed * second_sum) / row_count)
    )
    return (d_proj.astype(jnp.bfloat16), first_sum, second_sum)


def backward_block(
    hidden,
    upstream,
    point_low,
    spatial_low,
    affine,
    moments,
    row_count,
    tap_index,
    tap_mask,
    valid_rows,
):
    inputs = hidden.astype(jnp.bfloat16)
    proj_one = jnp.dot(inputs, point_low, preferred_element_type=jnp.float32)
    normed_one = (proj_one - moments[0]) * moments[1]
    mixed_one, slope_one = mish_parts(affine[0] * normed_one + affine[1])
    proj_two, stacked = spatial_apply(
        mixed_one.astype(jnp.bfloat16), tap_index, tap_mask, spatial_low
    )
    normed_two = (proj_two - moments[2]) * moments[3]
    slope_two = mish_slope(affine[2] * normed_two + affine[3])
    d_two, first_two, second_two = norm_back(
        valid_rows[:, None] * upstream * slope_two,
        normed_two,
        moments[3],
        affine[2],
        valid_rows,
        row_count,
    )
    grad_spatial = lax.dot_general(
        stacked, d_two, (((0,), (0,)), ((), ())), preferred_element_type=jnp.float32
    )
    flipped = d_two[tap_index[:, ::-1]] * tap_mask[:, ::-1, None].astype(jnp.bfloat16)
    d_mixed = lax.dot_general(
        flipped, spatial_low, (((1, 2), (0, 2)), ((), ())), preferred_element_type=jnp.float32
    )
    d_one, first_one, second_one = norm_back(
        d_mixed * slope_one, normed_one, moments[1], affine[0], valid_rows, row_count
    )
    grad_point = lax.dot_general(
        inputs, d_one, (((0,), (0,)), ((), ())), preferred_element_type=jnp.float32
    )
    d_hidden = upstream + lax.dot_general(
        d_one, point_low, (((1,), (1,)), ((), ())), preferred_element_type=jnp.float32
    )
    grad_affine = jnp.stack([second_one, first_one, second_two, first_two])
    return (d_hidden, grad_point, grad_spatial, grad_affine)


def store_slot(buffer, value, slot_index, active):
    previous = lax.dynamic_index_in_dim(buffer, slot_index, 0, keepdims=False)
    return lax.dynamic_update_index_in_dim(
        buffer, jnp.where(active, value, previous), slot_index, 0
    )


def lars_update(param, grad, momentum, param_sq, grad_sq, rate):
    trust = TRUST_COEF * jnp.sqrt(param_sq) / (jnp.sqrt(grad_sq) + EPS_NORM)
    new_mom = MOMENTUM * momentum + rate * trust * grad
    return (param - new_mom, new_mom)


def on_device(
    images, crop_big, w_point, w_spatial, norm_params, mom_point, mom_spatial, mom_norm, out_grad
):
    section_count = lax.axis_size("section")
    section_rank = lax.axis_index("section")
    micro_count = images.shape[0]
    total_rows = images.shape[1]
    width = images.shape[2]
    point = w_point[0]
    spatial = w_spatial[0]
    affine = norm_params[0]
    crop_counts = crop_big[:, 0]
    turns = micro_count + section_count - 1
    point_low, spatial_low = (
        lax.all_gather(point.astype(jnp.bfloat16), "batch", axis=0, tiled=True),
        lax.all_gather(spatial.astype(jnp.bfloat16), "batch", axis=1, tiled=True),
    )
    kept_inputs = jnp.zeros((micro_count, total_rows, width), jnp.float32)
    kept_moments = jnp.zeros((micro_count, 4, width), jnp.float32)
    kept_counts = jnp.zeros((micro_count,), jnp.float32)
    results = jnp.zeros((micro_count, total_rows, width), jnp.float32)
    incoming = jnp.zeros((total_rows, width), jnp.float32)
    for phase_turn in range(turns):
        slot_raw = phase_turn - section_rank
        active = (slot_raw >= 0) & (slot_raw < micro_count)
        slot_index = jnp.clip(slot_raw, 0, micro_count - 1)
        fresh_rows = lax.dynamic_index_in_dim(images, slot_index, 0, keepdims=False).astype(
            jnp.float32
        )
        hidden = jnp.where(section_rank == 0, fresh_rows, incoming)
        tap_index, tap_mask, valid_rows = crop_table(crop_counts[slot_index], total_rows)
        output, moments, row_count = forward_block(
            hidden, point_low, spatial_low, affine, tap_index, tap_mask, valid_rows
        )
        kept_inputs = store_slot(kept_inputs, hidden, slot_index, active)
        kept_moments = store_slot(kept_moments, moments, slot_index, active)
        kept_counts = store_slot(kept_counts, row_count, slot_index, active)
        results = store_slot(
            results, output, slot_index, active & (section_rank == section_count - 1)
        )
        if phase_turn + 1 < turns:
            incoming = from_behind(output.astype(jnp.bfloat16), "section", 1).astype(output.dtype)
    point_low, spatial_low = (
        lax.all_gather(point.astype(jnp.bfloat16), "batch", axis=0, tiled=True),
        lax.all_gather(spatial.astype(jnp.bfloat16), "batch", axis=1, tiled=True),
    )
    grad_point = jnp.zeros((width, width), jnp.float32)
    grad_spatial = jnp.zeros((9, width, width), jnp.float32)
    grad_affine = jnp.zeros((4, width), jnp.float32)
    collected = jnp.zeros((micro_count, total_rows, width), jnp.float32)
    returning = jnp.zeros((total_rows, width), jnp.float32)
    for phase_turn in range(turns):
        slot_raw = micro_count - 1 - phase_turn + (section_count - 1 - section_rank)
        active = (slot_raw >= 0) & (slot_raw < micro_count)
        slot_index = jnp.clip(slot_raw, 0, micro_count - 1)
        seeded = lax.dynamic_index_in_dim(out_grad, slot_index, 0, keepdims=False).astype(
            jnp.float32
        )
        upstream = jnp.where(section_rank == section_count - 1, seeded, returning)
        upstream = jnp.where(active, upstream, 0.0)
        tap_index, tap_mask, valid_rows = crop_table(crop_counts[slot_index], total_rows)
        hidden = lax.dynamic_index_in_dim(kept_inputs, slot_index, 0, keepdims=False)
        moments = lax.dynamic_index_in_dim(kept_moments, slot_index, 0, keepdims=False)
        row_count = lax.dynamic_index_in_dim(kept_counts, slot_index, 0, keepdims=False)
        d_hidden, part_point, part_spatial, part_affine = backward_block(
            hidden,
            upstream,
            point_low,
            spatial_low,
            affine,
            moments,
            row_count,
            tap_index,
            tap_mask,
            valid_rows,
        )
        grad_point = grad_point + part_point
        grad_spatial = grad_spatial + part_spatial
        grad_affine = grad_affine + part_affine
        collected = store_slot(collected, d_hidden, slot_index, active & (section_rank == 0))
        if phase_turn + 1 < turns:
            returning = from_behind(d_hidden.astype(jnp.bfloat16), "section", -1).astype(
                d_hidden.dtype
            )
    point_grad, spatial_grad = (
        lax.psum_scatter(grad_point, "batch", scatter_dimension=0, tiled=True),
        lax.psum_scatter(grad_spatial, "batch", scatter_dimension=1, tiled=True),
    )
    point_sq, spatial_sq, gpoint_sq, gspatial_sq = lax.psum(
        (
            jnp.sum(point * point),
            jnp.sum(spatial * spatial),
            jnp.sum(point_grad * point_grad),
            jnp.sum(spatial_grad * spatial_grad),
        ),
        "batch",
    )
    rate = BASE_RATE * (STEP + 1) / WARMUP
    new_point, new_mom_point = lars_update(
        point, point_grad, mom_point[0], point_sq, gpoint_sq, rate
    )
    new_spatial, new_mom_spatial = lars_update(
        spatial, spatial_grad, mom_spatial[0], spatial_sq, gspatial_sq, rate
    )
    affine_sq = jnp.sum(affine * affine, 1, keepdims=True)
    gaffine_sq = jnp.sum(grad_affine * grad_affine, 1, keepdims=True)
    new_affine, new_mom_affine = lars_update(
        affine, grad_affine, mom_norm[0], affine_sq, gaffine_sq, rate
    )
    sent_out = jnp.where(section_rank == section_count - 1, results, 0.0)
    sent_back = jnp.where(section_rank == 0, collected, 0.0)
    got_out, got_back = (
        lax.all_to_all(
            sent_out.astype(jnp.bfloat16), "section", split_axis=0, concat_axis=0, tiled=True
        ).astype(sent_out.dtype),
        lax.all_to_all(
            sent_back.astype(jnp.bfloat16), "section", split_axis=0, concat_axis=0, tiled=True
        ).astype(sent_back.dtype),
    )
    features = got_out[section_count - 1 : section_count]
    in_grad = got_back[0:1]
    return (
        features,
        in_grad,
        new_point[None],
        new_spatial[None],
        new_affine[None],
        new_mom_point[None],
        new_mom_spatial[None],
        new_mom_affine[None],
    )


def solution(mesh):
    return jax.shard_map(
        on_device,
        mesh=mesh,
        in_specs=(
            P(None, "batch", None),
            P(None, "batch"),
            P("section", "batch", None),
            P("section", None, "batch", None),
            P("section", None, None),
            P("section", "batch", None),
            P("section", None, "batch", None),
            P("section", None, None),
            P(None, "batch", None),
        ),
        out_specs=(
            P("section", "batch", None),
            P("section", "batch", None),
            P("section", "batch", None),
            P("section", None, "batch", None),
            P("section", None, None),
            P("section", "batch", None),
            P("section", None, "batch", None),
            P("section", None, None),
        ),
        check_vma=False,
    )
```

profile of v0, /device:TPU:0, one launch (start us, length us, event | category | flops | bytes accessed | tf_op | source)
XLA Modules:
  0.0 1434.9 jit_solution(16824565091797944551)
XLA Ops:
  72.7 16.6 %all_gather.8 = bf16[512,512]{1,0:T(8,128)(2,1)S(1)} all-gather(bf16[64,512]{1,0:T(8,128)(2,1)S(1)} %bitcast_convert_fusion.3), channel_id=1, replica_groups=mesh['section'=4,'batch'=8] {'batch'}, dimensions={0}, use_global_device_ids=true | all-gather | bytes 589824 | tf_op jit(solution)/shard_map/all_gather | solution.py:189
  90.6 17.8 %all-reduce.28 = (f32[512]{0:T(512)S(1)}, f32[]{:T(128)}, f32[512]{0:T(512)S(1)}) all-reduce(f32[512]{0:T(512)S(1)} %get-tuple-element.35, f32[]{:T(128)} %fusion.325, f32[512]{0:T(512)S(1)} %get-tuple-element.34), channel_id=1, replica_groups=mesh['section'=4,'batch'=8] {'batch'}, use_global_device_ids=true, to_apply=%region_5.6 | all-reduce | flops 1025 | bytes 8200 | tf_op jit(solution)/shard_map/psum | solution.py:74
  138.9 13.7 all-reduce.27
  166.5 14.4 %all-reduce.26 = (f32[512]{0:T(512)S(1)}, f32[]{:T(128)}, f32[512]{0:T(512)S(1)}) all-reduce(f32[512]{0:T(512)S(1)} %get-tuple-element.31, f32[]{:T(128)} %fusion.326, f32[512]{0:T(512)S(1)} %get-tuple-element.30), channel_id=1, replica_groups=mesh['section'=4,'batch'=8] {'batch'}, use_global_device_ids=true, to_apply=%region_15.16 | all-reduce | flops 1025 | bytes 8200 | tf_op jit(solution)/shard_map/psum | solution.py:74
  204.6 14.0 all-reduce.25
  234.1 14.4 %all-reduce.24 = (f32[512]{0:T(512)S(1)}, f32[]{:T(128)}, f32[512]{0:T(512)S(1)}) all-reduce(f32[512]{0:T(512)S(1)} %get-tuple-element.27, f32[]{:T(128)} %fusion.327, f32[512]{0:T(512)S(1)} %get-tuple-element.26), channel_id=1, replica_groups=mesh['section'=4,'batch'=8] {'batch'}, use_global_device_ids=true, to_apply=%region_25.26 | all-reduce | flops 1025 | bytes 8200 | tf_op jit(solution)/shard_map/psum | solution.py:74
  301.2 14.6 %all-reduce.22 = (f32[512]{0:T(512)S(1)}, f32[]{:T(128)}, f32[512]{0:T(512)S(1)}) all-reduce(f32[512]{0:T(512)S(1)} %get-tuple-element.23, f32[]{:T(128)} %fusion.328, f32[512]{0:T(512)S(1)} %get-tuple-element.22), channel_id=1, replica_groups=mesh['section'=4,'batch'=8] {'batch'}, use_global_device_ids=true, to_apply=%region_35.36 | all-reduce | flops 1025 | bytes 8200 | tf_op jit(solution)/shard_map/psum | solution.py:74
  370.2 14.6 %all-reduce.20 = (f32[512]{0:T(512)}, f32[]{:T(128)}, f32[512]{0:T(512)}) all-reduce(f32[512]{0:T(512)} %get-tuple-element.19, f32[]{:T(128)} %fusion.329, f32[512]{0:T(512)} %get-tuple-element.18), channel_id=1, replica_groups=mesh['section'=4,'batch'=8] {'batch'}, use_global_device_ids=true, to_apply=%region_45.46 | all-reduce | flops 1025 | bytes 8200 | tf_op jit(solution)/shard_map/psum | solution.py:74
  410.3 14.3 all-reduce.19
  442.4 14.6 %all-reduce.18 = (f32[512]{0:T(512)}, f32[]{:T(128)}, f32[512]{0:T(512)}) all-reduce(f32[512]{0:T(512)} %get-tuple-element.15, f32[]{:T(128)} %fusion.330, f32[512]{0:T(512)} %get-tuple-element.14), channel_id=1, replica_groups=mesh['section'=4,'batch'=8] {'batch'}, use_global_device_ids=true, to_apply=%region_55.56 | all-reduce | flops 1025 | bytes 8200 | tf_op jit(solution)/shard_map/psum | solution.py:74
  482.6 14.3 all-reduce.17
  514.4 14.6 %all-reduce.16 = (f32[512]{0:T(512)}, f32[]{:T(128)}, f32[512]{0:T(512)}) all-reduce(f32[512]{0:T(512)} %get-tuple-element.11, f32[]{:T(128)} %fusion.331, f32[512]{0:T(512)} %get-tuple-element.10), channel_id=1, replica_groups=mesh['section'=4,'batch'=8] {'batch'}, use_global_device_ids=true, to_apply=%region_65.66 | all-reduce | flops 1025 | bytes 8200 | tf_op jit(solution)/shard_map/psum | solution.py:74
  558.6 14.7 %all-reduce.15 = (f32[512]{0:T(512)}, f32[512]{0:T(512)}) all-reduce(f32[512]{0:T(512)} %get-tuple-element.9, f32[512]{0:T(512)} %get-tuple-element.8), channel_id=1, replica_groups=mesh['section'=4,'batch'=8] {'batch'}, use_global_device_ids=true, to_apply=%region_69.70 | all-reduce | flops 1024 | bytes 8192 | tf_op jit(solution)/shard_map/psum | solution.py:74
  631.2 13.7 all-reduce.14
  830.8 13.8 all-reduce.12
  908.9 14.1 all-reduce.10
  988.9 13.8 all-reduce.8
  1030.9 13.7 all-reduce.7
  1065.8 13.8 all-reduce.6
  1142.8 13.9 all-reduce.4
  1218.1 14.1 all-reduce.2
  1272.3 23.7 %add_add_fusion = f32[9,512,512]{2,1,0:T(8,128)} fusion(f32[9,512,512]{2,1,0:T(8,128)} %fusion.238, f32[9,512,512]{2,1,0:T(8,128)} %fusion.240, f32[9,512,512]{2,1,0:T(8,128)} %fusion.242, f32[9,512,512]{2,1,0:T(8,128)} %fusion.244, f32[9,512,512]{2,1,0:T(8,128)} %fusion.248, f32[9,512,512]{2,1,0:T(8,128)} %fusion.246, bf16[256,9,512]{0,2,1:T(8,128)(2,1)} %copy.198, ...), kind=kOutput, calls=%fused_computation.21 | convolution fusion | flops 1222115328 | bytes 68681728 | tf_op jit(solution)/shard_map/dot_general | solution.py:142
  1328.9 74.3 %reduce-scatter.5.cloned.1.call-done = f32[9,64,512]{2,1,0:T(8,128)} async-done(((f32[9,512,512]{2,1,0:T(8,128)}), f32[9,64,512]{2,1,0:T(8,128)}) %reduce-scatter.5.cloned.1.call-update) | async-done | bytes 1179664 | tf_op jit(solution)/shard_map/reduce_scatter | solution.py:261
  1406.3 14.2 all-reduce
  (947 shorter events, 986.9 us)
Async XLA Ops:
  7.2 125.2 %all-gather.2.cloned.1.call-start = ((), (), s32[]{:S(2)}) async-start(), calls=%async_computation.4 | async-start | bytes 5308416 | tf_op jit(solution)/shard_map/all_gather | solution.py:190
  9.4 1317.9 %reduce-scatter.3.cloned.1.call-start = ((), (), s32[]{:S(2)}) async-start(), calls=%async_computation.5 | async-start | bytes 1179648 | tf_op jit(solution)/shard_map/reduce_scatter | solution.py:260
  46.1 64.5 %copy-start.93 = (f32[1,4,512]{2,1,0:T(4,128)S(1)}, f32[1,4,512]{2,1,0:T(4,128)}, u32[]{:S(2)}) copy-start(f32[1,4,512]{2,1,0:T(4,128)} %param.13) | copy-start | bytes 24580
  122.3 231.5 %copy-start.145 = (f32[256]{0:T(256)}, f32[256]{0:T(256)S(1)}, u32[]{:S(2)}) copy-start(f32[256]{0:T(256)S(1)} %compare_convert_fusion.3) | copy-start | bytes 3076
  122.3 164.0 %copy-start.143 = (f32[256]{0:T(256)}, f32[256]{0:T(256)S(1)}, u32[]{:S(2)}) copy-start(f32[256]{0:T(256)S(1)} %compare_convert_fusion.4) | copy-start | bytes 3076
  122.4 96.8 %copy-start.141 = (f32[256]{0:T(256)}, f32[256]{0:T(256)S(1)}, u32[]{:S(2)}) copy-start(f32[256]{0:T(256)S(1)} %compare_convert_fusion.5) | copy-start | bytes 3076
  127.2 123.3 %copy-start.10 = (s32[3072]{0:T(1024)}, s32[3072]{0:T(1024)S(1)}, u32[]{:S(2)}) copy-start(s32[3072]{0:T(1024)S(1)} %get-tuple-element.385) | copy-start | bytes 36868
  127.2 190.7 %copy-start.12 = (s32[3072]{0:T(1024)}, s32[3072]{0:T(1024)S(1)}, u32[]{:S(2)}) copy-start(s32[3072]{0:T(1024)S(1)} %get-tuple-element.384) | copy-start | bytes 36868
  154.7 9.0 collective-permute-start
  221.7 10.2 collective-permute-start.1
  288.9 10.2 collective-permute-start.2
  356.3 11.1 collective-permute-start.3
  428.4 11.3 collective-permute-start.4
  500.6 11.1 collective-permute-start.5
  694.7 130.9 %collective-permute-start.6 = (bf16[256,512]{1,0:T(8,128)(2,1)}, bf16[256,512]{1,0:T(8,128)(2,1)S(1)}, u32[]{:S(2)}, u32[]{:S(2)}) collective-permute-start(bf16[256,512]{1,0:T(8,128)(2,1)} %get-tuple-element.288), channel_id=1, source_target_pairs={{8,0},{16,8},{24,16},{9,1},{17,9},{25,17},{10,2},{18,10},{26,18},{... | collective-permute-start | bytes 786440 | tf_op jit(solution)/shard_map/ppermute | solution.py:22
  891.7 12.1 collective-permute-start.7
  972.9 11.5 collective-permute-start.8
  1050.4 10.9 collective-permute-start.9
  1127.4 10.9 collective-permute-start.10
  1202.7 10.9 collective-permute-start.11
  1272.2 131.0 %reduce-scatter.5.cloned.1.call-start = ((), (), s32[]{:S(2)}) async-start(), calls=%async_computation.6 | async-start | bytes 10616832 | tf_op jit(solution)/shard_map/reduce_scatter | solution.py:261
  1299.4 18.4 %all-to-all-start = ((bf16[4,256,512]{2,1,0:T(8,128)(2,1)}), bf16[4,256,512]{2,1,0:T(8,128)(2,1)S(1)}, u32[]{:S(2)}, u32[]{:S(2)}) async-start(bf16[4,256,512]{2,1,0:T(8,128)(2,1)} %select_convert_fusion.1), calls=%async_computation | async-start | bytes 2097152 | tf_op jit(solution)/shard_map/all_to_all | solution.py:287
  1307.7 117.3 %copy-start.41 = (f32[1,9,64,512]{3,2,1,0:T(8,128)S(1)}, f32[1,9,64,512]{3,2,1,0:T(8,128)}, u32[]{:S(2)}) copy-start(f32[1,9,64,512]{3,2,1,0:T(8,128)} %param.15) | copy-start | bytes 3538948
  1318.8 86.6 %all-to-all-start.1 = ((bf16[4,256,512]{2,1,0:T(8,128)(2,1)}), bf16[4,256,512]{2,1,0:T(8,128)(2,1)S(1)}, u32[]{:S(2)}, u32[]{:S(2)}) async-start(bf16[4,256,512]{2,1,0:T(8,128)(2,1)} %select_convert_fusion), calls=%async_computation.1 | async-start | bytes 2097152 | tf_op jit(solution)/shard_map/all_to_all | solution.py:290
  (191 other events, 2629.4 us)
Sparse Core Ops, SparseCore 0:
  10.2 54.4 all-gather.1
  1272.3 30.7 reduce-scatter.2
  1305.5 97.7 reduce-scatter.4
where the time goes:
time: 1450 us; the launch traced here: 1430 us
  blocking collectives  427 us (29%)
  local copies, waits for them, and re-layouts  367 us (25%)
  matrix products  226 us (16%)
  other arithmetic  198 us (14%)
  waiting for transfers between devices  141 us (10%)
  starting transfers between devices  43.4 us (3%)
  between operations  32.3 us (2%)
    psum x14, blocking collectives, batch_moments(): lax.psum((jnp.sum(weighted, 0), jnp.sum(weighted * proj, 0), jnp.sum(vali...  203 us
    psum x14, blocking collectives, norm_back(): lax.psum((jnp.sum(d_value, 0), jnp.sum(d_value * normed, 0)), 'batch')  193 us
    gather x28, local copies, waits for them, and re-layouts, spatial_apply(): stacked = source[tap_index] * tap_mask[:, :, None].astype(source.dtype)  177 us
    gather x14, local copies, waits for them, and re-layouts, backward_block(): d_two[tap_index[:, ::-1]] * tap_mask[:, ::-1, None].astype(jnp.bfloat16)  90.3 us
    dot_general x14, matrix products, spatial_apply(): lax.dot_general(stacked, weights, (((1, 2), (0, 1)), ((), ())), preferred...  79.3 us
    reduce_scatter x1, waiting for transfers between devices, on_device(): lax.psum_scatter(grad_spatial, 'batch', scatter_dimension=1, tiled=True)  74.3 us
    dot_general x7, matrix products, backward_block(): lax.dot_general(stacked, d_two, (((0,), (0,)), ((), ())), preferred_eleme...  63.8 us
    ppermute x12, waiting for transfers between devices, from_behind(): return lax.ppermute(block, axis, route)  59.2 us
  transfers between devices with their start and end apart: 17, of which 13 were waited for; matrix products, arithmetic and copies ran while one was open for 19% of the time, Pallas kernels for 0%

commit v1 on v0

--- a/solution.py
+++ b/solution.py
@@ -1,6 +1,8 @@
 import jax
 import jax.numpy as jnp
 from jax import lax
+from jax.experimental import pallas as pl
+from jax.experimental.pallas import tpu as pltpu
 from jax.sharding import PartitionSpec as P
 
 BIG_SIDE = 7
@@ -305,9 +307,763 @@
     )
 
 
+def swap_copy(source, target, sent, landed, section, batch):
+    return pltpu.make_async_remote_copy(
+        src_ref=source,
+        dst_ref=target,
+        send_sem=sent,
+        recv_sem=landed,
+        device_id=(section, batch),
+        device_id_type=pl.DeviceIdType.MESH,
+    )
+
+
+def drain(like, sem):
+    pltpu.make_async_copy(like, like, sem).wait()
+
+
+def mish_terms(v):
+    e = jnp.exp(jnp.minimum(v, 20.0))
+    w = e * (e + 2.0)
+    r = 1.0 / (w + 2.0)
+    t = w * r
+    return v * t, t + v * (4.0 * e * (1.0 + e)) * (r * r)
+
+
+def pack(first, second):
+    parts = [v[:, i * 128 : (i + 1) * 128] for v in (first, second) for i in range(4)]
+    return jnp.concatenate(parts, axis=0)
+
+
+def unpack(tile):
+    rows = [tile[i : i + 1] for i in range(8)]
+    return jnp.concatenate(rows[:4], axis=1), jnp.concatenate(rows[4:], axis=1)
+
+
+def crop_codes(places, big, total_rows):
+    big_area = float(BIG_SIDE * BIG_SIDE)
+    small_area = float(SMALL_SIDE * SMALL_SIDE)
+    big_rows = big * big_area
+    small_rows = jnp.floor((total_rows - big_rows + 0.5) / small_area) * small_area
+    in_big = places < big_rows
+    offset = jnp.where(in_big, places, places - big_rows)
+    area = jnp.where(in_big, big_area, small_area)
+    side = jnp.where(in_big, float(BIG_SIDE), float(SMALL_SIDE))
+    crop = jnp.floor((offset + 0.5) / area)
+    within = offset - crop * area
+    row = jnp.floor((within + 0.5) / side)
+    col = within - row * side
+    crop = jnp.where(in_big, crop, crop + big)
+    return crop * 1024.0 + (row + 1.0) * 32.0 + (col + 1.0), places < big_rows + small_rows
+
+
+NT = (((1,), (1,)), ((), ()))
+TAPS = 10
+HALF = 5
+
+
+def train_kernel(
+    images, crop, w_point, w_spatial, norm_in, mom_point, mom_spatial, mom_norm, out_grad,
+    features, in_grad, new_point, new_spatial, new_norm, new_mom_point, new_mom_spatial,
+    new_mom_norm,
+    W, wown, pbuf, mbuf, h, g, zbuf, sv, gi, abuf, gbuf, Gm, caq, stage, Hb, GcT, dzq, gout, yrecv,
+    zs1, zrecv, fin, gfin, aff, gaff, gsend, st_in, st_own, st_all, cnt, cntx, cown,
+    sL, sS_s, sS_r, sZ_s, sZ_r, sH_s, sH_r, sA_s, sA_r, sB_s, sB_r, sD_s, sD_r,
+    sE_in_s, sE_in_r, sE_s, sE_r, sC_s, sC_r, sF_s, sF_r, sQ_s, sQ_r, sX_s, sX_r,
+    sY_s, sY_r, sK_s, sK_r, sR_s, sR_r, sG_s, sG_r, sO_s, sO_r, sW,
+):
+    s = lax.axis_index("section")
+    bat = lax.axis_index("batch")
+    z = bat // 2
+    c = lax.rem(bat, 2)
+    x = lax.rem(s, 2)
+    y = s // 2
+    u = 2 * x + c
+    R, D = h.shape
+
+    loads = [
+        pltpu.make_async_copy(w_point.at[0], pbuf.at[9], sL.at[0]),
+        pltpu.make_async_copy(w_spatial.at[0], pbuf.at[pl.ds(0, 9)], sL.at[1]),
+        pltpu.make_async_copy(images.at[s], abuf, sL.at[2]),
+        pltpu.make_async_copy(out_grad.at[s], gbuf, sL.at[3]),
+        pltpu.make_async_copy(mom_point.at[0], mbuf.at[9], sL.at[4]),
+        pltpu.make_async_copy(mom_spatial.at[0], mbuf.at[pl.ds(0, 9)], sL.at[5]),
+    ]
+    for load in loads:
+        load.start()
+
+    barrier = pltpu.get_barrier_semaphore()
+    greet = [(s, bat ^ j) for j in range(1, 8)]
+    greet += [(s ^ d, bat ^ j) for d in range(1, 4) for j in range(2)]
+    for sec, other in greet:
+        pl.semaphore_signal(
+            barrier, inc=1, device_id=(sec, other), device_id_type=pl.DeviceIdType.MESH
+        )
+    pl.semaphore_wait(barrier, len(greet))
+
+    loads[0].wait()
+    loads[1].wait()
+    for k in range(TAPS):
+        wown[k] = pbuf[k].astype(jnp.bfloat16).reshape(4, 16, D)
+
+    def scatter(d):
+        q = s ^ d
+        return swap_copy(
+            wown.at[:, q], W.at[s, :, bat, q], sS_s.at[d], sS_r.at[s, c], q, 2 * z
+        )
+
+    for d in range(1, 4):
+        scatter(d).start()
+
+    @pl.when(c == 1)
+    def _():
+        scatter(0).start()
+
+    @pl.when(c == 0)
+    def _():
+        pltpu.make_async_copy(wown.at[:, s], W.at[s, :, bat, s], sS_r.at[s, c]).start()
+
+    cown[...] = jnp.full((8, 128), crop[s, 0].astype(jnp.float32))
+    aff[s] = jnp.concatenate([norm_in[0], jnp.zeros((4, D), jnp.float32)], axis=0)
+    cnt[bat] = cown[...]
+    cntx[u] = cown[...]
+    for j in range(1, 8):
+        swap_copy(cown, cnt.at[bat], sC_s.at[j], sC_r.at[bat], s, bat ^ j).start()
+    for j in range(2):
+        swap_copy(cown, cntx.at[u], sC_s.at[8 + j], sC_r.at[8 + u], s ^ 1, bat ^ j).start()
+    for d in range(1, 4):
+        swap_copy(aff.at[s], aff.at[s], sF_s.at[d], sF_r.at[s], s ^ d, bat).start()
+
+    half = pl.ds(HALF * c, HALF)
+    first = jnp.where(c == 0, s ^ 1, s ^ 2)
+    second = jnp.where(c == 0, s ^ 2, s ^ 1)
+    both = s ^ 3
+
+    def pair(b, taps, zz, q):
+        return W.at[b, taps, pl.ds(2 * zz, 2), q]
+
+    def to_sibling(b, zz):
+        ref = pair(b, slice(None), zz, s)
+        return swap_copy(ref, ref, sH_s.at[b, zz], sH_r.at[b, zz], s, bat ^ 1)
+
+    def along_first(b, zz):
+        ref = pair(b, half, zz, s)
+        return swap_copy(ref, ref, sA_s.at[b, zz], sA_r.at[b, zz], first, bat)
+
+    def along_second(b, which, zz):
+        ref = pair(b, half, zz, s if which == 0 else first)
+        return swap_copy(ref, ref, sB_s.at[b, which, zz], sB_r.at[b, which, zz], second, bat)
+
+    def quarter_to_sibling(b, which):
+        ref = W.at[b, half, :, (first, second, both)[which]]
+        return swap_copy(ref, ref, sD_s.at[b, which], sD_r.at[b, which], s, bat ^ 1)
+
+    def own_ready(b, zz):
+        @pl.when(c == 0)
+        def _():
+            to_sibling(b, zz).start()
+
+        @pl.when(c == 1)
+        def _():
+            to_sibling(b, zz).wait_recv()
+
+        along_first(b, zz).start()
+        along_second(b, 0, zz).start()
+
+    def spread_z(b, j):
+        ref = pair(b, slice(None), z, s)
+        return swap_copy(ref, ref, sZ_s.at[b, j], sZ_r.at[b, z], s, bat ^ (2 * j))
+
+    def from_z(b, zz):
+        ref = pair(b, slice(None), zz, s)
+        return swap_copy(ref, ref, sZ_s.at[b, 0], sZ_r.at[b, zz], s, bat)
+
+    @pl.loop(0, 4)
+    def _(b):
+        @pl.when(c == 0)
+        def _():
+            for cc in range(2):
+                drain(W.at[b, :, 2 * z + cc, s], sS_r.at[b, cc])
+            for j in range(1, 4):
+                spread_z(b, j).start()
+
+        own_ready(b, z)
+
+    def gather_z(b):
+        for j in range(1, 4):
+            zz = z ^ j
+
+            @pl.when(c == 0)
+            def _():
+                from_z(b, zz).wait_recv()
+
+            own_ready(b, zz)
+
+    def gather_first(b):
+        for j in range(4):
+            zz = z ^ j
+            ref = pair(b, half, zz, first)
+            swap_copy(ref, ref, sA_s.at[b, zz], sA_r.at[b, zz], first, bat).wait_recv()
+            along_second(b, 1, zz).start()
+        quarter_to_sibling(b, 0).start()
+
+    def gather_second(b):
+        for which in range(2):
+            q = (second, both)[which]
+            for j in range(4):
+                zz = z ^ j
+                ref = pair(b, half, zz, q)
+                swap_copy(
+                    ref, ref, sB_s.at[b, which, zz], sB_r.at[b, which, zz], second, bat
+                ).wait_recv()
+            quarter_to_sibling(b, 1 + which).start()
+        other = pl.ds(HALF * (1 - c), HALF)
+        for which in range(3):
+            drain(W.at[b, other, :, (second, first, both)[which]], sD_r.at[b, which])
+
+    for j in range(1, 8):
+        drain(cnt.at[bat ^ j], sC_r.at[bat ^ j])
+    for j in range(2):
+        v = 2 * (1 - x) + j
+        drain(cntx.at[v], sC_r.at[8 + v])
+    cntx[2 * x + (1 - c)] = cnt[bat ^ 1]
+    total = jnp.zeros((1, 1), jnp.float32)
+    for j in range(8):
+        big = cnt[j][0:1, 0:1]
+        big_rows = big * float(BIG_SIDE * BIG_SIDE)
+        area = float(SMALL_SIDE * SMALL_SIDE)
+        total = total + big_rows + jnp.floor((R - big_rows + 0.5) / area) * area
+    row_count = total
+    down = lax.broadcasted_iota(jnp.int32, (R, 1), 0).astype(jnp.float32)
+    across = lax.broadcasted_iota(jnp.int32, (1, R), 1).astype(jnp.float32)
+
+    @pl.loop(0, 4)
+    def _(v):
+        big = cntx[v][0:1, 0:1]
+        code_down, ok_down = crop_codes(down, big, R)
+        code_across, ok_across = crop_codes(across, big, R)
+        code_down = jnp.where(ok_down, code_down, -5000.0)
+        code_across = jnp.where(ok_across, code_across, -1.0)
+        for k in range(9):
+            step = float(32 * (k // 3 - 1) + (k % 3 - 1))
+            hit = (code_down + step) == code_across
+            Gm[v, pl.ds(k * R, R)] = jnp.where(hit, 1.0, 0.0).astype(jnp.bfloat16)
+
+    _, own_valid = crop_codes(down, cown[0:1, 0:1], R)
+    valid = own_valid.astype(jnp.float32)
+    for d in range(1, 4):
+        drain(aff.at[s ^ d], sF_r.at[s ^ d])
+    loads[2].wait()
+    h[...] = abuf[...].astype(jnp.float32)
+
+    def sums_start(e, first_sum, second_sum):
+        st_own[e] = pack(first_sum, second_sum)
+
+        @pl.when(c == 0)
+        def _():
+            swap_copy(st_own.at[e], st_in.at[e], sE_in_s.at[e], sE_in_r.at[e], s, bat ^ 1).start()
+
+        @pl.when(c == 1)
+        def _():
+            swap_copy(
+                st_own.at[e], st_in.at[e], sE_in_s.at[e], sE_in_r.at[e], s, bat ^ 1
+            ).wait_recv()
+            st_all[e, z] = st_own[e] + st_in[e]
+            for j in (7, 6, 5, 4, 3, 2, 1):
+                swap_copy(
+                    st_all.at[e, z], st_all.at[e, z], sE_s.at[e, j], sE_r.at[e, z], s, bat ^ j
+                ).start()
+
+    def sums_finish(e):
+        for j in range(1, 4):
+            zz = z ^ j
+            drain(st_all.at[e, zz], sE_r.at[e, zz])
+
+        @pl.when(c == 0)
+        def _():
+            drain(st_all.at[e, z], sE_r.at[e, z])
+
+        return unpack(st_all[e, 0] + st_all[e, 1] + st_all[e, 2] + st_all[e, 3])
+
+    def sums_close(e):
+        @pl.when(c == 0)
+        def _():
+            drain(st_own.at[e], sE_in_s.at[e])
+
+        @pl.when(c == 1)
+        def _():
+            for j in range(1, 8):
+                drain(st_own.at[e], sE_s.at[e, j])
+
+    def moments(sums):
+        center = sums[0] / row_count
+        spread = lax.rsqrt(sums[1] / row_count - center * center + EPS)
+        return center, spread
+
+    def share(b, kind, rows):
+        turned = rows.T
+        for cc in range(2):
+            for xx in range(2):
+                for yy in range(2):
+                    for zz in range(4):
+                        at = (2 * zz + cc) * 64 + (2 * yy + xx) * 16
+                        stage[b, kind, 2 * xx + cc, 4 * yy + zz] = turned[at : at + 16].astype(
+                            jnp.bfloat16
+                        )
+        for j in range(1, 4):
+            v = u ^ j
+            swap_copy(
+                stage.at[b, kind, v], caq.at[b, kind, u], sQ_s.at[b, kind, j],
+                sQ_r.at[b, kind, u], s ^ (j // 2), bat ^ (j % 2),
+            ).start()
+        caq[b, kind, u] = stage[b, kind, u]
+
+    def forward(b):
+        gather_second(b)
+        hidden = h[...]
+        zbuf[...] = jnp.dot(
+            hidden.astype(jnp.bfloat16), W[b, 9].reshape(D, D), preferred_element_type=jnp.float32
+        )
+        z1 = zbuf[...]
+        kept = valid * z1
+        sums_start(
+            2 * b, jnp.sum(kept, 0, keepdims=True), jnp.sum(kept * z1, 0, keepdims=True)
+        )
+        share(b, 1, hidden)
+        norms = aff[b]
+        center, spread = moments(sums_finish(2 * b))
+        gi[b, 0:1] = norms[0:1] * spread
+        for i in range(0, R, 64):
+            xhat = (zbuf[i : i + 64] - center) * spread
+            value, slope = mish_terms(norms[0:1] * xhat + norms[1:2])
+            sv[b, 0, i : i + 64] = xhat.astype(sv.dtype)
+            sv[b, 1, i : i + 64] = slope.astype(sv.dtype)
+            abuf[i : i + 64] = value.astype(jnp.bfloat16)
+        mixed = abuf[...]
+        for k in range(9):
+            Hb[:, k * D : (k + 1) * D] = jnp.dot(
+                Gm[u, pl.ds(k * R, R)], mixed, preferred_element_type=jnp.float32
+            ).astype(jnp.bfloat16)
+        zbuf[...] = jnp.dot(
+            Hb[...], W[b, 0:9].reshape(9 * D, D), preferred_element_type=jnp.float32
+        )
+        z2 = zbuf[...]
+        kept = valid * z2
+        sums_start(
+            2 * b + 1, jnp.sum(kept, 0, keepdims=True), jnp.sum(kept * z2, 0, keepdims=True)
+        )
+        share(b, 0, mixed.astype(jnp.float32))
+        center, spread = moments(sums_finish(2 * b + 1))
+        gi[b, 1:2] = norms[2:3] * spread
+        for i in range(0, R, 64):
+            xhat = (zbuf[i : i + 64] - center) * spread
+            value, slope = mish_terms(norms[2:3] * xhat + norms[3:4])
+            sv[b, 2, i : i + 64] = xhat.astype(sv.dtype)
+            sv[b, 3, i : i + 64] = slope.astype(sv.dtype)
+            h[i : i + 64] = h[i : i + 64] + valid[i : i + 64] * value
+
+    gather_z(0)
+    gather_first(0)
+    gather_z(1)
+    gather_first(1)
+
+    @pl.loop(0, 4)
+    def _(b):
+        forward(b)
+
+        @pl.when(b < 2)
+        def _():
+            gather_z(b + 2)
+            gather_first(b + 2)
+
+    out_features = pltpu.make_async_copy(h, features.at[0], sO_s.at[0])
+    out_features.start()
+    loads[3].wait()
+    g[...] = gbuf[...].astype(jnp.float32)
+
+    def dz_copy(b, par, kind, j):
+        return swap_copy(
+            dzq.at[par, kind, u], dzq.at[par, kind, u], sX_s.at[b, kind, j],
+            sX_r.at[b, kind, u], s ^ (j // 2), bat ^ (j % 2),
+        )
+
+    def send_dz(b, par, kind):
+        for j in range(1, 4):
+            dz_copy(b, par, kind, j).start()
+
+    def wait_dz(b, par, kind):
+        for j in range(1, 4):
+            v = u ^ j
+            drain(dzq.at[par, kind, v], sX_r.at[b, kind, v])
+
+    CHUNKS = ((0, 5), (5, 4), (9, 1))
+
+    def y_copy(b, par, i):
+        at, size = CHUNKS[i]
+        return swap_copy(
+            gout.at[par, 1 - y, pl.ds(at, size)], yrecv.at[b, pl.ds(at, size)],
+            sY_s.at[b, i], sY_r.at[b, i], s ^ 2, bat,
+        )
+
+    def grad_tap(par, k, left, right):
+        part = jnp.dot(left, right, preferred_element_type=jnp.float32).astype(jnp.bfloat16)
+        for yy in range(2):
+            gout[par, yy, k] = part[64 * yy : 64 * yy + 64].reshape(4, 16, D)
+
+    def grad_spatial(b, par):
+        for v in range(4):
+            left = caq[b, 0, v].reshape(128, R)
+            for k in range(9):
+                GcT[k, :, v * R : (v + 1) * R] = lax.dot_general(
+                    left, Gm[v, pl.ds(k * R, R)], NT, preferred_element_type=jnp.float32
+                ).astype(jnp.bfloat16)
+        wait_dz(b, par, 1)
+        right = dzq[par, 1].reshape(4 * R, D)
+        for k in range(9):
+            grad_tap(par, k, GcT[k], right)
+            if k == 4:
+                y_copy(b, par, 0).start()
+        y_copy(b, par, 1).start()
+
+    def grad_point(b, par):
+        wait_dz(b, par, 0)
+        left = jnp.concatenate([caq[b, 1, v].reshape(128, R) for v in range(4)], axis=1)
+        grad_tap(par, 9, left, dzq[par, 0].reshape(4 * R, D))
+        y_copy(b, par, 2).start()
+
+    def add_y(b, par, i):
+        at, size = CHUNKS[i]
+        y_copy(b, par, i).wait_recv()
+        for k in range(at, at + size):
+            yrecv[b, k] = (
+                yrecv[b, k].astype(jnp.float32) + gout[par, y, k].astype(jnp.float32)
+            ).astype(jnp.bfloat16)
+
+    def core_copy(b, i):
+        at, size = CHUNKS[i]
+        return swap_copy(
+            yrecv.at[b, pl.ds(at, size)], zs1.at[b, pl.ds(at, size)],
+            sK_s.at[b, i], sK_r.at[b, i], s, bat ^ 1,
+        )
+
+    def z_copy(b, i, cc, j):
+        at, size = CHUNKS[i]
+        source = (yrecv, zs1)[cc].at[b, pl.ds(at, size), z ^ j]
+        return swap_copy(
+            source, zrecv.at[b, z, pl.ds(at, size)], sR_s.at[b, i, cc, j], sR_r.at[b, i, z],
+            s, 2 * (z ^ j) + cc,
+        )
+
+    def reduce_plane(b, par, i):
+        add_y(b, par, i)
+
+        @pl.when(c == 1)
+        def _():
+            core_copy(b, i).start()
+
+    def reduce_z(b, i):
+        @pl.when(c == 0)
+        def _():
+            core_copy(b, i).wait_recv()
+            for cc in range(2):
+                for j in range(1, 4):
+                    z_copy(b, i, cc, j).start()
+
+    def finish_z(b):
+        for i, (at, size) in enumerate(CHUNKS):
+            for j in range(1, 4):
+                drain(zrecv.at[b, z ^ j, pl.ds(at, size)], sR_r.at[b, i, z ^ j])
+        for k in range(TAPS):
+            done = yrecv[b, k, z].astype(jnp.float32)
+            for j in range(1, 4):
+                done = done + zrecv[b, z ^ j, k].astype(jnp.float32)
+            fin[b, k] = done.astype(jnp.bfloat16)
+
+        @pl.when(b == s)
+        def _():
+            gfin[:, s] = fin[b]
+
+        @pl.when(b != s)
+        def _():
+            swap_copy(fin.at[b], gfin.at[:, s], sG_s.at[b], sG_r.at[s], b, bat).start()
+
+    def backward(bi):
+        b = 3 - bi
+        par = lax.rem(bi, 2)
+        e = 8 + 2 * bi
+        first_sum = jnp.zeros((1, D), jnp.float32)
+        second_sum = jnp.zeros((1, D), jnp.float32)
+        for i in range(0, R, 64):
+            du = valid[i : i + 64] * g[i : i + 64] * sv[b, 3, i : i + 64].astype(jnp.float32)
+            zbuf[i : i + 64] = du
+            first_sum += jnp.sum(du, 0, keepdims=True)
+            second_sum += jnp.sum(du * sv[b, 2, i : i + 64].astype(jnp.float32), 0, keepdims=True)
+        sums_start(e, first_sum, second_sum)
+
+        @pl.when(bi > 0)
+        def _():
+            grad_point(b + 1, 1 - par)
+
+        @pl.when(bi > 1)
+        def _():
+            for i in range(3):
+                reduce_plane(b + 2, par, i)
+            for i in range(3):
+                y_copy(b + 2, par, i).wait_send()
+            for kind in range(2):
+                for j in range(1, 4):
+                    dz_copy(b + 2, par, kind, j).wait_send()
+
+        total_first, total_second = sums_finish(e)
+        for i in range(0, R, 64):
+            xhat = sv[b, 2, i : i + 64].astype(jnp.float32)
+            inner = zbuf[i : i + 64] - valid[i : i + 64] * (
+                (total_first + xhat * total_second) / row_count
+            )
+            dzq[par, 1, u, i : i + 64] = (gi[b, 1:2] * inner).astype(jnp.bfloat16)
+        send_dz(b, par, 1)
+        gsend[b, 2:3] = total_second
+        gsend[b, 3:4] = total_first
+        d_two = dzq[par, 1, u]
+        for k in range(9):
+            Hb[:, k * D : (k + 1) * D] = jnp.dot(
+                Gm[u, pl.ds((8 - k) * R, R)], d_two, preferred_element_type=jnp.float32
+            ).astype(jnp.bfloat16)
+        mixed = None
+        for k in range(9):
+            part = lax.dot_general(
+                Hb[:, k * D : (k + 1) * D], W[b, k].reshape(D, D), NT,
+                preferred_element_type=jnp.float32,
+            )
+            mixed = part if mixed is None else mixed + part
+        zbuf[...] = mixed
+        first_sum = jnp.zeros((1, D), jnp.float32)
+        second_sum = jnp.zeros((1, D), jnp.float32)
+        for i in range(0, R, 64):
+            du = zbuf[i : i + 64] * sv[b, 1, i : i + 64].astype(jnp.float32)
+            zbuf[i : i + 64] = du
+            first_sum += jnp.sum(du, 0, keepdims=True)
+            second_sum += jnp.sum(du * sv[b, 0, i : i + 64].astype(jnp.float32), 0, keepdims=True)
+        sums_start(e + 1, first_sum, second_sum)
+        for j in range(1, 4):
+            v = u ^ j
+            for kind in range(2):
+                drain(caq.at[b, kind, v], sQ_r.at[b, kind, v])
+        grad_spatial(b, par)
+
+        @pl.when(bi > 1)
+        def _():
+            for i in range(3):
+                reduce_z(b + 2, i)
+
+        total_first, total_second = sums_finish(e + 1)
+        for i in range(0, R, 64):
+            xhat = sv[b, 0, i : i + 64].astype(jnp.float32)
+            inner = zbuf[i : i + 64] - valid[i : i + 64] * (
+                (total_first + xhat * total_second) / row_count
+            )
+            dzq[par, 0, u, i : i + 64] = (gi[b, 0:1] * inner).astype(jnp.bfloat16)
+        send_dz(b, par, 0)
+        gsend[b, 0:1] = total_second
+        gsend[b, 1:2] = total_first
+        g[...] = g[...] + lax.dot_general(
+            dzq[par, 0, u], W[b, 9].reshape(D, D), NT, preferred_element_type=jnp.float32
+        )
+
+        @pl.when(b == s)
+        def _():
+            gaff[s] = gsend[b]
+
+        @pl.when(b != s)
+        def _():
+            swap_copy(gsend.at[b], gaff.at[s], sO_s.at[4 + b], sO_r.at[s], b, bat).start()
+
+    @pl.loop(0, 4)
+    def _(bi):
+        backward(bi)
+
+    out_grad_in = pltpu.make_async_copy(g, in_grad.at[0], sO_s.at[1])
+    out_grad_in.start()
+
+    finish_z(3)
+    for i in range(3):
+        reduce_plane(1, 0, i)
+    for i in range(3):
+        reduce_z(1, i)
+    grad_point(0, 1)
+    finish_z(2)
+    for i in range(3):
+        reduce_plane(0, 1, i)
+        reduce_z(0, i)
+    finish_z(1)
+    finish_z(0)
+    loads[4].wait()
+    loads[5].wait()
+    for d in range(1, 4):
+        drain(gfin.at[:, s ^ d], sG_r.at[s ^ d])
+        drain(gaff.at[s ^ d], sO_r.at[s ^ d])
+
+    def square(ref, taps):
+        part = jnp.zeros((1, D), jnp.float32)
+        for k in taps:
+            v = ref[k].astype(jnp.float32).reshape(64, D)
+            part += jnp.sum(v * v, 0, keepdims=True)
+        return part
+
+    def lane_sum(v):
+        return jnp.sum(v, axis=1, keepdims=True)
+
+    squares = [square(r, t) for r in (pbuf, gfin) for t in (range(9, 10), range(9))]
+    lanes = lax.broadcasted_iota(jnp.int32, (1, D), 1)
+    tile = jnp.zeros((1, D), jnp.float32)
+    for i, part in enumerate(squares):
+        tile = jnp.where(lanes == i, lane_sum(part), tile)
+    sums_start(16, tile, tile)
+    totals, _ = sums_finish(16)
+    rate = BASE_RATE * (STEP + 1) / WARMUP
+    point_sq, spatial_sq, gpoint_sq, gspatial_sq = [totals[:, i : i + 1] for i in range(4)]
+    step_point = rate * TRUST_COEF * jnp.sqrt(point_sq) / (jnp.sqrt(gpoint_sq) + EPS_NORM)
+    step_spatial = rate * TRUST_COEF * jnp.sqrt(spatial_sq) / (jnp.sqrt(gspatial_sq) + EPS_NORM)
+    for k in range(TAPS):
+        grad = gfin[k].astype(jnp.float32).reshape(64, D)
+        moved = MOMENTUM * mbuf[k] + (step_point if k == 9 else step_spatial) * grad
+        mbuf[k] = moved
+        pbuf[k] = pbuf[k] - moved
+    outs = [
+        pltpu.make_async_copy(pbuf.at[9], new_point.at[0], sW.at[0]),
+        pltpu.make_async_copy(pbuf.at[pl.ds(0, 9)], new_spatial.at[0], sW.at[1]),
+        pltpu.make_async_copy(mbuf.at[9], new_mom_point.at[0], sW.at[2]),
+        pltpu.make_async_copy(mbuf.at[pl.ds(0, 9)], new_mom_spatial.at[0], sW.at[3]),
+    ]
+    for out in outs:
+        out.start()
+    affine_grad = (gaff[0] + gaff[1] + gaff[2] + gaff[3])[0:4]
+    affine = norm_in[0]
+    affine_sq = lane_sum(affine * affine)
+    gaffine_sq = lane_sum(affine_grad * affine_grad)
+    trust = TRUST_COEF * jnp.sqrt(affine_sq) / (jnp.sqrt(gaffine_sq) + EPS_NORM)
+    moved = MOMENTUM * mom_norm[0] + rate * trust * affine_grad
+    new_mom_norm[0] = moved
+    new_norm[0] = affine - moved
+
+    for d in range(1, 4):
+        scatter(d).wait_send()
+        swap_copy(aff.at[s], aff.at[s], sF_s.at[d], sF_r.at[s], s ^ d, bat).wait_send()
+
+    @pl.when(c == 1)
+    def _():
+        scatter(0).wait_send()
+
+    for j in range(1, 10):
+        if j != 0:
+            drain(cown, sC_s.at[j])
+
+    @pl.loop(0, 4)
+    def _(b):
+        for zz in range(4):
+            drain(pair(b, half, zz, s), sA_s.at[b, zz])
+            for which in range(2):
+                drain(pair(b, half, zz, s), sB_s.at[b, which, zz])
+        for which in range(3):
+            drain(W.at[b, half, :, s], sD_s.at[b, which])
+        for kind in range(2):
+            for j in range(1, 4):
+                drain(stage.at[b, kind, u], sQ_s.at[b, kind, j])
+
+        @pl.when(c == 0)
+        def _():
+            for j in range(1, 4):
+                drain(pair(b, slice(None), z, s), sZ_s.at[b, j])
+            for zz in range(4):
+                drain(pair(b, slice(None), zz, s), sH_s.at[b, zz])
+            for i, (at, size) in enumerate(CHUNKS):
+                for cc in range(2):
+                    for j in range(1, 4):
+                        drain(zrecv.at[b, z, pl.ds(at, size)], sR_s.at[b, i, cc, j])
+
+        @pl.when(c == 1)
+        def _():
+            for i, (at, size) in enumerate(CHUNKS):
+                drain(zs1.at[b, pl.ds(at, size)], sK_s.at[b, i])
+
+        @pl.when(b != s)
+        def _():
+            drain(fin.at[b], sG_s.at[b])
+            drain(gsend.at[b], sO_s.at[4 + b])
+
+        @pl.when(b < 2)
+        def _():
+            par = lax.rem(3 - b, 2)
+            for i in range(3):
+                y_copy(b, par, i).wait_send()
+            for kind in range(2):
+                for j in range(1, 4):
+                    dz_copy(b, par, kind, j).wait_send()
+
+    @pl.loop(0, 17)
+    def _(e):
+        sums_close(e)
+
+    out_features.wait()
+    out_grad_in.wait()
+    for out in outs:
+        out.wait()
+
+
+def train_step(images, crop, w_point, w_spatial, norm_params, mom_point, mom_spatial, mom_norm, out_grad):
+    R, D = images.shape[1:]
+    f32, bf16 = jnp.float32, jnp.bfloat16
+    dma = pltpu.SemaphoreType.DMA
+    anywhere = pl.BlockSpec(memory_space=pl.ANY)
+    vmem = pl.BlockSpec(memory_space=pltpu.VMEM)
+    smem = pl.BlockSpec(memory_space=pltpu.SMEM)
+    V = pltpu.VMEM
+    scratch = dict(
+        W=V((4, TAPS, 8, 4, 16, D), bf16), wown=V((TAPS, 4, 16, D), bf16),
+        pbuf=V((TAPS, 64, D), f32), mbuf=V((TAPS, 64, D), f32),
+        h=V((R, D), f32), g=V((R, D), f32), zbuf=V((R, D), f32),
+        sv=V((4, 4, R, D), bf16), gi=V((4, 8, D), f32),
+        abuf=V((R, D), bf16), gbuf=V((R, D), bf16),
+        Gm=V((4, 9 * R, R), bf16), caq=V((4, 2, 4, 8, 16, R), bf16),
+        stage=V((4, 2, 4, 8, 16, R), bf16), Hb=V((R, 9 * D), bf16),
+        GcT=V((9, 128, 4 * R), bf16), dzq=V((2, 2, 4, R, D), bf16),
+        gout=V((2, 2, TAPS, 4, 16, D), bf16), yrecv=V((4, TAPS, 4, 16, D), bf16),
+        zs1=V((4, TAPS, 4, 16, D), bf16), zrecv=V((4, 4, TAPS, 16, D), bf16),
+        fin=V((4, TAPS, 16, D), bf16), gfin=V((TAPS, 4, 16, D), bf16),
+        aff=V((4, 8, D), f32), gaff=V((4, 8, D), f32), gsend=V((4, 8, D), f32),
+        st_in=V((17, 8, 128), f32), st_own=V((17, 8, 128), f32), st_all=V((17, 4, 8, 128), f32),
+        cnt=V((8, 8, 128), f32), cntx=V((4, 8, 128), f32), cown=V((8, 128), f32),
+        sL=dma((6,)), sS_s=dma((4,)), sS_r=dma((4, 2)), sZ_s=dma((4, 4)), sZ_r=dma((4, 4)),
+        sH_s=dma((4, 4)), sH_r=dma((4, 4)), sA_s=dma((4, 4)), sA_r=dma((4, 4)),
+        sB_s=dma((4, 2, 4)), sB_r=dma((4, 2, 4)), sD_s=dma((4, 3)), sD_r=dma((4, 3)),
+        sE_in_s=dma((17,)), sE_in_r=dma((17,)), sE_s=dma((17, 8)), sE_r=dma((17, 4)),
+        sC_s=dma((12,)), sC_r=dma((12,)), sF_s=dma((4,)), sF_r=dma((4,)),
+        sQ_s=dma((4, 2, 4)), sQ_r=dma((4, 2, 4)), sX_s=dma((4, 2, 4)), sX_r=dma((4, 2, 4)),
+        sY_s=dma((4, 3)), sY_r=dma((4, 3)), sK_s=dma((4, 3)), sK_r=dma((4, 3)),
+        sR_s=dma((4, 3, 2, 4)), sR_r=dma((4, 3, 4)), sG_s=dma((4,)), sG_r=dma((4,)),
+        sO_s=dma((8,)), sO_r=dma((4,)), sW=dma((4,)),
+    )
+    shape = jax.ShapeDtypeStruct
+    return pl.pallas_call(
+        train_kernel,
+        out_shape=(
+            shape((1, R, D), f32), shape((1, R, D), f32),
+            shape(w_point.shape, f32), shape(w_spatial.shape, f32), shape(norm_params.shape, f32),
+            shape(w_point.shape, f32), shape(w_spatial.shape, f32), shape(norm_params.shape, f32),
+        ),
+        in_specs=[anywhere, smem, anywhere, anywhere, vmem, anywhere, anywhere, vmem, anywhere],
+        out_specs=(anywhere, anywhere, anywhere, anywhere, vmem, anywhere, anywhere, vmem),
+        scratch_shapes=list(scratch.values()),
+        compiler_params=pltpu.CompilerParams(
+            collective_id=0, has_side_effects=True, vmem_limit_bytes=64 * 1024 * 1024
+        ),
+    )(images, crop, w_point, w_spatial, norm_params, mom_point, mom_spatial, mom_norm, out_grad)
+
+
 def solution(mesh):
+    tuned = mesh.shape["section"] == 4 and mesh.shape["batch"] == 8
     return jax.shard_map(
-        on_device,
+        train_step if tuned else on_device,
         mesh=mesh,
         in_specs=(
             P(None, "batch", None),

time: 1450 us -> 325 us (0.22); the launches traced: 1430 us -> 325 us
  blocking collectives: 427 us -> 0 us
  local copies, waits for them, and re-layouts: 367 us -> 8.67 us
  Pallas kernels: 0 us -> 315 us
  matrix products: 226 us -> 0 us
  other arithmetic: 198 us -> 0 us
  waiting for transfers between devices: 141 us -> 0 us
  starting transfers between devices: 43.4 us -> 0 us
  between operations: 32.3 us -> 0.68 us
    psum x29 -> x0, blocking collectives: 410 us -> none  [the longest x14 203 us: batch_moments(): lax.psum((jnp.sum(weighted, 0), jnp.sum(weighted * proj, 0), jnp.sum(vali...]
    pallas_call x0 -> x1, Pallas kernels: none -> 315 us  [train_step(): pl.pallas_call(train_kernel, out_shape=(shape((1, R, D), f32), shape((1,...]
    gather x42 -> x0, local copies, waits for them, and re-layouts: 268 us -> none  [the longest x28 177 us: spatial_apply(): stacked = source[tap_index] * tap_mask[:, :, None].astype(source.dtype)]
    dot_general x56 -> x0, matrix products: 226 us -> none  [the longest x14 79.3 us: spatial_apply(): lax.dot_general(stacked, weights, (((1, 2), (0, 1)), ((), ())), preferred...]
    reduce_scatter x2 -> x0, waiting for transfers between devices: 74.4 us -> none  [the longest x1 74.3 us: on_device(): lax.psum_scatter(grad_spatial, 'batch', scatter_dimension=1, tiled=True)]
    mul x24 -> x0, other arithmetic: 67.8 us -> none  [the longest x14 47.1 us: spatial_apply(): stacked = source[tap_index] * tap_mask[:, :, None].astype(source.dtype)]
    ppermute x12 -> x0, waiting for transfers between devices: 59.2 us -> none  [from_behind(): return lax.ppermute(block, axis, route)]
    mul x7 -> x0, local copies, waits for them, and re-layouts: 50 us -> none  [spatial_apply(): stacked = source[tap_index] * tap_mask[:, :, None].astype(source.dtype)]
  transfers between devices with their start and end apart: 17 -> 0, of which waited for: 13 -> 0; matrix products, arithmetic and copies ran while one was open for 19% -> 0% of each run, Pallas kernels for 0% -> 0%
where the time goes in v1:
time: 325 us
  Pallas kernels  315 us (97%)
  local copies, waits for them, and re-layouts  8.67 us (3%)
    pallas_call x1, Pallas kernels, train_step(): pl.pallas_call(train_kernel, out_shape=(shape((1, R, D), f32), shape((1,...  315 us
    unnamed x23, local copies, waits for them, and re-layouts  8.67 us

profile of v1, /device:TPU:0, one launch (start us, length us, event | category | flops | bytes accessed | tf_op | source)
XLA Modules:
  0.0 324.6 jit_solution(11773830006547689939)
XLA Ops:
  0.6 1.3 copy.17.crop
  1.9 315.2 %shard_map.152 = (f32[1,256,512]{2,1,0:T(8,128)}, f32[1,256,512]{2,1,0:T(8,128)}, f32[1,64,512]{2,1,0:T(8,128)}, f32[1,9,64,512]{3,2,1,0:T(8,128)}, f32[1,4,512]...) custom-call(bf16[4,256,512]{2,1,0:T(8,128)(2,1)} %images.1, ...), custom_call_target="tpu_custom_call" | custom-call | tf_op jit(solution)/shard_map/pallas_call | solution.py:1047
  317.2 0.0 copy-start.2
  317.2 0.0 copy-start.4
  317.2 0.0 copy-start.1
  317.2 2.0 copy.26
  319.2 0.0 copy-done.2
  319.2 0.8 copy.27
  320.0 0.0 copy-done.4
  320.0 0.7 copy.28
  320.7 0.0 copy-done.1
  320.7 0.0 copy-start.6
  320.7 0.0 copy-start.3
  320.7 0.0 copy-start
  320.7 1.0 copy.29
  321.7 0.0 copy-done.6
  321.7 0.6 copy.30
  322.3 0.0 copy-done.3
  322.3 0.7 copy.31
  322.9 0.0 copy-done
  322.9 0.0 copy-start.5
  322.9 1.0 copy.32
  324.0 0.0 copy-done.5
  324.0 0.6 copy.33
Async XLA Ops:
  317.2 2.0 copy-start.2
  317.2 2.8 copy-start.4
  317.2 3.5 %copy-start.1 = (f32[1,9,64,512]{3,2,1,0:T(8,128)S(1)}, f32[1,9,64,512]{3,2,1,0:T(8,128)}, u32[]{:S(2)}) copy-start(f32[1,9,64,512]{3,2,1,0:T(8,128)} %get-tuple-element.19) | copy-start | bytes 3538948
  320.7 1.0 copy-start.6
  320.7 1.6 copy-start.3
  320.7 2.3 copy-start
  322.9 1.0 copy-start.5

commit v2 on v1

--- a/solution.py
+++ b/solution.py
@@ -363,14 +363,13 @@
 
 
 def train_kernel(
-    images, crop, w_point, w_spatial, norm_in, mom_point, mom_spatial, mom_norm, out_grad,
-    features, in_grad, new_point, new_spatial, new_norm, new_mom_point, new_mom_spatial,
-    new_mom_norm,
-    W, wown, pbuf, mbuf, h, g, zbuf, sv, gi, abuf, gbuf, Gm, caq, stage, Hb, GcT, dzq, gout, yrecv,
-    zs1, zrecv, fin, gfin, aff, gaff, gsend, st_in, st_own, st_all, cnt, cntx, cown,
+    images, crop, w_point, w_spatial, norm_in, out_grad,
+    features, in_grad, grads, totals_out, affine_out,
+    W, wown, F, sv, gi, abuf, gbuf, Gm, caq, stage, Hb, dzq, gout, yrecv,
+    zs1, zrecv, gfin, aff, gaff, gsend, st_in, st_own, st_all, cnt, cntx, cown,
     sL, sS_s, sS_r, sZ_s, sZ_r, sH_s, sH_r, sA_s, sA_r, sB_s, sB_r, sD_s, sD_r,
     sE_in_s, sE_in_r, sE_s, sE_r, sC_s, sC_r, sF_s, sF_r, sQ_s, sQ_r, sX_s, sX_r,
-    sY_s, sY_r, sK_s, sK_r, sR_s, sR_r, sG_s, sG_r, sO_s, sO_r, sW,
+    sY_s, sY_r, sK_s, sK_r, sN_s, sN_r, sT_s, sT_r, sG_s, sG_r, sO_s, sO_r,
 ):
     s = lax.axis_index("section")
     bat = lax.axis_index("batch")
@@ -379,15 +378,19 @@
     x = lax.rem(s, 2)
     y = s // 2
     u = 2 * x + c
-    R, D = h.shape
+    R, D = abuf.shape
+    h = F.at[pl.ds(0, R)]
+    g = F.at[pl.ds(R, R)]
+    zbuf = F.at[pl.ds(2 * R, R)]
 
     loads = [
-        pltpu.make_async_copy(w_point.at[0], pbuf.at[9], sL.at[0]),
-        pltpu.make_async_copy(w_spatial.at[0], pbuf.at[pl.ds(0, 9)], sL.at[1]),
-        pltpu.make_async_copy(images.at[s], abuf, sL.at[2]),
-        pltpu.make_async_copy(out_grad.at[s], gbuf, sL.at[3]),
-        pltpu.make_async_copy(mom_point.at[0], mbuf.at[9], sL.at[4]),
-        pltpu.make_async_copy(mom_spatial.at[0], mbuf.at[pl.ds(0, 9)], sL.at[5]),
+        pltpu.make_async_copy(w_point.at[0], F.at[pl.ds(9 * 64, 64)], sL.at[9]),
+        *[
+            pltpu.make_async_copy(w_spatial.at[0, k], F.at[pl.ds(k * 64, 64)], sL.at[k])
+            for k in range(9)
+        ],
+        pltpu.make_async_copy(images.at[s], abuf, sL.at[10]),
+        pltpu.make_async_copy(out_grad.at[s], gbuf, sL.at[11]),
     ]
     for load in loads:
         load.start()
@@ -399,17 +402,27 @@
         pl.semaphore_signal(
             barrier, inc=1, device_id=(sec, other), device_id_type=pl.DeviceIdType.MESH
         )
-    pl.semaphore_wait(barrier, len(greet))
-
-    loads[0].wait()
-    loads[1].wait()
+
+    def square(rows):
+        return jnp.sum(rows * rows, 0, keepdims=True)
+
+    spatial_squares = jnp.zeros((1, D), jnp.float32)
+    for load in loads[:10]:
+        load.wait()
     for k in range(TAPS):
-        wown[k] = pbuf[k].astype(jnp.bfloat16).reshape(4, 16, D)
+        rows = F[k * 64 : k * 64 + 64]
+        wown[k] = rows.astype(jnp.bfloat16).reshape(4, 16, D)
+        if k < 9:
+            spatial_squares += square(rows)
+        else:
+            point_squares = square(rows)
+    with jax.named_scope("greet"):
+        pl.semaphore_wait(barrier, len(greet))
 
     def scatter(d):
         q = s ^ d
         return swap_copy(
-            wown.at[:, q], W.at[s, :, bat, q], sS_s.at[d], sS_r.at[s, c], q, 2 * z
+            wown.at[:, q], W.at[s, :, bat, q], sS_s, sS_r.at[s, c], q, 2 * z
         )
 
     for d in range(1, 4):
@@ -423,16 +436,16 @@
     def _():
         pltpu.make_async_copy(wown.at[:, s], W.at[s, :, bat, s], sS_r.at[s, c]).start()
 
-    cown[...] = jnp.full((8, 128), crop[s, 0].astype(jnp.float32))
+    cown[...] = jnp.full((8, 128), crop[0, s].astype(jnp.float32))
     aff[s] = jnp.concatenate([norm_in[0], jnp.zeros((4, D), jnp.float32)], axis=0)
     cnt[bat] = cown[...]
-    cntx[u] = cown[...]
+    cntx[c] = cown[...]
     for j in range(1, 8):
-        swap_copy(cown, cnt.at[bat], sC_s.at[j], sC_r.at[bat], s, bat ^ j).start()
+        swap_copy(cown, cnt.at[bat], sC_s, sC_r.at[0], s, bat ^ j).start()
     for j in range(2):
-        swap_copy(cown, cntx.at[u], sC_s.at[8 + j], sC_r.at[8 + u], s ^ 1, bat ^ j).start()
+        swap_copy(cown, cntx.at[2 + c], sC_s, sC_r.at[1], s ^ 1, bat ^ j).start()
     for d in range(1, 4):
-        swap_copy(aff.at[s], aff.at[s], sF_s.at[d], sF_r.at[s], s ^ d, bat).start()
+        swap_copy(aff.at[s], aff.at[s], sF_s, sF_r, s ^ d, bat).start()
 
     half = pl.ds(HALF * c, HALF)
     first = jnp.where(c == 0, s ^ 1, s ^ 2)
@@ -444,15 +457,15 @@
 
     def to_sibling(b, zz):
         ref = pair(b, slice(None), zz, s)
-        return swap_copy(ref, ref, sH_s.at[b, zz], sH_r.at[b, zz], s, bat ^ 1)
+        return swap_copy(ref, ref, sH_s.at[b], sH_r.at[b, zz], s, bat ^ 1)
 
     def along_first(b, zz):
         ref = pair(b, half, zz, s)
-        return swap_copy(ref, ref, sA_s.at[b, zz], sA_r.at[b, zz], first, bat)
+        return swap_copy(ref, ref, sA_s.at[b], sA_r.at[b, zz], first, bat)
 
     def along_second(b, which, zz):
         ref = pair(b, half, zz, s if which == 0 else first)
-        return swap_copy(ref, ref, sB_s.at[b, which, zz], sB_r.at[b, which, zz], second, bat)
+        return swap_copy(ref, ref, sB_s.at[b, which], sB_r.at[b, which], second, bat)
 
     def quarter_to_sibling(b, which):
         ref = W.at[b, half, :, (first, second, both)[which]]
@@ -472,13 +485,14 @@
 
     def spread_z(b, j):
         ref = pair(b, slice(None), z, s)
-        return swap_copy(ref, ref, sZ_s.at[b, j], sZ_r.at[b, z], s, bat ^ (2 * j))
+        return swap_copy(ref, ref, sZ_s.at[b], sZ_r.at[b, z], s, bat ^ (2 * j))
 
     def from_z(b, zz):
         ref = pair(b, slice(None), zz, s)
-        return swap_copy(ref, ref, sZ_s.at[b, 0], sZ_r.at[b, zz], s, bat)
+        return swap_copy(ref, ref, sZ_s.at[b], sZ_r.at[b, zz], s, bat)
 
     @pl.loop(0, 4)
+    @jax.named_scope("own_quarter")
     def _(b):
         @pl.when(c == 0)
         def _():
@@ -487,8 +501,11 @@
             for j in range(1, 4):
                 spread_z(b, j).start()
 
-        own_ready(b, z)
-
+        @pl.when(b < 2)
+        def _():
+            own_ready(b, z)
+
+    @jax.named_scope("gather_z")
     def gather_z(b):
         for j in range(1, 4):
             zz = z ^ j
@@ -499,34 +516,30 @@
 
             own_ready(b, zz)
 
+    @jax.named_scope("gather_first")
     def gather_first(b):
         for j in range(4):
             zz = z ^ j
             ref = pair(b, half, zz, first)
-            swap_copy(ref, ref, sA_s.at[b, zz], sA_r.at[b, zz], first, bat).wait_recv()
+            swap_copy(ref, ref, sA_s.at[b], sA_r.at[b, zz], first, bat).wait_recv()
             along_second(b, 1, zz).start()
         quarter_to_sibling(b, 0).start()
 
+    @jax.named_scope("gather_second")
     def gather_second(b):
         for which in range(2):
-            q = (second, both)[which]
-            for j in range(4):
-                zz = z ^ j
-                ref = pair(b, half, zz, q)
-                swap_copy(
-                    ref, ref, sB_s.at[b, which, zz], sB_r.at[b, which, zz], second, bat
-                ).wait_recv()
+            drain(W.at[b, half, :, (second, both)[which]], sB_r.at[b, which])
             quarter_to_sibling(b, 1 + which).start()
+
+    @jax.named_scope("gather_last")
+    def gather_last(b):
         other = pl.ds(HALF * (1 - c), HALF)
         for which in range(3):
             drain(W.at[b, other, :, (second, first, both)[which]], sD_r.at[b, which])
 
-    for j in range(1, 8):
-        drain(cnt.at[bat ^ j], sC_r.at[bat ^ j])
-    for j in range(2):
-        v = 2 * (1 - x) + j
-        drain(cntx.at[v], sC_r.at[8 + v])
-    cntx[2 * x + (1 - c)] = cnt[bat ^ 1]
+    drain(cnt.at[pl.ds(0, 7)], sC_r.at[0])
+    drain(cntx.at[pl.ds(2, 2)], sC_r.at[1])
+    cntx[1 - c] = cnt[bat ^ 1]
     total = jnp.zeros((1, 1), jnp.float32)
     for j in range(8):
         big = cnt[j][0:1, 0:1]
@@ -538,6 +551,7 @@
     across = lax.broadcasted_iota(jnp.int32, (1, R), 1).astype(jnp.float32)
 
     @pl.loop(0, 4)
+    @jax.named_scope("tables")
     def _(v):
         big = cntx[v][0:1, 0:1]
         code_down, ok_down = crop_codes(down, big, R)
@@ -551,11 +565,11 @@
 
     _, own_valid = crop_codes(down, cown[0:1, 0:1], R)
     valid = own_valid.astype(jnp.float32)
-    for d in range(1, 4):
-        drain(aff.at[s ^ d], sF_r.at[s ^ d])
-    loads[2].wait()
+    drain(aff.at[pl.ds(0, 3)], sF_r)
+    loads[10].wait()
     h[...] = abuf[...].astype(jnp.float32)
 
+    @jax.named_scope("sums_start")
     def sums_start(e, first_sum, second_sum):
         st_own[e] = pack(first_sum, second_sum)
 
@@ -571,17 +585,18 @@
             st_all[e, z] = st_own[e] + st_in[e]
             for j in (7, 6, 5, 4, 3, 2, 1):
                 swap_copy(
-                    st_all.at[e, z], st_all.at[e, z], sE_s.at[e, j], sE_r.at[e, z], s, bat ^ j
+                    st_all.at[e, z], st_all.at[e, z], sE_s.at[e], sE_r.at[e], s, bat ^ j
                 ).start()
 
+    @jax.named_scope("sums_finish")
     def sums_finish(e):
-        for j in range(1, 4):
-            zz = z ^ j
-            drain(st_all.at[e, zz], sE_r.at[e, zz])
-
         @pl.when(c == 0)
         def _():
-            drain(st_all.at[e, z], sE_r.at[e, z])
+            drain(st_all.at[e], sE_r.at[e])
+
+        @pl.when(c == 1)
+        def _():
+            drain(st_all.at[e, pl.ds(0, 3)], sE_r.at[e])
 
         return unpack(st_all[e, 0] + st_all[e, 1] + st_all[e, 2] + st_all[e, 3])
 
@@ -592,14 +607,14 @@
 
         @pl.when(c == 1)
         def _():
-            for j in range(1, 8):
-                drain(st_own.at[e], sE_s.at[e, j])
+            drain(cnt.at[pl.ds(0, 7)], sE_s.at[e])
 
     def moments(sums):
         center = sums[0] / row_count
         spread = lax.rsqrt(sums[1] / row_count - center * center + EPS)
         return center, spread
 
+    @jax.named_scope("share")
     def share(b, kind, rows):
         turned = rows.T
         for cc in range(2):
@@ -610,16 +625,33 @@
                         stage[b, kind, 2 * xx + cc, 4 * yy + zz] = turned[at : at + 16].astype(
                             jnp.bfloat16
                         )
+        caq[b, kind, u] = stage[b, kind, u]
+
+        @pl.when(b == 3)
+        def _():
+            send_share(b, kind)
+
+    def send_share(b, kind):
         for j in range(1, 4):
-            v = u ^ j
             swap_copy(
-                stage.at[b, kind, v], caq.at[b, kind, u], sQ_s.at[b, kind, j],
-                sQ_r.at[b, kind, u], s ^ (j // 2), bat ^ (j % 2),
+                stage.at[b, kind, u ^ j], caq.at[b, kind, u], sQ_s.at[b, kind],
+                sQ_r.at[b, kind], s ^ (j // 2), bat ^ (j % 2),
             ).start()
-        caq[b, kind, u] = stage[b, kind, u]
-
+
+    @jax.named_scope("wait_share")
+    def wait_share(b, kind):
+        drain(caq.at[b, kind, pl.ds(0, 3)], sQ_r.at[b, kind])
+
+    @jax.named_scope("forward")
     def forward(b):
-        gather_second(b)
+        gather_last(b)
+
+        @pl.when(b == 3)
+        def _():
+            for early in (2, 1):
+                for kind in range(2):
+                    send_share(early, kind)
+
         hidden = h[...]
         zbuf[...] = jnp.dot(
             hidden.astype(jnp.bfloat16), W[b, 9].reshape(D, D), preferred_element_type=jnp.float32
@@ -630,6 +662,11 @@
             2 * b, jnp.sum(kept, 0, keepdims=True), jnp.sum(kept * z1, 0, keepdims=True)
         )
         share(b, 1, hidden)
+
+        @pl.when(b < 2)
+        def _():
+            gather_z(b + 2)
+
         norms = aff[b]
         center, spread = moments(sums_finish(2 * b))
         gi[b, 0:1] = norms[0:1] * spread
@@ -642,7 +679,7 @@
         mixed = abuf[...]
         for k in range(9):
             Hb[:, k * D : (k + 1) * D] = jnp.dot(
-                Gm[u, pl.ds(k * R, R)], mixed, preferred_element_type=jnp.float32
+                Gm[c, pl.ds(k * R, R)], mixed, preferred_element_type=jnp.float32
             ).astype(jnp.bfloat16)
         zbuf[...] = jnp.dot(
             Hb[...], W[b, 0:9].reshape(9 * D, D), preferred_element_type=jnp.float32
@@ -653,6 +690,15 @@
             2 * b + 1, jnp.sum(kept, 0, keepdims=True), jnp.sum(kept * z2, 0, keepdims=True)
         )
         share(b, 0, mixed.astype(jnp.float32))
+
+        @pl.when(b < 2)
+        def _():
+            gather_first(b + 2)
+
+        @pl.when(b < 3)
+        def _():
+            gather_second(b + 1)
+
         center, spread = moments(sums_finish(2 * b + 1))
         gi[b, 1:2] = norms[2:3] * spread
         for i in range(0, R, 64):
@@ -663,81 +709,141 @@
             h[i : i + 64] = h[i : i + 64] + valid[i : i + 64] * value
 
     gather_z(0)
+    own_ready(2, z)
     gather_first(0)
+    own_ready(3, z)
     gather_z(1)
     gather_first(1)
+    gather_second(0)
 
     @pl.loop(0, 4)
     def _(b):
         forward(b)
 
-        @pl.when(b < 2)
-        def _():
-            gather_z(b + 2)
-            gather_first(b + 2)
-
     out_features = pltpu.make_async_copy(h, features.at[0], sO_s.at[0])
     out_features.start()
-    loads[3].wait()
+    loads[11].wait()
     g[...] = gbuf[...].astype(jnp.float32)
 
-    def dz_copy(b, par, kind, j):
+    @jax.named_scope("close_gather")
+    def close_gather():
+        drain(aff.at[pl.ds(0, 3)], sF_s)
+        drain(st_own.at[pl.ds(0, 9)], sC_s)
+
+        @pl.when(c == 0)
+        def _():
+            drain(wown.at[:, pl.ds(0, 3)], sS_s)
+
+        @pl.when(c == 1)
+        def _():
+            drain(wown, sS_s)
+
+        @pl.loop(0, 4)
+        def _(b):
+            drain(W.at[b, half, :, s], sA_s.at[b])
+            for which in range(2):
+                drain(W.at[b, half, :, s], sB_s.at[b, which])
+            for which in range(3):
+                drain(W.at[b, half, :, s], sD_s.at[b, which])
+
+            @pl.when(c == 0)
+            def _():
+                drain(W.at[b, :, pl.ds(0, 6), s], sZ_s.at[b])
+                drain(W.at[b, :, :, s], sH_s.at[b])
+
+    @jax.named_scope("close_rest")
+    def close_rest():
+        @pl.loop(0, 4)
+        def _(b):
+            for kind in range(2):
+                drain(stage.at[b, kind, pl.ds(0, 3)], sQ_s.at[b, kind])
+                drain(dzq.at[b, kind, pl.ds(0, 3)], sX_s.at[b, kind])
+
+            @pl.when(b != s)
+            def _():
+                drain(gsend.at[b], sO_s.at[4 + b])
+
+            for i in range(3):
+                y_copy(b, i).wait_send()
+
+            @pl.when(c == 1)
+            def _():
+                for i, (at, size) in enumerate(CHUNKS):
+                    drain(zs1.at[b, pl.ds(at, size)], sK_s.at[b, i])
+
+            @pl.when(c == 0)
+            def _():
+                for i, (at, size) in enumerate(CHUNKS):
+                    drain(zrecv.at[b, :, pl.ds(0, 2), pl.ds(at, size)], sN_s.at[b, i])
+                    drain(zrecv.at[b, :, 2, pl.ds(at, size)], sT_s.at[b, i])
+
+        @pl.loop(0, 16)
+        def _(e):
+            sums_close(e)
+
+    CHUNKS = ((0, 5), (5, 4), (9, 1))
+
+    def dz_copy(b, kind, j):
+        v = u ^ 2 if j == 3 else u
+        ref = dzq.at[b, kind, v]
         return swap_copy(
-            dzq.at[par, kind, u], dzq.at[par, kind, u], sX_s.at[b, kind, j],
-            sX_r.at[b, kind, u], s ^ (j // 2), bat ^ (j % 2),
-        )
-
-    def send_dz(b, par, kind):
-        for j in range(1, 4):
-            dz_copy(b, par, kind, j).start()
-
-    def wait_dz(b, par, kind):
-        for j in range(1, 4):
-            v = u ^ j
-            drain(dzq.at[par, kind, v], sX_r.at[b, kind, v])
-
-    CHUNKS = ((0, 5), (5, 4), (9, 1))
-
-    def y_copy(b, par, i):
+            ref, ref, sX_s.at[b, kind], sX_r.at[b, kind, v],
+            s ^ 1 if j == 2 else s, bat if j == 2 else bat ^ 1,
+        )
+
+    def send_dz(b, kind):
+        dz_copy(b, kind, 2).start()
+        dz_copy(b, kind, 1).start()
+
+    @jax.named_scope("forward_dz")
+    def forward_dz(b, kind):
+        v = u ^ 2
+        drain(dzq.at[b, kind, v], sX_r.at[b, kind, v])
+        dz_copy(b, kind, 3).start()
+
+    @jax.named_scope("wait_dz")
+    def wait_dz(b, kind):
+        for v in (u ^ 1, u ^ 3):
+            drain(dzq.at[b, kind, v], sX_r.at[b, kind, v])
+
+    def y_copy(b, i):
         at, size = CHUNKS[i]
         return swap_copy(
-            gout.at[par, 1 - y, pl.ds(at, size)], yrecv.at[b, pl.ds(at, size)],
+            gout.at[b, 1 - y, pl.ds(at, size)], yrecv.at[b, pl.ds(at, size)],
             sY_s.at[b, i], sY_r.at[b, i], s ^ 2, bat,
         )
 
-    def grad_tap(par, k, left, right):
+    def grad_tap(b, k, left, right):
         part = jnp.dot(left, right, preferred_element_type=jnp.float32).astype(jnp.bfloat16)
         for yy in range(2):
-            gout[par, yy, k] = part[64 * yy : 64 * yy + 64].reshape(4, 16, D)
-
-    def grad_spatial(b, par):
-        for v in range(4):
-            left = caq[b, 0, v].reshape(128, R)
-            for k in range(9):
-                GcT[k, :, v * R : (v + 1) * R] = lax.dot_general(
-                    left, Gm[v, pl.ds(k * R, R)], NT, preferred_element_type=jnp.float32
+            gout[b, yy, k] = part[64 * yy : 64 * yy + 64].reshape(4, 16, D)
+
+    @jax.named_scope("grad_spatial")
+    def grad_spatial(b):
+        wait_share(b, 0)
+        wait_dz(b, 1)
+        tables = [jnp.where(x == v // 2, 0, 2) + v % 2 for v in range(4)]
+        right = dzq[b, 1].reshape(4 * R, D)
+        for k in range(9):
+            left = [
+                lax.dot_general(
+                    caq[b, 0, v].reshape(128, R), Gm[tables[v], pl.ds(k * R, R)], NT,
+                    preferred_element_type=jnp.float32,
                 ).astype(jnp.bfloat16)
-        wait_dz(b, par, 1)
-        right = dzq[par, 1].reshape(4 * R, D)
-        for k in range(9):
-            grad_tap(par, k, GcT[k], right)
+                for v in range(4)
+            ]
+            grad_tap(b, k, jnp.concatenate(left, axis=1), right)
             if k == 4:
-                y_copy(b, par, 0).start()
-        y_copy(b, par, 1).start()
-
-    def grad_point(b, par):
-        wait_dz(b, par, 0)
+                y_copy(b, 0).start()
+        y_copy(b, 1).start()
+
+    @jax.named_scope("grad_point")
+    def grad_point(b):
+        wait_share(b, 1)
+        wait_dz(b, 0)
         left = jnp.concatenate([caq[b, 1, v].reshape(128, R) for v in range(4)], axis=1)
-        grad_tap(par, 9, left, dzq[par, 0].reshape(4 * R, D))
-        y_copy(b, par, 2).start()
-
-    def add_y(b, par, i):
-        at, size = CHUNKS[i]
-        y_copy(b, par, i).wait_recv()
-        for k in range(at, at + size):
-            yrecv[b, k] = (
-                yrecv[b, k].astype(jnp.float32) + gout[par, y, k].astype(jnp.float32)
-            ).astype(jnp.bfloat16)
+        grad_tap(b, 9, left, dzq[b, 0].reshape(4 * R, D))
+        y_copy(b, 2).start()
 
     def core_copy(b, i):
         at, size = CHUNKS[i]
@@ -746,50 +852,94 @@
             sK_s.at[b, i], sK_r.at[b, i], s, bat ^ 1,
         )
 
-    def z_copy(b, i, cc, j):
+    @jax.named_scope("reduce_plane")
+    def reduce_plane(b, i):
         at, size = CHUNKS[i]
-        source = (yrecv, zs1)[cc].at[b, pl.ds(at, size), z ^ j]
+        y_copy(b, i).wait_recv()
+        for k in range(at, at + size):
+            yrecv[b, k] = (
+                yrecv[b, k].astype(jnp.float32) + gout[b, y, k].astype(jnp.float32)
+            ).astype(jnp.bfloat16)
+
+        @pl.when(c == 1)
+        def _():
+            core_copy(b, i).start()
+
+    def z_near(b, i, cc, slot):
+        at, size = CHUNKS[i]
         return swap_copy(
-            source, zrecv.at[b, z, pl.ds(at, size)], sR_s.at[b, i, cc, j], sR_r.at[b, i, z],
-            s, 2 * (z ^ j) + cc,
-        )
-
-    def reduce_plane(b, par, i):
-        add_y(b, par, i)
-
-        @pl.when(c == 1)
-        def _():
-            core_copy(b, i).start()
-
-    def reduce_z(b, i):
+            (yrecv, zs1)[cc].at[b, pl.ds(at, size), z ^ (3 if slot else 1)],
+            zrecv.at[b, cc, slot, pl.ds(at, size)], sN_s.at[b, i], sN_r.at[b, i], s, bat ^ 2,
+        )
+
+    def z_far(b, i, cc):
+        at, size = CHUNKS[i]
+        return swap_copy(
+            zrecv.at[b, cc, 1, pl.ds(at, size)], zrecv.at[b, cc, 2, pl.ds(at, size)],
+            sT_s.at[b, i], sT_r.at[b, i], s, bat ^ 4,
+        )
+
+    @jax.named_scope("reduce_near")
+    def reduce_near(b, i):
         @pl.when(c == 0)
         def _():
             core_copy(b, i).wait_recv()
             for cc in range(2):
-                for j in range(1, 4):
-                    z_copy(b, i, cc, j).start()
-
-    def finish_z(b):
-        for i, (at, size) in enumerate(CHUNKS):
-            for j in range(1, 4):
-                drain(zrecv.at[b, z ^ j, pl.ds(at, size)], sR_r.at[b, i, z ^ j])
-        for k in range(TAPS):
-            done = yrecv[b, k, z].astype(jnp.float32)
-            for j in range(1, 4):
-                done = done + zrecv[b, z ^ j, k].astype(jnp.float32)
-            fin[b, k] = done.astype(jnp.bfloat16)
-
-        @pl.when(b == s)
-        def _():
-            gfin[:, s] = fin[b]
-
-        @pl.when(b != s)
-        def _():
-            swap_copy(fin.at[b], gfin.at[:, s], sG_s.at[b], sG_r.at[s], b, bat).start()
-
+                for slot in (1, 0):
+                    z_near(b, i, cc, slot).start()
+
+    @jax.named_scope("reduce_far")
+    def reduce_far(b, i):
+        at, size = CHUNKS[i]
+
+        @pl.when(c == 0)
+        def _():
+            drain(zrecv.at[b, :, pl.ds(0, 2), pl.ds(at, size)], sN_r.at[b, i])
+            for cc in range(2):
+                mine = (yrecv, zs1)[cc]
+                for k in range(at, at + size):
+                    zrecv[b, cc, 1, k] = (
+                        zrecv[b, cc, 1, k].astype(jnp.float32) + mine[b, k, z ^ 2].astype(jnp.float32)
+                    ).astype(jnp.bfloat16)
+                z_far(b, i, cc).start()
+
+    @jax.named_scope("finish")
+    def finish(b, i):
+        at, size = CHUNKS[i]
+
+        @pl.when(c == 0)
+        def _():
+            drain(zrecv.at[b, :, 2, pl.ds(at, size)], sT_r.at[b, i])
+            for cc in range(2):
+                mine = (yrecv, zs1)[cc]
+                for k in range(at, at + size):
+                    zrecv[b, cc, 0, k] = (
+                        zrecv[b, cc, 0, k].astype(jnp.float32)
+                        + zrecv[b, cc, 2, k].astype(jnp.float32)
+                        + mine[b, k, z].astype(jnp.float32)
+                    ).astype(jnp.bfloat16)
+
+                def deliver(section, core):
+                    swap_copy(
+                        zrecv.at[b, cc, 0, pl.ds(at, size)], gfin.at[pl.ds(at, size), s],
+                        sG_s.at[b, cc], sG_r.at[s], section, 2 * z + core,
+                    ).start()
+
+                @pl.when(b != s)
+                def _():
+                    deliver(b, cc)
+
+                @pl.when(b == s)
+                def _():
+                    if cc == 0:
+                        for k in range(at, at + size):
+                            gfin[k, s] = zrecv[b, 0, 0, k]
+                    else:
+                        deliver(s, 1)
+
+    @jax.named_scope("backward")
     def backward(bi):
         b = 3 - bi
-        par = lax.rem(bi, 2)
         e = 8 + 2 * bi
         first_sum = jnp.zeros((1, D), jnp.float32)
         second_sum = jnp.zeros((1, D), jnp.float32)
@@ -800,19 +950,23 @@
             second_sum += jnp.sum(du * sv[b, 2, i : i + 64].astype(jnp.float32), 0, keepdims=True)
         sums_start(e, first_sum, second_sum)
 
+        @pl.when(bi == 0)
+        def _():
+            close_gather()
+
         @pl.when(bi > 0)
         def _():
-            grad_point(b + 1, 1 - par)
+            forward_dz(b + 1, 1)
 
         @pl.when(bi > 1)
         def _():
-            for i in range(3):
-                reduce_plane(b + 2, par, i)
-            for i in range(3):
-                y_copy(b + 2, par, i).wait_send()
-            for kind in range(2):
-                for j in range(1, 4):
-                    dz_copy(b + 2, par, kind, j).wait_send()
+            grad_point(b + 2)
+
+        @pl.when(bi > 2)
+        def _():
+            reduce_near(3, 0)
+            reduce_plane(3, 1)
+            reduce_plane(3, 2)
 
         total_first, total_second = sums_finish(e)
         for i in range(0, R, 64):
@@ -820,14 +974,19 @@
             inner = zbuf[i : i + 64] - valid[i : i + 64] * (
                 (total_first + xhat * total_second) / row_count
             )
-            dzq[par, 1, u, i : i + 64] = (gi[b, 1:2] * inner).astype(jnp.bfloat16)
-        send_dz(b, par, 1)
+            dzq[b, 1, u, i : i + 64] = (gi[b, 1:2] * inner).astype(jnp.bfloat16)
+        send_dz(b, 1)
+
+        @pl.when(bi == 3)
+        def _():
+            send_share(0, 1)
+
         gsend[b, 2:3] = total_second
         gsend[b, 3:4] = total_first
-        d_two = dzq[par, 1, u]
+        d_two = dzq[b, 1, u]
         for k in range(9):
             Hb[:, k * D : (k + 1) * D] = jnp.dot(
-                Gm[u, pl.ds((8 - k) * R, R)], d_two, preferred_element_type=jnp.float32
+                Gm[c, pl.ds((8 - k) * R, R)], d_two, preferred_element_type=jnp.float32
             ).astype(jnp.bfloat16)
         mixed = None
         for k in range(9):
@@ -845,16 +1004,22 @@
             first_sum += jnp.sum(du, 0, keepdims=True)
             second_sum += jnp.sum(du * sv[b, 0, i : i + 64].astype(jnp.float32), 0, keepdims=True)
         sums_start(e + 1, first_sum, second_sum)
-        for j in range(1, 4):
-            v = u ^ j
-            for kind in range(2):
-                drain(caq.at[b, kind, v], sQ_r.at[b, kind, v])
-        grad_spatial(b, par)
-
-        @pl.when(bi > 1)
-        def _():
-            for i in range(3):
-                reduce_z(b + 2, i)
+
+        @pl.when(bi > 0)
+        def _():
+            grad_spatial(b + 1)
+            forward_dz(b + 1, 0)
+
+        @pl.when(bi == 2)
+        def _():
+            reduce_plane(3, 0)
+
+        @pl.when(bi > 2)
+        def _():
+            reduce_near(3, 1)
+            reduce_near(3, 2)
+            reduce_plane(2, 0)
+            reduce_far(3, 0)
 
         total_first, total_second = sums_finish(e + 1)
         for i in range(0, R, 64):
@@ -862,12 +1027,17 @@
             inner = zbuf[i : i + 64] - valid[i : i + 64] * (
                 (total_first + xhat * total_second) / row_count
             )
-            dzq[par, 0, u, i : i + 64] = (gi[b, 0:1] * inner).astype(jnp.bfloat16)
-        send_dz(b, par, 0)
+            dzq[b, 0, u, i : i + 64] = (gi[b, 0:1] * inner).astype(jnp.bfloat16)
+        send_dz(b, 0)
+
+        @pl.when(bi == 2)
+        def _():
+            send_share(0, 0)
+
         gsend[b, 0:1] = total_second
         gsend[b, 1:2] = total_first
         g[...] = g[...] + lax.dot_general(
-            dzq[par, 0, u], W[b, 9].reshape(D, D), NT, preferred_element_type=jnp.float32
+            dzq[b, 0, u], W[b, 9].reshape(D, D), NT, preferred_element_type=jnp.float32
         )
 
         @pl.when(b == s)
@@ -876,7 +1046,7 @@
 
         @pl.when(b != s)
         def _():
-            swap_copy(gsend.at[b], gaff.at[s], sO_s.at[4 + b], sO_r.at[s], b, bat).start()
+            swap_copy(gsend.at[b], gaff.at[s], sO_s.at[4 + b], sO_r, b, bat).start()
 
     @pl.loop(0, 4)
     def _(bi):
@@ -885,129 +1055,156 @@
     out_grad_in = pltpu.make_async_copy(g, in_grad.at[0], sO_s.at[1])
     out_grad_in.start()
 
-    finish_z(3)
-    for i in range(3):
-        reduce_plane(1, 0, i)
-    for i in range(3):
-        reduce_z(1, i)
-    grad_point(0, 1)
-    finish_z(2)
-    for i in range(3):
-        reduce_plane(0, 1, i)
-        reduce_z(0, i)
-    finish_z(1)
-    finish_z(0)
-    loads[4].wait()
-    loads[5].wait()
+    reduce_near(2, 0)
+    grad_point(1)
+    reduce_far(3, 1)
+    reduce_far(3, 2)
+    reduce_plane(2, 1)
+    forward_dz(0, 1)
+    grad_spatial(0)
+    reduce_near(2, 1)
+    reduce_plane(2, 2)
+    reduce_far(2, 0)
+    finish(3, 0)
+    finish(3, 1)
+    reduce_near(2, 2)
+    forward_dz(0, 0)
+    reduce_plane(1, 0)
+    grad_point(0)
+    reduce_near(1, 0)
+    reduce_far(2, 1)
+    finish(3, 2)
+    finish(2, 0)
+    reduce_far(2, 2)
+    reduce_plane(1, 1)
+    reduce_plane(1, 2)
+    reduce_near(1, 1)
+    reduce_near(1, 2)
+    reduce_far(1, 0)
+    finish(2, 1)
+    finish(2, 2)
+    reduce_plane(0, 0)
+    reduce_near(0, 0)
+    reduce_far(1, 1)
+    reduce_far(1, 2)
+    finish(1, 0)
+    finish(1, 1)
+    reduce_plane(0, 1)
+    reduce_plane(0, 2)
+    reduce_near(0, 1)
+    reduce_near(0, 2)
+    reduce_far(0, 0)
+    finish(1, 2)
+    finish(0, 0)
+    reduce_far(0, 1)
+    reduce_far(0, 2)
+    finish(0, 1)
+    close_rest()
+    finish(0, 2)
     for d in range(1, 4):
         drain(gfin.at[:, s ^ d], sG_r.at[s ^ d])
-        drain(gaff.at[s ^ d], sO_r.at[s ^ d])
-
-    def square(ref, taps):
-        part = jnp.zeros((1, D), jnp.float32)
-        for k in taps:
-            v = ref[k].astype(jnp.float32).reshape(64, D)
-            part += jnp.sum(v * v, 0, keepdims=True)
-        return part
+
+    @pl.when(c == 1)
+    def _():
+        drain(gfin.at[:, s], sG_r.at[s])
+
+    grads_out = pltpu.make_async_copy(gfin, grads, sO_s.at[2])
+    grads_out.start()
 
     def lane_sum(v):
         return jnp.sum(v, axis=1, keepdims=True)
 
-    squares = [square(r, t) for r in (pbuf, gfin) for t in (range(9, 10), range(9))]
+    gspatial_squares = jnp.zeros((1, D), jnp.float32)
+    for k in range(9):
+        gspatial_squares += square(gfin[k].astype(jnp.float32).reshape(64, D))
+    gpoint_squares = square(gfin[9].astype(jnp.float32).reshape(64, D))
     lanes = lax.broadcasted_iota(jnp.int32, (1, D), 1)
     tile = jnp.zeros((1, D), jnp.float32)
-    for i, part in enumerate(squares):
+    for i, part in enumerate((point_squares, spatial_squares, gpoint_squares, gspatial_squares)):
         tile = jnp.where(lanes == i, lane_sum(part), tile)
     sums_start(16, tile, tile)
+    drain(gaff.at[pl.ds(0, 3)], sO_r)
+    affine_out[...] = gaff[0] + gaff[1] + gaff[2] + gaff[3]
     totals, _ = sums_finish(16)
+    totals_out[...] = jnp.concatenate([totals] * 8, axis=0)
+
+    with jax.named_scope("close_last"):
+        sums_close(16)
+
+        @pl.when(c == 0)
+        def _():
+            @pl.loop(0, 4)
+            def _(b):
+                drain(zrecv.at[b, 1, 0], sG_s.at[b, 1])
+
+                @pl.when(b != s)
+                def _():
+                    drain(zrecv.at[b, 0, 0], sG_s.at[b, 0])
+
+    with jax.named_scope("close_outputs"):
+        grads_out.wait()
+        out_features.wait()
+        out_grad_in.wait()
+
+
+def lars_kernel(
+    feat, ing, grads_in, totals_in, affine_in, w_point, w_spatial, norm_in, mom_point, mom_spatial, mom_norm,
+    features, in_grad, new_point, new_spatial, new_norm, new_mom_point, new_mom_spatial, new_mom_norm,
+    P, M, G, feat_rows, grad_rows, totals, affine_grad, affine, affine_mom, sem, out_sem,
+):
+    loads = [
+        (totals_in, totals), (affine_in, affine_grad), (norm_in.at[0], affine), (mom_norm.at[0], affine_mom),
+        (grads_in, G), (w_spatial.at[0], P.at[pl.ds(0, 9)]), (mom_spatial.at[0], M.at[pl.ds(0, 9)]),
+        (w_point.at[0], P.at[9]), (mom_point.at[0], M.at[9]),
+    ]
+    loads = [pltpu.make_async_copy(a, b, sem.at[i]) for i, (a, b) in enumerate(loads)]
+    for load in loads:
+        load.start()
+    passed = [
+        pltpu.make_async_copy(feat, feat_rows, sem.at[9]),
+        pltpu.make_async_copy(ing, grad_rows, sem.at[10]),
+    ]
+    for copy in passed:
+        copy.start()
+    for load in loads:
+        load.wait()
+    D = affine.shape[1]
     rate = BASE_RATE * (STEP + 1) / WARMUP
-    point_sq, spatial_sq, gpoint_sq, gspatial_sq = [totals[:, i : i + 1] for i in range(4)]
+    point_sq, spatial_sq, gpoint_sq, gspatial_sq = [totals[0:1, i : i + 1] for i in range(4)]
     step_point = rate * TRUST_COEF * jnp.sqrt(point_sq) / (jnp.sqrt(gpoint_sq) + EPS_NORM)
     step_spatial = rate * TRUST_COEF * jnp.sqrt(spatial_sq) / (jnp.sqrt(gspatial_sq) + EPS_NORM)
-    for k in range(TAPS):
-        grad = gfin[k].astype(jnp.float32).reshape(64, D)
-        moved = MOMENTUM * mbuf[k] + (step_point if k == 9 else step_spatial) * grad
-        mbuf[k] = moved
-        pbuf[k] = pbuf[k] - moved
-    outs = [
-        pltpu.make_async_copy(pbuf.at[9], new_point.at[0], sW.at[0]),
-        pltpu.make_async_copy(pbuf.at[pl.ds(0, 9)], new_spatial.at[0], sW.at[1]),
-        pltpu.make_async_copy(mbuf.at[9], new_mom_point.at[0], sW.at[2]),
-        pltpu.make_async_copy(mbuf.at[pl.ds(0, 9)], new_mom_spatial.at[0], sW.at[3]),
-    ]
-    for out in outs:
-        out.start()
-    affine_grad = (gaff[0] + gaff[1] + gaff[2] + gaff[3])[0:4]
-    affine = norm_in[0]
-    affine_sq = lane_sum(affine * affine)
-    gaffine_sq = lane_sum(affine_grad * affine_grad)
+    outs = []
+
+    def store(source, target):
+        outs.append(pltpu.make_async_copy(source, target, out_sem.at[len(outs)]))
+        outs[-1].start()
+
+    for k in range(10):
+        grad = G[k].astype(jnp.float32).reshape(64, D)
+        moved = MOMENTUM * M[k] + (step_point if k == 9 else step_spatial) * grad
+        M[k] = moved
+        P[k] = P[k] - moved
+        if k in (2, 5, 8):
+            taps = pl.ds(k - 2, 3)
+            store(M.at[taps], new_mom_spatial.at[0, taps])
+            store(P.at[taps], new_spatial.at[0, taps])
+    for copy, rows, target in zip(passed, (feat_rows, grad_rows), (features, in_grad)):
+        copy.wait()
+        store(rows, target)
+    store(M.at[9], new_mom_point.at[0])
+    store(P.at[9], new_point.at[0])
+    grad = affine_grad[0:4]
+    old = affine[...]
+    affine_sq = jnp.sum(old * old, axis=1, keepdims=True)
+    gaffine_sq = jnp.sum(grad * grad, axis=1, keepdims=True)
     trust = TRUST_COEF * jnp.sqrt(affine_sq) / (jnp.sqrt(gaffine_sq) + EPS_NORM)
-    moved = MOMENTUM * mom_norm[0] + rate * trust * affine_grad
-    new_mom_norm[0] = moved
-    new_norm[0] = affine - moved
-
-    for d in range(1, 4):
-        scatter(d).wait_send()
-        swap_copy(aff.at[s], aff.at[s], sF_s.at[d], sF_r.at[s], s ^ d, bat).wait_send()
-
-    @pl.when(c == 1)
-    def _():
-        scatter(0).wait_send()
-
-    for j in range(1, 10):
-        if j != 0:
-            drain(cown, sC_s.at[j])
-
-    @pl.loop(0, 4)
-    def _(b):
-        for zz in range(4):
-            drain(pair(b, half, zz, s), sA_s.at[b, zz])
-            for which in range(2):
-                drain(pair(b, half, zz, s), sB_s.at[b, which, zz])
-        for which in range(3):
-            drain(W.at[b, half, :, s], sD_s.at[b, which])
-        for kind in range(2):
-            for j in range(1, 4):
-                drain(stage.at[b, kind, u], sQ_s.at[b, kind, j])
-
-        @pl.when(c == 0)
-        def _():
-            for j in range(1, 4):
-                drain(pair(b, slice(None), z, s), sZ_s.at[b, j])
-            for zz in range(4):
-                drain(pair(b, slice(None), zz, s), sH_s.at[b, zz])
-            for i, (at, size) in enumerate(CHUNKS):
-                for cc in range(2):
-                    for j in range(1, 4):
-                        drain(zrecv.at[b, z, pl.ds(at, size)], sR_s.at[b, i, cc, j])
-
-        @pl.when(c == 1)
-        def _():
-            for i, (at, size) in enumerate(CHUNKS):
-                drain(zs1.at[b, pl.ds(at, size)], sK_s.at[b, i])
-
-        @pl.when(b != s)
-        def _():
-            drain(fin.at[b], sG_s.at[b])
-            drain(gsend.at[b], sO_s.at[4 + b])
-
-        @pl.when(b < 2)
-        def _():
-            par = lax.rem(3 - b, 2)
-            for i in range(3):
-                y_copy(b, par, i).wait_send()
-            for kind in range(2):
-                for j in range(1, 4):
-                    dz_copy(b, par, kind, j).wait_send()
-
-    @pl.loop(0, 17)
-    def _(e):
-        sums_close(e)
-
-    out_features.wait()
-    out_grad_in.wait()
-    for out in outs:
-        out.wait()
+    moved = MOMENTUM * affine_mom[...] + rate * trust * grad
+    affine_mom[...] = moved
+    affine[...] = old - moved
+    store(affine_mom, new_mom_norm.at[0])
+    store(affine, new_norm.at[0])
+    for copy in outs:
+        copy.wait()
 
 
 def train_step(images, crop, w_point, w_spatial, norm_params, mom_point, mom_spatial, mom_norm, out_grad):
@@ -1016,48 +1213,62 @@
     dma = pltpu.SemaphoreType.DMA
     anywhere = pl.BlockSpec(memory_space=pl.ANY)
     vmem = pl.BlockSpec(memory_space=pltpu.VMEM)
+    hbm = pl.BlockSpec(memory_space=pltpu.HBM)
     smem = pl.BlockSpec(memory_space=pltpu.SMEM)
     V = pltpu.VMEM
     scratch = dict(
         W=V((4, TAPS, 8, 4, 16, D), bf16), wown=V((TAPS, 4, 16, D), bf16),
-        pbuf=V((TAPS, 64, D), f32), mbuf=V((TAPS, 64, D), f32),
-        h=V((R, D), f32), g=V((R, D), f32), zbuf=V((R, D), f32),
+        F=V((3 * R, D), f32),
         sv=V((4, 4, R, D), bf16), gi=V((4, 8, D), f32),
         abuf=V((R, D), bf16), gbuf=V((R, D), bf16),
         Gm=V((4, 9 * R, R), bf16), caq=V((4, 2, 4, 8, 16, R), bf16),
         stage=V((4, 2, 4, 8, 16, R), bf16), Hb=V((R, 9 * D), bf16),
-        GcT=V((9, 128, 4 * R), bf16), dzq=V((2, 2, 4, R, D), bf16),
-        gout=V((2, 2, TAPS, 4, 16, D), bf16), yrecv=V((4, TAPS, 4, 16, D), bf16),
-        zs1=V((4, TAPS, 4, 16, D), bf16), zrecv=V((4, 4, TAPS, 16, D), bf16),
-        fin=V((4, TAPS, 16, D), bf16), gfin=V((TAPS, 4, 16, D), bf16),
+        dzq=V((4, 2, 4, R, D), bf16),
+        gout=V((4, 2, TAPS, 4, 16, D), bf16), yrecv=V((4, TAPS, 4, 16, D), bf16),
+        zs1=V((4, TAPS, 4, 16, D), bf16), zrecv=V((4, 2, 3, TAPS, 16, D), bf16),
+        gfin=V((TAPS, 4, 16, D), bf16),
         aff=V((4, 8, D), f32), gaff=V((4, 8, D), f32), gsend=V((4, 8, D), f32),
         st_in=V((17, 8, 128), f32), st_own=V((17, 8, 128), f32), st_all=V((17, 4, 8, 128), f32),
         cnt=V((8, 8, 128), f32), cntx=V((4, 8, 128), f32), cown=V((8, 128), f32),
-        sL=dma((6,)), sS_s=dma((4,)), sS_r=dma((4, 2)), sZ_s=dma((4, 4)), sZ_r=dma((4, 4)),
-        sH_s=dma((4, 4)), sH_r=dma((4, 4)), sA_s=dma((4, 4)), sA_r=dma((4, 4)),
-        sB_s=dma((4, 2, 4)), sB_r=dma((4, 2, 4)), sD_s=dma((4, 3)), sD_r=dma((4, 3)),
-        sE_in_s=dma((17,)), sE_in_r=dma((17,)), sE_s=dma((17, 8)), sE_r=dma((17, 4)),
-        sC_s=dma((12,)), sC_r=dma((12,)), sF_s=dma((4,)), sF_r=dma((4,)),
-        sQ_s=dma((4, 2, 4)), sQ_r=dma((4, 2, 4)), sX_s=dma((4, 2, 4)), sX_r=dma((4, 2, 4)),
+        sL=dma((12,)), sS_s=dma, sS_r=dma((4, 2)), sZ_s=dma((4,)), sZ_r=dma((4, 4)),
+        sH_s=dma((4,)), sH_r=dma((4, 4)), sA_s=dma((4,)), sA_r=dma((4, 4)),
+        sB_s=dma((4, 2)), sB_r=dma((4, 2)), sD_s=dma((4, 3)), sD_r=dma((4, 3)),
+        sE_in_s=dma((17,)), sE_in_r=dma((17,)), sE_s=dma((17,)), sE_r=dma((17,)),
+        sC_s=dma, sC_r=dma((2,)), sF_s=dma, sF_r=dma,
+        sQ_s=dma((4, 2)), sQ_r=dma((4, 2)), sX_s=dma((4, 2)), sX_r=dma((4, 2, 4)),
         sY_s=dma((4, 3)), sY_r=dma((4, 3)), sK_s=dma((4, 3)), sK_r=dma((4, 3)),
-        sR_s=dma((4, 3, 2, 4)), sR_r=dma((4, 3, 4)), sG_s=dma((4,)), sG_r=dma((4,)),
-        sO_s=dma((8,)), sO_r=dma((4,)), sW=dma((4,)),
+        sN_s=dma((4, 3)), sN_r=dma((4, 3)), sT_s=dma((4, 3)), sT_r=dma((4, 3)), sG_s=dma((4, 2)), sG_r=dma((4,)),
+        sO_s=dma((8,)), sO_r=dma,
     )
     shape = jax.ShapeDtypeStruct
+    feat, ing, grads, totals, affine_grad = pl.pallas_call(
+        train_kernel,
+        out_shape=(
+            shape((1, R, D), f32), shape((1, R, D), f32), shape((TAPS, 4, 16, D), bf16),
+            shape((8, D), f32), shape((8, D), f32),
+        ),
+        in_specs=[anywhere, smem, anywhere, anywhere, vmem, anywhere],
+        out_specs=(anywhere, anywhere, anywhere, vmem, vmem),
+        scratch_shapes=list(scratch.values()),
+        compiler_params=pltpu.CompilerParams(
+            collective_id=0, has_side_effects=True, vmem_limit_bytes=64 * 1024 * 1024
+        ),
+    )(images, crop.T, w_point, w_spatial, norm_params, out_grad)
     return pl.pallas_call(
-        train_kernel,
+        lars_kernel,
         out_shape=(
             shape((1, R, D), f32), shape((1, R, D), f32),
             shape(w_point.shape, f32), shape(w_spatial.shape, f32), shape(norm_params.shape, f32),
             shape(w_point.shape, f32), shape(w_spatial.shape, f32), shape(norm_params.shape, f32),
         ),
-        in_specs=[anywhere, smem, anywhere, anywhere, vmem, anywhere, anywhere, vmem, anywhere],
-        out_specs=(anywhere, anywhere, anywhere, anywhere, vmem, anywhere, anywhere, vmem),
-        scratch_shapes=list(scratch.values()),
-        compiler_params=pltpu.CompilerParams(
-            collective_id=0, has_side_effects=True, vmem_limit_bytes=64 * 1024 * 1024
-        ),
-    )(images, crop, w_point, w_spatial, norm_params, mom_point, mom_spatial, mom_norm, out_grad)
+        in_specs=[hbm] * 11,
+        out_specs=(hbm,) * 8,
+        scratch_shapes=[
+            V((TAPS, 64, D), f32), V((TAPS, 64, D), f32), V((TAPS, 4, 16, D), bf16), V((1, R, D), f32),
+            V((1, R, D), f32), V((8, D), f32), V((8, D), f32), V((4, D), f32), V((4, D), f32), dma((11,)), dma((12,)),
+        ],
+        compiler_params=pltpu.CompilerParams(vmem_limit_bytes=64 * 1024 * 1024),
+    )(feat, ing, grads, totals, affine_grad, w_point, w_spatial, norm_params, mom_point, mom_spatial, mom_norm)
 
 
 def solution(mesh):

time: 325 us -> 238 us (0.73)
  Pallas kernels: 315 us -> 237 us
  local copies, waits for them, and re-layouts: 8.67 us -> 0 us
    pallas_call x1, Pallas kernels: 315 us -> 233 us  [train_step(): pl.pallas_call(train_kernel, out_shape=(shape((1, R, D), f32), shape((1,...]
    unnamed x23 -> x0, local copies, waits for them, and re-layouts: 8.67 us -> none
    pallas_call x0 -> x1, Pallas kernels: none -> 4.2 us  [train_step(): pl.pallas_call(lars_kernel, out_shape=(shape((1, R, D), f32), shape((1, R...]
where the time goes in v2:
time: 238 us
  Pallas kernels  237 us (100%)
    pallas_call x1, Pallas kernels, train_step(): pl.pallas_call(train_kernel, out_shape=(shape((1, R, D), f32), shape((1,...  233 us

profile of v2, /device:TPU:0, one launch (start us, length us, event | category | flops | bytes accessed | tf_op | source)
XLA Modules:
  0.0 238.1 jit_solution(8931086597483688165)
XLA Ops:
  0.6 233.1 %shard_map.152 = (f32[1,256,512]{2,1,0:T(8,128)}, f32[1,256,512]{2,1,0:T(8,128)}, bf16[10,4,16,512]{3,2,1,0:T(8,128)(2,1)}, f32[8,512]{1,0:T(8,128)}, f32[8,512]{1,0:T(8,128)}) custom-call(bf16[4,256,512]{2,1,0:T(8,128)(2,1)} %images.1, s32[1,4]{1,0:T(1,128)} %bitcast.1, f32[1,64,512]{2,1,0:T(8,128)} %w_point.3, f32[1,9,64,512]{3,2,1,0:T(8,128)} %w_spatial.3, ...), custom_call_target="tpu_custom_call" | custom-call | tf_op jit(solution)/shard_map/pallas_call | solution.py:1244
  233.7 4.2 %shard_map.153 = (f32[1,256,512]{2,1,0:T(8,128)}, f32[1,256,512]{2,1,0:T(8,128)}, f32[1,64,512]{2,1,0:T(8,128)}, f32[1,9,64,512]{3,2,1,0:T(8,128)}, f32[1,4,512]...) custom-call(f32[1,256,512]{2,1,0:T(8,128)} %get-tuple-element.13.feat, ...), custom_call_target="tpu_custom_call" | custom-call | tf_op jit(solution)/shard_map/pallas_call | solution.py:1257

commit v3 on v2

--- a/solution.py
+++ b/solution.py
@@ -1,3 +1,5 @@
+import functools
+
 import jax
 import jax.numpy as jnp
 from jax import lax
@@ -365,10 +367,10 @@
 def train_kernel(
     images, crop, w_point, w_spatial, norm_in, out_grad,
     features, in_grad, grads, totals_out, affine_out,
-    W, wown, F, sv, gi, abuf, gbuf, Gm, caq, stage, Hb, dzq, gout, yrecv,
+    W, wown, F, sv, gi, abuf, Gm, caq, stage, stage_a, Hb, dzq, dz1q, pgrad, precv, gout, yrecv,
     zs1, zrecv, gfin, aff, gaff, gsend, st_in, st_own, st_all, cnt, cntx, cown,
     sL, sS_s, sS_r, sZ_s, sZ_r, sH_s, sH_r, sA_s, sA_r, sB_s, sB_r, sD_s, sD_r,
-    sE_in_s, sE_in_r, sE_s, sE_r, sC_s, sC_r, sF_s, sF_r, sQ_s, sQ_r, sX_s, sX_r,
+    sE_in_s, sE_in_r, sE_s, sE_r, sC_s, sC_r, sF_s, sF_r, sQ_s, sQ_r, sX_s, sX_r, sM_s, sM_r, sP_s, sP_r,
     sY_s, sY_r, sK_s, sK_r, sN_s, sN_r, sT_s, sT_r, sG_s, sG_r, sO_s, sO_r,
 ):
     s = lax.axis_index("section")
@@ -377,7 +379,6 @@
     c = lax.rem(bat, 2)
     x = lax.rem(s, 2)
     y = s // 2
-    u = 2 * x + c
     R, D = abuf.shape
     h = F.at[pl.ds(0, R)]
     g = F.at[pl.ds(R, R)]
@@ -390,7 +391,6 @@
             for k in range(9)
         ],
         pltpu.make_async_copy(images.at[s], abuf, sL.at[10]),
-        pltpu.make_async_copy(out_grad.at[s], gbuf, sL.at[11]),
     ]
     for load in loads:
         load.start()
@@ -443,7 +443,8 @@
     for j in range(1, 8):
         swap_copy(cown, cnt.at[bat], sC_s, sC_r.at[0], s, bat ^ j).start()
     for j in range(2):
-        swap_copy(cown, cntx.at[2 + c], sC_s, sC_r.at[1], s ^ 1, bat ^ j).start()
+        for near in (1, 2):
+            swap_copy(cown, cntx.at[2 * near + c], sC_s, sC_r.at[1], s ^ near, bat ^ j).start()
     for d in range(1, 4):
         swap_copy(aff.at[s], aff.at[s], sF_s, sF_r, s ^ d, bat).start()
 
@@ -501,7 +502,7 @@
             for j in range(1, 4):
                 spread_z(b, j).start()
 
-        @pl.when(b < 2)
+        @pl.when(b < 3)
         def _():
             own_ready(b, z)
 
@@ -538,7 +539,7 @@
             drain(W.at[b, other, :, (second, first, both)[which]], sD_r.at[b, which])
 
     drain(cnt.at[pl.ds(0, 7)], sC_r.at[0])
-    drain(cntx.at[pl.ds(2, 2)], sC_r.at[1])
+    drain(cntx.at[pl.ds(2, 4)], sC_r.at[1])
     cntx[1 - c] = cnt[bat ^ 1]
     total = jnp.zeros((1, 1), jnp.float32)
     for j in range(8):
@@ -550,7 +551,7 @@
     down = lax.broadcasted_iota(jnp.int32, (R, 1), 0).astype(jnp.float32)
     across = lax.broadcasted_iota(jnp.int32, (1, R), 1).astype(jnp.float32)
 
-    @pl.loop(0, 4)
+    @pl.loop(0, 6)
     @jax.named_scope("tables")
     def _(v):
         big = cntx[v][0:1, 0:1]
@@ -614,33 +615,55 @@
         spread = lax.rsqrt(sums[1] / row_count - center * center + EPS)
         return center, spread
 
+    def pairing(b):
+        odd = lax.rem(b, 2) == 1
+        return jnp.where(odd, x, y), jnp.where(odd, y, x), jnp.where(odd, 1, 2)
+
     @jax.named_scope("share")
     def share(b, kind, rows):
         turned = rows.T
+        rows_to = stage_a if kind == 1 else stage.at[b]
+        if kind == 1:
+            @pl.when(b > 0)
+            def _():
+                drain(stage_a.at[pl.ds(0, 2)], sQ_s.at[b - 1, 1])
+
+        odd = lax.rem(b, 2) == 1
         for cc in range(2):
             for xx in range(2):
                 for yy in range(2):
+                    one, two = jnp.where(odd, xx, yy), jnp.where(odd, yy, xx)
                     for zz in range(4):
                         at = (2 * zz + cc) * 64 + (2 * yy + xx) * 16
-                        stage[b, kind, 2 * xx + cc, 4 * yy + zz] = turned[at : at + 16].astype(
+                        rows_to[2 * one + cc, 4 * two + zz] = turned[at : at + 16].astype(
                             jnp.bfloat16
                         )
-        caq[b, kind, u] = stage[b, kind, u]
-
-        @pl.when(b == 3)
-        def _():
-            send_share(b, kind)
-
-    def send_share(b, kind):
+        if kind == 1:
+            for half_of_pair in range(2):
+                v = 2 * half_of_pair
+                caq[b, 1, v + c] = stage_a[v + c]
+                swap_copy(
+                    stage_a.at[v + 1 - c], caq.at[b, 1, v + c], sQ_s.at[b, 1], sQ_r.at[b, 1], s, bat ^ 1
+                ).start()
+        else:
+            u = 2 * pairing(b)[0] + c
+            caq[b, 0, u] = stage[b, u]
+
+            @pl.when(b == 3)
+            def _():
+                send_share(b)
+
+    def send_share(b):
+        mine, _, near = pairing(b)
+        u = 2 * mine + c
         for j in range(1, 4):
             swap_copy(
-                stage.at[b, kind, u ^ j], caq.at[b, kind, u], sQ_s.at[b, kind],
-                sQ_r.at[b, kind], s ^ (j // 2), bat ^ (j % 2),
+                stage.at[b, u ^ j], caq.at[b, 0, u], sQ_s.at[b, 0], sQ_r.at[b, 0],
+                s ^ near if j > 1 else s, bat ^ (j % 2),
             ).start()
 
-    @jax.named_scope("wait_share")
     def wait_share(b, kind):
-        drain(caq.at[b, kind, pl.ds(0, 3)], sQ_r.at[b, kind])
+        drain(caq.at[b, kind, pl.ds(0, 2 if kind == 1 else 3)], sQ_r.at[b, kind])
 
     @jax.named_scope("forward")
     def forward(b):
@@ -648,9 +671,8 @@
 
         @pl.when(b == 3)
         def _():
-            for early in (2, 1):
-                for kind in range(2):
-                    send_share(early, kind)
+            for early in (2, 1, 0):
+                send_share(early)
 
         hidden = h[...]
         zbuf[...] = jnp.dot(
@@ -665,7 +687,8 @@
 
         @pl.when(b < 2)
         def _():
-            gather_z(b + 2)
+            gather_first(b + 1)
+
 
         norms = aff[b]
         center, spread = moments(sums_finish(2 * b))
@@ -691,13 +714,18 @@
         )
         share(b, 0, mixed.astype(jnp.float32))
 
-        @pl.when(b < 2)
-        def _():
-            gather_first(b + 2)
-
-        @pl.when(b < 3)
-        def _():
-            gather_second(b + 1)
+        @pl.when(b == 0)
+        def _():
+            gather_z(2)
+
+        @pl.when(b == 1)
+        def _():
+            own_ready(3, z)
+            gather_z(3)
+
+        @pl.when(b == 2)
+        def _():
+            gather_first(3)
 
         center, spread = moments(sums_finish(2 * b + 1))
         gi[b, 1:2] = norms[2:3] * spread
@@ -709,26 +737,30 @@
             h[i : i + 64] = h[i : i + 64] + valid[i : i + 64] * value
 
     gather_z(0)
-    own_ready(2, z)
     gather_first(0)
-    own_ready(3, z)
     gather_z(1)
-    gather_first(1)
     gather_second(0)
 
     @pl.loop(0, 4)
     def _(b):
         forward(b)
 
+        @pl.when(b < 3)
+        def _():
+            gather_second(b + 1)
+
+    out_grad_rows = pltpu.make_async_copy(out_grad.at[s], abuf, sL.at[11])
     out_features = pltpu.make_async_copy(h, features.at[0], sO_s.at[0])
     out_features.start()
-    loads[11].wait()
-    g[...] = gbuf[...].astype(jnp.float32)
+    out_grad_rows.start()
+    out_grad_rows.wait()
+    g[...] = abuf[...].astype(jnp.float32)
 
     @jax.named_scope("close_gather")
     def close_gather():
         drain(aff.at[pl.ds(0, 3)], sF_s)
-        drain(st_own.at[pl.ds(0, 9)], sC_s)
+        drain(st_own.at[pl.ds(0, 11)], sC_s)
+        drain(stage_a.at[pl.ds(0, 2)], sQ_s.at[3, 1])
 
         @pl.when(c == 0)
         def _():
@@ -755,62 +787,78 @@
     def close_rest():
         @pl.loop(0, 4)
         def _(b):
-            for kind in range(2):
-                drain(stage.at[b, kind, pl.ds(0, 3)], sQ_s.at[b, kind])
-                drain(dzq.at[b, kind, pl.ds(0, 3)], sX_s.at[b, kind])
+            drain(stage.at[b, pl.ds(0, 3)], sQ_s.at[b, 0])
+            drain(dzq.at[b, pl.ds(0, 3)], sX_s.at[b])
+            dz_one_copy(b).wait_send()
+            point_copy(b).wait_send()
 
             @pl.when(b != s)
             def _():
                 drain(gsend.at[b], sO_s.at[4 + b])
 
-            for i in range(3):
+            for i in range(len(CHUNKS)):
                 y_copy(b, i).wait_send()
 
-            @pl.when(c == 1)
-            def _():
-                for i, (at, size) in enumerate(CHUNKS):
-                    drain(zs1.at[b, pl.ds(at, size)], sK_s.at[b, i])
-
-            @pl.when(c == 0)
-            def _():
-                for i, (at, size) in enumerate(CHUNKS):
-                    drain(zrecv.at[b, :, pl.ds(0, 2), pl.ds(at, size)], sN_s.at[b, i])
-                    drain(zrecv.at[b, :, 2, pl.ds(at, size)], sT_s.at[b, i])
+        @pl.when(c == 1)
+        def _():
+            for i, (at, size) in enumerate(CHUNKS):
+                drain(zs1.at[pl.ds(at, size)], sK_s.at[3, i])
+
+        def close_z(b, parts):
+            for i in range(len(CHUNKS)):
+                drain(near_like(b, i, parts), sN_s.at[b, i])
+                drain(far_like(b, i, parts), sT_s.at[b, i])
+
+        for b in range(4):
+            carriers(b, functools.partial(close_z, b))
 
         @pl.loop(0, 16)
         def _(e):
             sums_close(e)
 
-    CHUNKS = ((0, 5), (5, 4), (9, 1))
-
-    def dz_copy(b, kind, j):
-        v = u ^ 2 if j == 3 else u
-        ref = dzq.at[b, kind, v]
+    CHUNKS = ((0, 3), (3, 3), (6, 3), (9, 1))
+    LAST = len(CHUNKS) - 1
+
+    def dz_copy(b, j):
+        mine, _, near = pairing(b)
+        v = 2 * mine + c
+        v = v ^ 2 if j == 3 else v
+        ref = dzq.at[b, v]
         return swap_copy(
-            ref, ref, sX_s.at[b, kind], sX_r.at[b, kind, v],
-            s ^ 1 if j == 2 else s, bat if j == 2 else bat ^ 1,
-        )
-
-    def send_dz(b, kind):
-        dz_copy(b, kind, 2).start()
-        dz_copy(b, kind, 1).start()
+            ref, ref, sX_s.at[b], sX_r.at[b, v], s ^ near if j == 2 else s, bat if j == 2 else bat ^ 1
+        )
+
+    def send_dz(b):
+        dz_copy(b, 2).start()
+        dz_copy(b, 1).start()
 
     @jax.named_scope("forward_dz")
-    def forward_dz(b, kind):
-        v = u ^ 2
-        drain(dzq.at[b, kind, v], sX_r.at[b, kind, v])
-        dz_copy(b, kind, 3).start()
+    def forward_dz(b):
+        v = (2 * pairing(b)[0] + c) ^ 2
+        drain(dzq.at[b, v], sX_r.at[b, v])
+        dz_copy(b, 3).start()
 
     @jax.named_scope("wait_dz")
-    def wait_dz(b, kind):
+    def wait_dz(b):
+        u = 2 * pairing(b)[0] + c
         for v in (u ^ 1, u ^ 3):
-            drain(dzq.at[b, kind, v], sX_r.at[b, kind, v])
+            drain(dzq.at[b, v], sX_r.at[b, v])
+
+    def dz_one_copy(b):
+        ref = dz1q.at[b, c]
+        return swap_copy(ref, ref, sM_s.at[b], sM_r.at[b], s, bat ^ 1)
+
+    def point_copy(b):
+        mine, _, near = pairing(b)
+        return swap_copy(
+            pgrad.at[b, 1 - mine], precv.at[b], sP_s.at[b], sP_r.at[b], s ^ near, bat
+        )
 
     def y_copy(b, i):
         at, size = CHUNKS[i]
         return swap_copy(
-            gout.at[b, 1 - y, pl.ds(at, size)], yrecv.at[b, pl.ds(at, size)],
-            sY_s.at[b, i], sY_r.at[b, i], s ^ 2, bat,
+            gout.at[b, 1 - pairing(b)[1], pl.ds(at, size)], yrecv.at[b, pl.ds(at, size)],
+            sY_s.at[b, i], sY_r.at[b, i], s ^ 3 ^ pairing(b)[2], bat,
         )
 
     def grad_tap(b, k, left, right):
@@ -821,9 +869,10 @@
     @jax.named_scope("grad_spatial")
     def grad_spatial(b):
         wait_share(b, 0)
-        wait_dz(b, 1)
-        tables = [jnp.where(x == v // 2, 0, 2) + v % 2 for v in range(4)]
-        right = dzq[b, 1].reshape(4 * R, D)
+        wait_dz(b)
+        mine, _, near = pairing(b)
+        tables = [jnp.where(mine == v // 2, 0, 2 * near) + v % 2 for v in range(4)]
+        right = dzq[b].reshape(4 * R, D)
         for k in range(9):
             left = [
                 lax.dot_general(
@@ -833,22 +882,40 @@
                 for v in range(4)
             ]
             grad_tap(b, k, jnp.concatenate(left, axis=1), right)
-            if k == 4:
-                y_copy(b, 0).start()
-        y_copy(b, 1).start()
+            if k % 3 == 2:
+                y_copy(b, k // 3).start()
 
     @jax.named_scope("grad_point")
     def grad_point(b):
         wait_share(b, 1)
-        wait_dz(b, 0)
-        left = jnp.concatenate([caq[b, 1, v].reshape(128, R) for v in range(4)], axis=1)
-        grad_tap(b, 9, left, dzq[b, 0].reshape(4 * R, D))
-        y_copy(b, 2).start()
+        drain(dz1q.at[b, 1 - c], sM_r.at[b])
+        left = jnp.concatenate(
+            [
+                jnp.concatenate([caq[b, 1, 2 * v + k].reshape(128, R) for v in range(2)], axis=0)
+                for k in range(2)
+            ],
+            axis=1,
+        )
+        part = jnp.dot(
+            left, dz1q[b].reshape(2 * R, D), preferred_element_type=jnp.float32
+        ).astype(jnp.bfloat16)
+        pgrad[b] = part.reshape(2, 2, 4, 16, D)
+        point_copy(b).start()
+
+    @jax.named_scope("pair_point")
+    def pair_point(b):
+        point_copy(b).wait_recv()
+        mine = pairing(b)[0]
+        for yy in range(2):
+            gout[b, yy, 9] = (
+                pgrad[b, mine, yy].astype(jnp.float32) + precv[b, yy].astype(jnp.float32)
+            ).astype(jnp.bfloat16)
+        y_copy(b, LAST).start()
 
     def core_copy(b, i):
         at, size = CHUNKS[i]
         return swap_copy(
-            yrecv.at[b, pl.ds(at, size)], zs1.at[b, pl.ds(at, size)],
+            yrecv.at[b, pl.ds(at, size)], zs1.at[pl.ds(at, size)],
             sK_s.at[b, i], sK_r.at[b, i], s, bat ^ 1,
         )
 
@@ -856,91 +923,114 @@
     def reduce_plane(b, i):
         at, size = CHUNKS[i]
         y_copy(b, i).wait_recv()
+        rest = pairing(b)[1]
         for k in range(at, at + size):
             yrecv[b, k] = (
-                yrecv[b, k].astype(jnp.float32) + gout[b, y, k].astype(jnp.float32)
+                yrecv[b, k].astype(jnp.float32) + gout[b, rest, k].astype(jnp.float32)
             ).astype(jnp.bfloat16)
 
-        @pl.when(c == 1)
-        def _():
-            core_copy(b, i).start()
+        if b == 3:
+
+            @pl.when(c == 1)
+            def _():
+                core_copy(b, i).start()
+
+    def carriers(b, work):
+        if b == 3:
+            pl.when(c == 0)(functools.partial(work, (0, 1)))
+        else:
+            work((0,))
 
     def z_near(b, i, cc, slot):
         at, size = CHUNKS[i]
         return swap_copy(
-            (yrecv, zs1)[cc].at[b, pl.ds(at, size), z ^ (3 if slot else 1)],
-            zrecv.at[b, cc, slot, pl.ds(at, size)], sN_s.at[b, i], sN_r.at[b, i], s, bat ^ 2,
+            (yrecv.at[b], zs1)[cc].at[pl.ds(at, size), z ^ (3 if slot else 1)],
+            zrecv.at[b + cc, slot, pl.ds(at, size)], sN_s.at[b, i], sN_r.at[b, i], s, bat ^ 2,
         )
 
     def z_far(b, i, cc):
         at, size = CHUNKS[i]
         return swap_copy(
-            zrecv.at[b, cc, 1, pl.ds(at, size)], zrecv.at[b, cc, 2, pl.ds(at, size)],
+            zrecv.at[b + cc, 1, pl.ds(at, size)], zrecv.at[b + cc, 2, pl.ds(at, size)],
             sT_s.at[b, i], sT_r.at[b, i], s, bat ^ 4,
         )
+
+    def near_like(b, i, parts):
+        at, size = CHUNKS[i]
+        return zrecv.at[pl.ds(b, len(parts)), pl.ds(0, 2), pl.ds(at, size)]
+
+    def far_like(b, i, parts):
+        at, size = CHUNKS[i]
+        return zrecv.at[pl.ds(b, len(parts)), 2, pl.ds(at, size)]
 
     @jax.named_scope("reduce_near")
     def reduce_near(b, i):
-        @pl.when(c == 0)
-        def _():
-            core_copy(b, i).wait_recv()
-            for cc in range(2):
-                for slot in (1, 0):
+        def work(parts):
+            if b == 3:
+                core_copy(b, i).wait_recv()
+            for slot in (1, 0):
+                for cc in parts:
                     z_near(b, i, cc, slot).start()
+
+        carriers(b, work)
 
     @jax.named_scope("reduce_far")
     def reduce_far(b, i):
         at, size = CHUNKS[i]
 
-        @pl.when(c == 0)
-        def _():
-            drain(zrecv.at[b, :, pl.ds(0, 2), pl.ds(at, size)], sN_r.at[b, i])
-            for cc in range(2):
-                mine = (yrecv, zs1)[cc]
+        def work(parts):
+            drain(near_like(b, i, parts), sN_r.at[b, i])
+            for cc in parts:
+                mine = (yrecv.at[b], zs1)[cc]
                 for k in range(at, at + size):
-                    zrecv[b, cc, 1, k] = (
-                        zrecv[b, cc, 1, k].astype(jnp.float32) + mine[b, k, z ^ 2].astype(jnp.float32)
+                    zrecv[b + cc, 1, k] = (
+                        zrecv[b + cc, 1, k].astype(jnp.float32) + mine[k, z ^ 2].astype(jnp.float32)
                     ).astype(jnp.bfloat16)
                 z_far(b, i, cc).start()
+
+        carriers(b, work)
+
+    def deliver(b, i, cc, section, core):
+        at, size = CHUNKS[i]
+        swap_copy(
+            zrecv.at[b + cc, 0, pl.ds(at, size)], gfin.at[pl.ds(at, size), s],
+            sG_s.at[b, cc], sG_r.at[s], section, 2 * z + core,
+        ).start()
 
     @jax.named_scope("finish")
     def finish(b, i):
         at, size = CHUNKS[i]
 
-        @pl.when(c == 0)
-        def _():
-            drain(zrecv.at[b, :, 2, pl.ds(at, size)], sT_r.at[b, i])
-            for cc in range(2):
-                mine = (yrecv, zs1)[cc]
+        def work(parts):
+            drain(far_like(b, i, parts), sT_r.at[b, i])
+            for cc in parts:
+                mine = (yrecv.at[b], zs1)[cc]
                 for k in range(at, at + size):
-                    zrecv[b, cc, 0, k] = (
-                        zrecv[b, cc, 0, k].astype(jnp.float32)
-                        + zrecv[b, cc, 2, k].astype(jnp.float32)
-                        + mine[b, k, z].astype(jnp.float32)
+                    zrecv[b + cc, 0, k] = (
+                        zrecv[b + cc, 0, k].astype(jnp.float32)
+                        + zrecv[b + cc, 2, k].astype(jnp.float32)
+                        + mine[k, z].astype(jnp.float32)
                     ).astype(jnp.bfloat16)
-
-                def deliver(section, core):
-                    swap_copy(
-                        zrecv.at[b, cc, 0, pl.ds(at, size)], gfin.at[pl.ds(at, size), s],
-                        sG_s.at[b, cc], sG_r.at[s], section, 2 * z + core,
-                    ).start()
 
                 @pl.when(b != s)
                 def _():
-                    deliver(b, cc)
+                    deliver(b, i, cc, b, cc if b == 3 else c)
 
                 @pl.when(b == s)
                 def _():
                     if cc == 0:
                         for k in range(at, at + size):
-                            gfin[k, s] = zrecv[b, 0, 0, k]
+                            gfin[k, s] = zrecv[b, 0, k]
                     else:
-                        deliver(s, 1)
+                        deliver(b, i, 1, s, 1)
+
+        carriers(b, work)
 
     @jax.named_scope("backward")
     def backward(bi):
         b = 3 - bi
         e = 8 + 2 * bi
+        u = 2 * pairing(b)[0] + c
         first_sum = jnp.zeros((1, D), jnp.float32)
         second_sum = jnp.zeros((1, D), jnp.float32)
         for i in range(0, R, 64):
@@ -954,19 +1044,24 @@
         def _():
             close_gather()
 
+        @pl.when(bi == 3)
+        def _():
+            reduce_near(3, 1)
+
         @pl.when(bi > 0)
         def _():
-            forward_dz(b + 1, 1)
-
-        @pl.when(bi > 1)
-        def _():
-            grad_point(b + 2)
-
-        @pl.when(bi > 2)
-        def _():
-            reduce_near(3, 0)
-            reduce_plane(3, 1)
+            forward_dz(b + 1)
+            grad_point(b + 1)
+
+        @pl.when(bi == 2)
+        def _():
+            pair_point(3)
+            reduce_plane(3, 0)
+
+        @pl.when(bi == 3)
+        def _():
             reduce_plane(3, 2)
+            reduce_far(3, 0)
 
         total_first, total_second = sums_finish(e)
         for i in range(0, R, 64):
@@ -974,16 +1069,11 @@
             inner = zbuf[i : i + 64] - valid[i : i + 64] * (
                 (total_first + xhat * total_second) / row_count
             )
-            dzq[b, 1, u, i : i + 64] = (gi[b, 1:2] * inner).astype(jnp.bfloat16)
-        send_dz(b, 1)
-
-        @pl.when(bi == 3)
-        def _():
-            send_share(0, 1)
-
+            dzq[b, u, i : i + 64] = (gi[b, 1:2] * inner).astype(jnp.bfloat16)
+        send_dz(b)
         gsend[b, 2:3] = total_second
         gsend[b, 3:4] = total_first
-        d_two = dzq[b, 1, u]
+        d_two = dzq[b, u]
         for k in range(9):
             Hb[:, k * D : (k + 1) * D] = jnp.dot(
                 Gm[c, pl.ds((8 - k) * R, R)], d_two, preferred_element_type=jnp.float32
@@ -1005,21 +1095,28 @@
             second_sum += jnp.sum(du * sv[b, 0, i : i + 64].astype(jnp.float32), 0, keepdims=True)
         sums_start(e + 1, first_sum, second_sum)
 
+        @pl.when(bi == 2)
+        def _():
+            reduce_near(3, 0)
+
+        @pl.when(bi == 3)
+        def _():
+            reduce_near(3, 2)
+
         @pl.when(bi > 0)
         def _():
             grad_spatial(b + 1)
-            forward_dz(b + 1, 0)
 
         @pl.when(bi == 2)
         def _():
-            reduce_plane(3, 0)
-
-        @pl.when(bi > 2)
-        def _():
-            reduce_near(3, 1)
-            reduce_near(3, 2)
+            reduce_plane(3, 1)
+
+        @pl.when(bi == 3)
+        def _():
+            reduce_plane(3, 3)
             reduce_plane(2, 0)
-            reduce_far(3, 0)
+            reduce_far(3, 1)
+            reduce_near(2, 0)
 
         total_first, total_second = sums_finish(e + 1)
         for i in range(0, R, 64):
@@ -1027,17 +1124,12 @@
             inner = zbuf[i : i + 64] - valid[i : i + 64] * (
                 (total_first + xhat * total_second) / row_count
             )
-            dzq[b, 0, u, i : i + 64] = (gi[b, 0:1] * inner).astype(jnp.bfloat16)
-        send_dz(b, 0)
-
-        @pl.when(bi == 2)
-        def _():
-            send_share(0, 0)
-
+            dz1q[b, c, i : i + 64] = (gi[b, 0:1] * inner).astype(jnp.bfloat16)
+        dz_one_copy(b).start()
         gsend[b, 0:1] = total_second
         gsend[b, 1:2] = total_first
         g[...] = g[...] + lax.dot_general(
-            dzq[b, 0, u], W[b, 9].reshape(D, D), NT, preferred_element_type=jnp.float32
+            dz1q[b, c], W[b, 9].reshape(D, D), NT, preferred_element_type=jnp.float32
         )
 
         @pl.when(b == s)
@@ -1055,56 +1147,70 @@
     out_grad_in = pltpu.make_async_copy(g, in_grad.at[0], sO_s.at[1])
     out_grad_in.start()
 
-    reduce_near(2, 0)
-    grad_point(1)
-    reduce_far(3, 1)
+    reduce_near(3, 3)
+    forward_dz(0)
+    pair_point(2)
+    reduce_plane(2, 1)
+    reduce_near(2, 1)
+    grad_spatial(0)
+    grad_point(0)
     reduce_far(3, 2)
-    reduce_plane(2, 1)
-    forward_dz(0, 1)
-    grad_spatial(0)
-    reduce_near(2, 1)
+    reduce_far(2, 0)
+    pair_point(1)
     reduce_plane(2, 2)
-    reduce_far(2, 0)
+    reduce_near(2, 2)
+    reduce_far(3, 3)
     finish(3, 0)
-    finish(3, 1)
-    reduce_near(2, 2)
-    forward_dz(0, 0)
     reduce_plane(1, 0)
-    grad_point(0)
     reduce_near(1, 0)
     reduce_far(2, 1)
+    reduce_plane(2, 3)
+    reduce_near(2, 3)
+    finish(3, 1)
+    finish(2, 0)
+    reduce_plane(1, 1)
+    reduce_near(1, 1)
+    reduce_far(2, 2)
     finish(3, 2)
-    finish(2, 0)
-    reduce_far(2, 2)
-    reduce_plane(1, 1)
     reduce_plane(1, 2)
-    reduce_near(1, 1)
     reduce_near(1, 2)
     reduce_far(1, 0)
+    finish(3, 3)
     finish(2, 1)
-    finish(2, 2)
+    pair_point(0)
     reduce_plane(0, 0)
     reduce_near(0, 0)
+    reduce_far(2, 3)
     reduce_far(1, 1)
+    reduce_plane(1, 3)
+    reduce_near(1, 3)
+    finish(2, 2)
+    finish(1, 0)
+    reduce_plane(0, 1)
+    reduce_near(0, 1)
     reduce_far(1, 2)
-    finish(1, 0)
+    reduce_plane(0, 2)
+    reduce_near(0, 2)
+    reduce_plane(0, 3)
+    reduce_near(0, 3)
+    reduce_far(0, 0)
+    finish(2, 3)
     finish(1, 1)
-    reduce_plane(0, 1)
-    reduce_plane(0, 2)
-    reduce_near(0, 1)
-    reduce_near(0, 2)
-    reduce_far(0, 0)
+    reduce_far(1, 3)
+    reduce_far(0, 1)
     finish(1, 2)
+    finish(1, 3)
     finish(0, 0)
-    reduce_far(0, 1)
     reduce_far(0, 2)
+    reduce_far(0, 3)
     finish(0, 1)
     close_rest()
     finish(0, 2)
+    finish(0, 3)
     for d in range(1, 4):
         drain(gfin.at[:, s ^ d], sG_r.at[s ^ d])
 
-    @pl.when(c == 1)
+    @pl.when((c == 1) & (s == 3))
     def _():
         drain(gfin.at[:, s], sG_r.at[s])
 
@@ -1133,13 +1239,13 @@
 
         @pl.when(c == 0)
         def _():
-            @pl.loop(0, 4)
-            def _(b):
-                drain(zrecv.at[b, 1, 0], sG_s.at[b, 1])
-
-                @pl.when(b != s)
-                def _():
-                    drain(zrecv.at[b, 0, 0], sG_s.at[b, 0])
+            drain(zrecv.at[4, 0], sG_s.at[3, 1])
+
+        @pl.loop(0, 4)
+        def _(b):
+            @pl.when((b != s) & ((b < 3) | (c == 0)))
+            def _():
+                drain(zrecv.at[b, 0], sG_s.at[b, 0])
 
     with jax.named_scope("close_outputs"):
         grads_out.wait()
@@ -1220,24 +1326,25 @@
         W=V((4, TAPS, 8, 4, 16, D), bf16), wown=V((TAPS, 4, 16, D), bf16),
         F=V((3 * R, D), f32),
         sv=V((4, 4, R, D), bf16), gi=V((4, 8, D), f32),
-        abuf=V((R, D), bf16), gbuf=V((R, D), bf16),
-        Gm=V((4, 9 * R, R), bf16), caq=V((4, 2, 4, 8, 16, R), bf16),
-        stage=V((4, 2, 4, 8, 16, R), bf16), Hb=V((R, 9 * D), bf16),
-        dzq=V((4, 2, 4, R, D), bf16),
+        abuf=V((R, D), bf16),
+        Gm=V((6, 9 * R, R), bf16), caq=V((4, 2, 4, 8, 16, R), bf16),
+        stage=V((4, 4, 8, 16, R), bf16), stage_a=V((4, 8, 16, R), bf16), Hb=V((R, 9 * D), bf16),
+        dzq=V((4, 4, R, D), bf16), dz1q=V((4, 2, R, D), bf16),
+        pgrad=V((4, 2, 2, 4, 16, D), bf16), precv=V((4, 2, 4, 16, D), bf16),
         gout=V((4, 2, TAPS, 4, 16, D), bf16), yrecv=V((4, TAPS, 4, 16, D), bf16),
-        zs1=V((4, TAPS, 4, 16, D), bf16), zrecv=V((4, 2, 3, TAPS, 16, D), bf16),
+        zs1=V((TAPS, 4, 16, D), bf16), zrecv=V((5, 3, TAPS, 16, D), bf16),
         gfin=V((TAPS, 4, 16, D), bf16),
         aff=V((4, 8, D), f32), gaff=V((4, 8, D), f32), gsend=V((4, 8, D), f32),
         st_in=V((17, 8, 128), f32), st_own=V((17, 8, 128), f32), st_all=V((17, 4, 8, 128), f32),
-        cnt=V((8, 8, 128), f32), cntx=V((4, 8, 128), f32), cown=V((8, 128), f32),
+        cnt=V((8, 8, 128), f32), cntx=V((6, 8, 128), f32), cown=V((8, 128), f32),
         sL=dma((12,)), sS_s=dma, sS_r=dma((4, 2)), sZ_s=dma((4,)), sZ_r=dma((4, 4)),
         sH_s=dma((4,)), sH_r=dma((4, 4)), sA_s=dma((4,)), sA_r=dma((4, 4)),
         sB_s=dma((4, 2)), sB_r=dma((4, 2)), sD_s=dma((4, 3)), sD_r=dma((4, 3)),
         sE_in_s=dma((17,)), sE_in_r=dma((17,)), sE_s=dma((17,)), sE_r=dma((17,)),
         sC_s=dma, sC_r=dma((2,)), sF_s=dma, sF_r=dma,
-        sQ_s=dma((4, 2)), sQ_r=dma((4, 2)), sX_s=dma((4, 2)), sX_r=dma((4, 2, 4)),
-        sY_s=dma((4, 3)), sY_r=dma((4, 3)), sK_s=dma((4, 3)), sK_r=dma((4, 3)),
-        sN_s=dma((4, 3)), sN_r=dma((4, 3)), sT_s=dma((4, 3)), sT_r=dma((4, 3)), sG_s=dma((4, 2)), sG_r=dma((4,)),
+        sQ_s=dma((4, 2)), sQ_r=dma((4, 2)), sX_s=dma((4,)), sX_r=dma((4, 4)), sM_s=dma((4,)), sM_r=dma((4,)), sP_s=dma((4,)), sP_r=dma((4,)),
+        sY_s=dma((4, 4)), sY_r=dma((4, 4)), sK_s=dma((4, 4)), sK_r=dma((4, 4)),
+        sN_s=dma((4, 4)), sN_r=dma((4, 4)), sT_s=dma((4, 4)), sT_r=dma((4, 4)), sG_s=dma((4, 2)), sG_r=dma((4,)),
         sO_s=dma((8,)), sO_r=dma,
     )
     shape = jax.ShapeDtypeStruct

time: 238 us -> 224 us (0.941)
  Pallas kernels: 237 us -> 223 us
    pallas_call x1, Pallas kernels: 233 us -> 218 us  [train_step(): pl.pallas_call(train_kernel, out_shape=(shape((1, R, D), f32), shape((1,...]
where the time goes in v3:
time: 224 us; the launch traced here: 223 us
  Pallas kernels  223 us (100%)
    pallas_call x1, Pallas kernels, train_step(): pl.pallas_call(train_kernel, out_shape=(shape((1, R, D), f32), shape((1,...  218 us

profile of v3, /device:TPU:0, one launch (start us, length us, event | category | flops | bytes accessed | tf_op | source)
XLA Modules:
  0.0 223.5 jit_solution(8923651567640155121)
XLA Ops:
  0.6 218.5 %shard_map.152 = (f32[1,256,512]{2,1,0:T(8,128)}, f32[1,256,512]{2,1,0:T(8,128)}, bf16[10,4,16,512]{3,2,1,0:T(8,128)(2,1)}, f32[8,512]{1,0:T(8,128)}, f32[8,512]{1,0:T(8,128)}) custom-call(bf16[4,256,512]{2,1,0:T(8,128)(2,1)} %images.1, s32[1,4]{1,0:T(1,128)} %bitcast.1, f32[1,64,512]{2,1,0:T(8,128)} %w_point.3, f32[1,9,64,512]{3,2,1,0:T(8,128)} %w_spatial.3, ...), custom_call_target="tpu_custom_call" | custom-call | tf_op jit(solution)/shard_map/pallas_call | solution.py:1351
  219.1 4.2 %shard_map.153 = (f32[1,256,512]{2,1,0:T(8,128)}, f32[1,256,512]{2,1,0:T(8,128)}, f32[1,64,512]{2,1,0:T(8,128)}, f32[1,9,64,512]{3,2,1,0:T(8,128)}, f32[1,4,512]...) custom-call(f32[1,256,512]{2,1,0:T(8,128)} %get-tuple-element.13.feat, ...), custom_call_target="tpu_custom_call" | custom-call | tf_op jit(solution)/shard_map/pallas_call | solution.py:1364

commit v4 on v3

--- a/solution.py
+++ b/solution.py
@@ -361,7 +361,8 @@
 
 NT = (((1,), (1,)), ((), ()))
 TAPS = 10
-HALF = 5
+WHOLE = 2
+HALF = (TAPS - WHOLE) // 2
 
 
 def train_kernel(
@@ -369,7 +370,7 @@
     features, in_grad, grads, totals_out, affine_out,
     W, wown, F, sv, gi, abuf, Gm, caq, stage, stage_a, Hb, dzq, dz1q, pgrad, precv, gout, yrecv,
     zs1, zrecv, gfin, aff, gaff, gsend, st_in, st_own, st_all, cnt, cntx, cown,
-    sL, sS_s, sS_r, sZ_s, sZ_r, sH_s, sH_r, sA_s, sA_r, sB_s, sB_r, sD_s, sD_r,
+    sL, sS_s, sS_r, sU_s, sU_r, sV_s, sV_r, sJ_s, sJ_r, sZ_s, sZ_r, sH_s, sH_r, sA_s, sA_r, sB_r, sD_r,
     sE_in_s, sE_in_r, sE_s, sE_r, sC_s, sC_r, sF_s, sF_r, sQ_s, sQ_r, sX_s, sX_r, sM_s, sM_r, sP_s, sP_r,
     sY_s, sY_r, sK_s, sK_r, sN_s, sN_r, sT_s, sT_r, sG_s, sG_r, sO_s, sO_r,
 ):
@@ -385,12 +386,12 @@
     zbuf = F.at[pl.ds(2 * R, R)]
 
     loads = [
-        pltpu.make_async_copy(w_point.at[0], F.at[pl.ds(9 * 64, 64)], sL.at[9]),
+        pltpu.make_async_copy(w_point.at[0], F.at[pl.ds(9 * 64, 64)], sL.at[0]),
         *[
-            pltpu.make_async_copy(w_spatial.at[0, k], F.at[pl.ds(k * 64, 64)], sL.at[k])
+            pltpu.make_async_copy(w_spatial.at[0, k], F.at[pl.ds(k * 64, 64)], sL.at[0])
             for k in range(9)
         ],
-        pltpu.make_async_copy(images.at[s], abuf, sL.at[10]),
+        pltpu.make_async_copy(images.at[s], abuf, sL.at[1]),
     ]
     for load in loads:
         load.start()
@@ -407,8 +408,7 @@
         return jnp.sum(rows * rows, 0, keepdims=True)
 
     spatial_squares = jnp.zeros((1, D), jnp.float32)
-    for load in loads[:10]:
-        load.wait()
+    drain(F.at[pl.ds(0, 64 * TAPS)], sL.at[0])
     for k in range(TAPS):
         rows = F[k * 64 : k * 64 + 64]
         wown[k] = rows.astype(jnp.bfloat16).reshape(4, 16, D)
@@ -418,23 +418,6 @@
             point_squares = square(rows)
     with jax.named_scope("greet"):
         pl.semaphore_wait(barrier, len(greet))
-
-    def scatter(d):
-        q = s ^ d
-        return swap_copy(
-            wown.at[:, q], W.at[s, :, bat, q], sS_s, sS_r.at[s, c], q, 2 * z
-        )
-
-    for d in range(1, 4):
-        scatter(d).start()
-
-    @pl.when(c == 1)
-    def _():
-        scatter(0).start()
-
-    @pl.when(c == 0)
-    def _():
-        pltpu.make_async_copy(wown.at[:, s], W.at[s, :, bat, s], sS_r.at[s, c]).start()
 
     cown[...] = jnp.full((8, 128), crop[0, s].astype(jnp.float32))
     aff[s] = jnp.concatenate([norm_in[0], jnp.zeros((4, D), jnp.float32)], axis=0)
@@ -448,6 +431,31 @@
     for d in range(1, 4):
         swap_copy(aff.at[s], aff.at[s], sF_s, sF_r, s ^ d, bat).start()
 
+    def scatter(d):
+        q = s ^ d
+        return swap_copy(
+            wown.at[split, q], W.at[s, split, bat, q], sS_s, sS_r.at[s], q, 2 * z
+        )
+
+    def scatter_whole(d):
+        return swap_copy(
+            wown.at[whole], W.at[s, whole, bat], sU_s, sU_r.at[s], s ^ d, 2 * z
+        )
+
+    split, whole = pl.ds(0, 2 * HALF), pl.ds(2 * HALF, WHOLE)
+    for send in (scatter, scatter_whole):
+        for d in range(1, 4):
+            send(d).start()
+
+        @pl.when(c == 1)
+        def _():
+            send(0).start()
+
+    @pl.when(c == 0)
+    def _():
+        pltpu.make_async_copy(wown.at[split, s], W.at[s, split, bat, s], sS_r.at[s]).start()
+        pltpu.make_async_copy(wown.at[whole], W.at[s, whole, bat], sU_r.at[s]).start()
+
     half = pl.ds(HALF * c, HALF)
     first = jnp.where(c == 0, s ^ 1, s ^ 2)
     second = jnp.where(c == 0, s ^ 2, s ^ 1)
@@ -457,20 +465,20 @@
         return W.at[b, taps, pl.ds(2 * zz, 2), q]
 
     def to_sibling(b, zz):
-        ref = pair(b, slice(None), zz, s)
-        return swap_copy(ref, ref, sH_s.at[b], sH_r.at[b, zz], s, bat ^ 1)
+        ref = pair(b, split, zz, s)
+        return swap_copy(ref, ref, sH_s, sH_r.at[b, zz], s, bat ^ 1)
 
     def along_first(b, zz):
         ref = pair(b, half, zz, s)
-        return swap_copy(ref, ref, sA_s.at[b], sA_r.at[b, zz], first, bat)
+        return swap_copy(ref, ref, sA_s, sA_r.at[b, zz], first, bat)
 
     def along_second(b, which, zz):
         ref = pair(b, half, zz, s if which == 0 else first)
-        return swap_copy(ref, ref, sB_s.at[b, which], sB_r.at[b, which], second, bat)
+        return swap_copy(ref, ref, sA_s, sB_r.at[b, which], second, bat)
 
     def quarter_to_sibling(b, which):
         ref = W.at[b, half, :, (first, second, both)[which]]
-        return swap_copy(ref, ref, sD_s.at[b, which], sD_r.at[b, which], s, bat ^ 1)
+        return swap_copy(ref, ref, sA_s, sD_r.at[b], s, bat ^ 1)
 
     def own_ready(b, zz):
         @pl.when(c == 0)
@@ -484,45 +492,85 @@
         along_first(b, zz).start()
         along_second(b, 0, zz).start()
 
-    def spread_z(b, j):
-        ref = pair(b, slice(None), z, s)
-        return swap_copy(ref, ref, sZ_s.at[b], sZ_r.at[b, z], s, bat ^ (2 * j))
-
-    def from_z(b, zz):
-        ref = pair(b, slice(None), zz, s)
-        return swap_copy(ref, ref, sZ_s.at[b], sZ_r.at[b, zz], s, bat)
-
-    @pl.loop(0, 4)
+    def along_z(b, zz, j):
+        ref = pair(b, split, zz, s)
+        return swap_copy(ref, ref, sZ_s, sZ_r.at[b, zz], s, bat ^ (2 * j))
+
+    def whole_along_z(b, zz, j):
+        ref = W.at[b, whole, pl.ds(2 * zz, 2)]
+        return swap_copy(ref, ref, sV_s, sV_r.at[b, j - 1], s, bat ^ (2 * j))
+
+    def whole_to_sibling(b, zz):
+        ref = W.at[b, whole, pl.ds(2 * zz, 2)]
+        return swap_copy(ref, ref, sJ_s, sJ_r.at[b], s, bat ^ 1)
+
+    def on_first_core(work):
+        pl.when(c == 0)(work)
+
     @jax.named_scope("own_quarter")
-    def _(b):
-        @pl.when(c == 0)
-        def _():
-            for cc in range(2):
-                drain(W.at[b, :, 2 * z + cc, s], sS_r.at[b, cc])
-            for j in range(1, 4):
-                spread_z(b, j).start()
-
-        @pl.when(b < 3)
-        def _():
-            own_ready(b, z)
-
-    @jax.named_scope("gather_z")
-    def gather_z(b):
-        for j in range(1, 4):
-            zz = z ^ j
-
-            @pl.when(c == 0)
+    def own_quarter(b):
+        @on_first_core
+        def _():
+            drain(pair(b, split, z, s), sS_r.at[b])
+
+        own_ready(b, z)
+
+    @jax.named_scope("start_z")
+    def start_z(b):
+        @on_first_core
+        def _():
+            along_z(b, z, 2).start()
+            along_z(b, z, 1).start()
+
+    @jax.named_scope("start_whole")
+    def start_whole(b):
+        @on_first_core
+        def _():
+            drain(W.at[b, whole, pl.ds(2 * z, 2)], sU_r.at[b])
+            whole_along_z(b, z, 2).start()
+            whole_along_z(b, z, 1).start()
+            whole_to_sibling(b, z).start()
+
+    @jax.named_scope("relay_z")
+    def relay_z(b):
+        @on_first_core
+        def _():
+            drain(pair(b, split, z ^ 2, s), sZ_r.at[b, z ^ 2])
+            along_z(b, z ^ 2, 1).start()
+
+        own_ready(b, z ^ 2)
+
+    @jax.named_scope("rest_z")
+    def rest_z(b):
+        for j in (1, 3):
+            @on_first_core
             def _():
-                from_z(b, zz).wait_recv()
-
-            own_ready(b, zz)
+                drain(pair(b, split, z ^ j, s), sZ_r.at[b, z ^ j])
+
+            own_ready(b, z ^ j)
+
+    @jax.named_scope("relay_whole")
+    def relay_whole(b):
+        @on_first_core
+        def _():
+            drain(W.at[b, whole, pl.ds(2 * (z ^ 2), 2)], sV_r.at[b, 1])
+            whole_along_z(b, z ^ 2, 1).start()
+            whole_to_sibling(b, z ^ 2).start()
+
+    @jax.named_scope("rest_whole")
+    def rest_whole(b):
+        @on_first_core
+        def _():
+            drain(W.at[b, whole, pl.ds(0, 4)], sV_r.at[b, 0])
+            for j in (1, 3):
+                whole_to_sibling(b, z ^ j).start()
 
     @jax.named_scope("gather_first")
     def gather_first(b):
         for j in range(4):
             zz = z ^ j
             ref = pair(b, half, zz, first)
-            swap_copy(ref, ref, sA_s.at[b], sA_r.at[b, zz], first, bat).wait_recv()
+            swap_copy(ref, ref, sA_s, sA_r.at[b, zz], first, bat).wait_recv()
             along_second(b, 1, zz).start()
         quarter_to_sibling(b, 0).start()
 
@@ -535,8 +583,19 @@
     @jax.named_scope("gather_last")
     def gather_last(b):
         other = pl.ds(HALF * (1 - c), HALF)
-        for which in range(3):
-            drain(W.at[b, other, :, (second, first, both)[which]], sD_r.at[b, which])
+        drain(W.at[b, other, :, pl.ds(0, 3)], sD_r.at[b])
+
+        @pl.when(c == 1)
+        def _():
+            drain(W.at[b, whole], sJ_r.at[b])
+
+    for b in range(3):
+        own_quarter(b)
+        if b == 0:
+            start_z(0)
+    relay_z(0)
+    start_whole(0)
+    start_z(1)
 
     drain(cnt.at[pl.ds(0, 7)], sC_r.at[0])
     drain(cntx.at[pl.ds(2, 4)], sC_r.at[1])
@@ -572,43 +631,51 @@
 
     @jax.named_scope("sums_start")
     def sums_start(e, first_sum, second_sum):
+        slot = lax.rem(e, 2)
         st_own[e] = pack(first_sum, second_sum)
+        to_core = swap_copy(st_own.at[e], st_in.at[e], sE_in_s.at[slot], sE_in_r.at[slot], s, bat ^ 1)
+
+        @pl.when(e > 1)
+        def _():
+            sums_close(e)
 
         @pl.when(c == 0)
         def _():
-            swap_copy(st_own.at[e], st_in.at[e], sE_in_s.at[e], sE_in_r.at[e], s, bat ^ 1).start()
+            to_core.start()
 
         @pl.when(c == 1)
         def _():
-            swap_copy(
-                st_own.at[e], st_in.at[e], sE_in_s.at[e], sE_in_r.at[e], s, bat ^ 1
-            ).wait_recv()
+            to_core.wait_recv()
             st_all[e, z] = st_own[e] + st_in[e]
             for j in (7, 6, 5, 4, 3, 2, 1):
                 swap_copy(
-                    st_all.at[e, z], st_all.at[e, z], sE_s.at[e], sE_r.at[e], s, bat ^ j
+                    st_all.at[e, z], st_all.at[e, z], sE_s.at[slot], sE_r.at[slot], s, bat ^ j
                 ).start()
 
     @jax.named_scope("sums_finish")
     def sums_finish(e):
+        slot = lax.rem(e, 2)
+
         @pl.when(c == 0)
         def _():
-            drain(st_all.at[e], sE_r.at[e])
+            drain(st_all.at[e], sE_r.at[slot])
 
         @pl.when(c == 1)
         def _():
-            drain(st_all.at[e, pl.ds(0, 3)], sE_r.at[e])
+            drain(st_all.at[e, pl.ds(0, 3)], sE_r.at[slot])
 
         return unpack(st_all[e, 0] + st_all[e, 1] + st_all[e, 2] + st_all[e, 3])
 
     def sums_close(e):
+        slot = lax.rem(e, 2)
+
         @pl.when(c == 0)
         def _():
-            drain(st_own.at[e], sE_in_s.at[e])
+            drain(st_own.at[0], sE_in_s.at[slot])
 
         @pl.when(c == 1)
         def _():
-            drain(cnt.at[pl.ds(0, 7)], sE_s.at[e])
+            drain(cnt.at[pl.ds(0, 7)], sE_s.at[slot])
 
     def moments(sums):
         center = sums[0] / row_count
@@ -626,7 +693,7 @@
         if kind == 1:
             @pl.when(b > 0)
             def _():
-                drain(stage_a.at[pl.ds(0, 2)], sQ_s.at[b - 1, 1])
+                drain(stage_a.at[pl.ds(0, 2)], sQ_s.at[1])
 
         odd = lax.rem(b, 2) == 1
         for cc in range(2):
@@ -643,7 +710,7 @@
                 v = 2 * half_of_pair
                 caq[b, 1, v + c] = stage_a[v + c]
                 swap_copy(
-                    stage_a.at[v + 1 - c], caq.at[b, 1, v + c], sQ_s.at[b, 1], sQ_r.at[b, 1], s, bat ^ 1
+                    stage_a.at[v + 1 - c], caq.at[b, 1, v + c], sQ_s.at[1], sQ_r.at[b, 1], s, bat ^ 1
                 ).start()
         else:
             u = 2 * pairing(b)[0] + c
@@ -658,7 +725,7 @@
         u = 2 * mine + c
         for j in range(1, 4):
             swap_copy(
-                stage.at[b, u ^ j], caq.at[b, 0, u], sQ_s.at[b, 0], sQ_r.at[b, 0],
+                stage.at[b, u ^ j], caq.at[b, 0, u], sQ_s.at[0], sQ_r.at[b, 0],
                 s ^ near if j > 1 else s, bat ^ (j % 2),
             ).start()
 
@@ -685,10 +752,22 @@
         )
         share(b, 1, hidden)
 
-        @pl.when(b < 2)
-        def _():
-            gather_first(b + 1)
-
+        @pl.when(b == 0)
+        def _():
+            gather_first(1)
+            relay_whole(1)
+            own_quarter(3)
+            start_z(3)
+
+        @pl.when(b == 1)
+        def _():
+            relay_z(3)
+            gather_first(2)
+
+        @pl.when(b == 2)
+        def _():
+            gather_first(3)
+            relay_whole(3)
 
         norms = aff[b]
         center, spread = moments(sums_finish(2 * b))
@@ -716,16 +795,18 @@
 
         @pl.when(b == 0)
         def _():
-            gather_z(2)
+            rest_z(2)
+            start_whole(2)
 
         @pl.when(b == 1)
         def _():
-            own_ready(3, z)
-            gather_z(3)
+            relay_whole(2)
+            rest_z(3)
+            start_whole(3)
 
         @pl.when(b == 2)
         def _():
-            gather_first(3)
+            rest_whole(3)
 
         center, spread = moments(sums_finish(2 * b + 1))
         gi[b, 1:2] = norms[2:3] * spread
@@ -736,20 +817,30 @@
             sv[b, 3, i : i + 64] = slope.astype(sv.dtype)
             h[i : i + 64] = h[i : i + 64] + valid[i : i + 64] * value
 
-    gather_z(0)
+    rest_z(0)
+    relay_whole(0)
+    start_z(2)
     gather_first(0)
-    gather_z(1)
+    relay_z(1)
+    start_whole(1)
+    rest_whole(0)
     gather_second(0)
+    relay_z(2)
+    rest_z(1)
 
     @pl.loop(0, 4)
     def _(b):
         forward(b)
 
+        @pl.when(b < 2)
+        def _():
+            rest_whole(b + 1)
+
         @pl.when(b < 3)
         def _():
             gather_second(b + 1)
 
-    out_grad_rows = pltpu.make_async_copy(out_grad.at[s], abuf, sL.at[11])
+    out_grad_rows = pltpu.make_async_copy(out_grad.at[s], abuf, sL.at[2])
     out_features = pltpu.make_async_copy(h, features.at[0], sO_s.at[0])
     out_features.start()
     out_grad_rows.start()
@@ -760,61 +851,46 @@
     def close_gather():
         drain(aff.at[pl.ds(0, 3)], sF_s)
         drain(st_own.at[pl.ds(0, 11)], sC_s)
-        drain(stage_a.at[pl.ds(0, 2)], sQ_s.at[3, 1])
+        drain(stage_a.at[pl.ds(0, 2)], sQ_s.at[1])
 
         @pl.when(c == 0)
         def _():
-            drain(wown.at[:, pl.ds(0, 3)], sS_s)
+            drain(wown.at[split, pl.ds(0, 3)], sS_s)
+            drain(W.at[0, whole, pl.ds(0, 3)], sU_s)
 
         @pl.when(c == 1)
         def _():
-            drain(wown, sS_s)
-
-        @pl.loop(0, 4)
-        def _(b):
-            drain(W.at[b, half, :, s], sA_s.at[b])
-            for which in range(2):
-                drain(W.at[b, half, :, s], sB_s.at[b, which])
-            for which in range(3):
-                drain(W.at[b, half, :, s], sD_s.at[b, which])
-
-            @pl.when(c == 0)
-            def _():
-                drain(W.at[b, :, pl.ds(0, 6), s], sZ_s.at[b])
-                drain(W.at[b, :, :, s], sH_s.at[b])
+            drain(wown.at[split], sS_s)
+            drain(W.at[0, whole, pl.ds(0, 4)], sU_s)
+
+        drain(W.at[:, split, :, pl.ds(0, 3)], sA_s)
+
+        @on_first_core
+        def _():
+            drain(W.at[:, split, pl.ds(0, 6), s], sZ_s)
+            drain(W.at[:, split, :, s], sH_s)
+            drain(W.at[:, whole, pl.ds(0, 6)], sV_s)
+            drain(W.at[:, whole], sJ_s)
 
     @jax.named_scope("close_rest")
     def close_rest():
-        @pl.loop(0, 4)
-        def _(b):
-            drain(stage.at[b, pl.ds(0, 3)], sQ_s.at[b, 0])
-            drain(dzq.at[b, pl.ds(0, 3)], sX_s.at[b])
-            dz_one_copy(b).wait_send()
-            point_copy(b).wait_send()
-
-            @pl.when(b != s)
-            def _():
-                drain(gsend.at[b], sO_s.at[4 + b])
-
-            for i in range(len(CHUNKS)):
-                y_copy(b, i).wait_send()
+        drain(stage.at[:, pl.ds(0, 3)], sQ_s.at[0])
+        drain(dzq.at[:, pl.ds(0, 3)], sX_s)
+        drain(dz1q.at[:, 0], sM_s)
+        drain(precv, sP_s)
+        drain(gsend.at[pl.ds(0, 3)], sO_s.at[3])
+        drain(gout.at[:, 0], sY_s)
+
+        @pl.when(c == 0)
+        def _():
+            drain(zrecv.at[:, pl.ds(0, 2)], sN_s)
+            drain(zrecv.at[:, 2], sT_s)
 
         @pl.when(c == 1)
         def _():
-            for i, (at, size) in enumerate(CHUNKS):
-                drain(zs1.at[pl.ds(at, size)], sK_s.at[3, i])
-
-        def close_z(b, parts):
-            for i in range(len(CHUNKS)):
-                drain(near_like(b, i, parts), sN_s.at[b, i])
-                drain(far_like(b, i, parts), sT_s.at[b, i])
-
-        for b in range(4):
-            carriers(b, functools.partial(close_z, b))
-
-        @pl.loop(0, 16)
-        def _(e):
-            sums_close(e)
+            drain(zs1, sK_s)
+            drain(zrecv.at[pl.ds(0, 3), pl.ds(0, 2)], sN_s)
+            drain(zrecv.at[pl.ds(0, 3), 2], sT_s)
 
     CHUNKS = ((0, 3), (3, 3), (6, 3), (9, 1))
     LAST = len(CHUNKS) - 1
@@ -825,7 +901,7 @@
         v = v ^ 2 if j == 3 else v
         ref = dzq.at[b, v]
         return swap_copy(
-            ref, ref, sX_s.at[b], sX_r.at[b, v], s ^ near if j == 2 else s, bat if j == 2 else bat ^ 1
+            ref, ref, sX_s, sX_r.at[b, 0 if j == 2 else 1], s ^ near if j == 2 else s, bat if j == 2 else bat ^ 1
         )
 
     def send_dz(b):
@@ -835,30 +911,28 @@
     @jax.named_scope("forward_dz")
     def forward_dz(b):
         v = (2 * pairing(b)[0] + c) ^ 2
-        drain(dzq.at[b, v], sX_r.at[b, v])
+        drain(dzq.at[b, v], sX_r.at[b, 0])
         dz_copy(b, 3).start()
 
     @jax.named_scope("wait_dz")
     def wait_dz(b):
-        u = 2 * pairing(b)[0] + c
-        for v in (u ^ 1, u ^ 3):
-            drain(dzq.at[b, v], sX_r.at[b, v])
+        drain(dzq.at[b, pl.ds(0, 2)], sX_r.at[b, 1])
 
     def dz_one_copy(b):
         ref = dz1q.at[b, c]
-        return swap_copy(ref, ref, sM_s.at[b], sM_r.at[b], s, bat ^ 1)
+        return swap_copy(ref, ref, sM_s, sM_r.at[b], s, bat ^ 1)
 
     def point_copy(b):
         mine, _, near = pairing(b)
         return swap_copy(
-            pgrad.at[b, 1 - mine], precv.at[b], sP_s.at[b], sP_r.at[b], s ^ near, bat
+            pgrad.at[b, 1 - mine], precv.at[b], sP_s, sP_r.at[b], s ^ near, bat
         )
 
     def y_copy(b, i):
         at, size = CHUNKS[i]
         return swap_copy(
             gout.at[b, 1 - pairing(b)[1], pl.ds(at, size)], yrecv.at[b, pl.ds(at, size)],
-            sY_s.at[b, i], sY_r.at[b, i], s ^ 3 ^ pairing(b)[2], bat,
+            sY_s, sY_r.at[b, i], s ^ 3 ^ pairing(b)[2], bat,
         )
 
     def grad_tap(b, k, left, right):
@@ -916,7 +990,7 @@
         at, size = CHUNKS[i]
         return swap_copy(
             yrecv.at[b, pl.ds(at, size)], zs1.at[pl.ds(at, size)],
-            sK_s.at[b, i], sK_r.at[b, i], s, bat ^ 1,
+            sK_s, sK_r.at[i], s, bat ^ 1,
         )
 
     @jax.named_scope("reduce_plane")
@@ -945,14 +1019,14 @@
         at, size = CHUNKS[i]
         return swap_copy(
             (yrecv.at[b], zs1)[cc].at[pl.ds(at, size), z ^ (3 if slot else 1)],
-            zrecv.at[b + cc, slot, pl.ds(at, size)], sN_s.at[b, i], sN_r.at[b, i], s, bat ^ 2,
+            zrecv.at[b + cc, slot, pl.ds(at, size)], sN_s, sN_r.at[b, i], s, bat ^ 2,
         )
 
     def z_far(b, i, cc):
         at, size = CHUNKS[i]
         return swap_copy(
             zrecv.at[b + cc, 1, pl.ds(at, size)], zrecv.at[b + cc, 2, pl.ds(at, size)],
-            sT_s.at[b, i], sT_r.at[b, i], s, bat ^ 4,
+            sT_s, sT_r.at[b, i], s, bat ^ 4,
         )
 
     def near_like(b, i, parts):
@@ -994,7 +1068,7 @@
         at, size = CHUNKS[i]
         swap_copy(
             zrecv.at[b + cc, 0, pl.ds(at, size)], gfin.at[pl.ds(at, size), s],
-            sG_s.at[b, cc], sG_r.at[s], section, 2 * z + core,
+            sG_s, sG_r.at[s], section, 2 * z + core,
         ).start()
 
     @jax.named_scope("finish")
@@ -1056,7 +1130,6 @@
         @pl.when(bi == 2)
         def _():
             pair_point(3)
-            reduce_plane(3, 0)
 
         @pl.when(bi == 3)
         def _():
@@ -1097,26 +1170,29 @@
 
         @pl.when(bi == 2)
         def _():
+            reduce_plane(3, 0)
+
+        @pl.when(bi == 3)
+        def _():
+            reduce_near(3, 2)
+            reduce_plane(2, 0)
+            reduce_near(2, 0)
+
+        @pl.when(bi > 0)
+        def _():
+            grad_spatial(b + 1)
+
+        @pl.when(bi == 2)
+        def _():
             reduce_near(3, 0)
+            reduce_plane(3, 1)
 
         @pl.when(bi == 3)
         def _():
-            reduce_near(3, 2)
-
-        @pl.when(bi > 0)
-        def _():
-            grad_spatial(b + 1)
-
-        @pl.when(bi == 2)
-        def _():
-            reduce_plane(3, 1)
-
-        @pl.when(bi == 3)
-        def _():
             reduce_plane(3, 3)
-            reduce_plane(2, 0)
             reduce_far(3, 1)
-            reduce_near(2, 0)
+            reduce_plane(2, 1)
+            reduce_near(2, 1)
 
         total_first, total_second = sums_finish(e + 1)
         for i in range(0, R, 64):
@@ -1138,7 +1214,7 @@
 
         @pl.when(b != s)
         def _():
-            swap_copy(gsend.at[b], gaff.at[s], sO_s.at[4 + b], sO_r, b, bat).start()
+            swap_copy(gsend.at[b], gaff.at[s], sO_s.at[3], sO_r, b, bat).start()
 
     @pl.loop(0, 4)
     def _(bi):
@@ -1150,45 +1226,43 @@
     reduce_near(3, 3)
     forward_dz(0)
     pair_point(2)
-    reduce_plane(2, 1)
-    reduce_near(2, 1)
+    reduce_far(2, 0)
+    reduce_far(3, 2)
+    reduce_plane(2, 2)
+    reduce_near(2, 2)
     grad_spatial(0)
     grad_point(0)
-    reduce_far(3, 2)
-    reduce_far(2, 0)
     pair_point(1)
-    reduce_plane(2, 2)
-    reduce_near(2, 2)
-    reduce_far(3, 3)
+    reduce_far(2, 1)
     finish(3, 0)
+    reduce_plane(2, 3)
+    reduce_near(2, 3)
     reduce_plane(1, 0)
     reduce_near(1, 0)
-    reduce_far(2, 1)
-    reduce_plane(2, 3)
-    reduce_near(2, 3)
+    reduce_far(3, 3)
     finish(3, 1)
+    reduce_far(2, 2)
     finish(2, 0)
     reduce_plane(1, 1)
     reduce_near(1, 1)
-    reduce_far(2, 2)
     finish(3, 2)
+    reduce_far(1, 0)
     reduce_plane(1, 2)
     reduce_near(1, 2)
-    reduce_far(1, 0)
     finish(3, 3)
     finish(2, 1)
     pair_point(0)
+    reduce_far(2, 3)
     reduce_plane(0, 0)
     reduce_near(0, 0)
-    reduce_far(2, 3)
     reduce_far(1, 1)
     reduce_plane(1, 3)
     reduce_near(1, 3)
     finish(2, 2)
     finish(1, 0)
+    reduce_far(1, 2)
     reduce_plane(0, 1)
     reduce_near(0, 1)
-    reduce_far(1, 2)
     reduce_plane(0, 2)
     reduce_near(0, 2)
     reduce_plane(0, 3)
@@ -1228,24 +1302,27 @@
     tile = jnp.zeros((1, D), jnp.float32)
     for i, part in enumerate((point_squares, spatial_squares, gpoint_squares, gspatial_squares)):
         tile = jnp.where(lanes == i, lane_sum(part), tile)
-    sums_start(16, tile, tile)
+    sums_start(jnp.int32(16), tile, tile)
     drain(gaff.at[pl.ds(0, 3)], sO_r)
     affine_out[...] = gaff[0] + gaff[1] + gaff[2] + gaff[3]
     totals, _ = sums_finish(16)
     totals_out[...] = jnp.concatenate([totals] * 8, axis=0)
 
     with jax.named_scope("close_last"):
-        sums_close(16)
+        sums_close(0)
+        sums_close(1)
 
         @pl.when(c == 0)
         def _():
-            drain(zrecv.at[4, 0], sG_s.at[3, 1])
-
-        @pl.loop(0, 4)
-        def _(b):
-            @pl.when((b != s) & ((b < 3) | (c == 0)))
-            def _():
-                drain(zrecv.at[b, 0], sG_s.at[b, 0])
+            drain(zrecv.at[pl.ds(0, 4), 0], sG_s)
+
+        @pl.when((c == 1) & (s == 3))
+        def _():
+            drain(zrecv.at[pl.ds(0, 3), 0], sG_s)
+
+        @pl.when((c == 1) & (s != 3))
+        def _():
+            drain(zrecv.at[pl.ds(0, 2), 0], sG_s)
 
     with jax.named_scope("close_outputs"):
         grads_out.wait()
@@ -1337,15 +1414,16 @@
         aff=V((4, 8, D), f32), gaff=V((4, 8, D), f32), gsend=V((4, 8, D), f32),
         st_in=V((17, 8, 128), f32), st_own=V((17, 8, 128), f32), st_all=V((17, 4, 8, 128), f32),
         cnt=V((8, 8, 128), f32), cntx=V((6, 8, 128), f32), cown=V((8, 128), f32),
-        sL=dma((12,)), sS_s=dma, sS_r=dma((4, 2)), sZ_s=dma((4,)), sZ_r=dma((4, 4)),
-        sH_s=dma((4,)), sH_r=dma((4, 4)), sA_s=dma((4,)), sA_r=dma((4, 4)),
-        sB_s=dma((4, 2)), sB_r=dma((4, 2)), sD_s=dma((4, 3)), sD_r=dma((4, 3)),
-        sE_in_s=dma((17,)), sE_in_r=dma((17,)), sE_s=dma((17,)), sE_r=dma((17,)),
+        sL=dma((3,)), sS_s=dma, sS_r=dma((4,)), sU_s=dma, sU_r=dma((4,)), sV_s=dma, sV_r=dma((4, 2)),
+        sJ_s=dma, sJ_r=dma((4,)), sZ_s=dma, sZ_r=dma((4, 4)),
+        sH_s=dma, sH_r=dma((4, 4)), sA_s=dma, sA_r=dma((4, 4)),
+        sB_r=dma((4, 2)), sD_r=dma((4,)),
+        sE_in_s=dma((2,)), sE_in_r=dma((2,)), sE_s=dma((2,)), sE_r=dma((2,)),
         sC_s=dma, sC_r=dma((2,)), sF_s=dma, sF_r=dma,
-        sQ_s=dma((4, 2)), sQ_r=dma((4, 2)), sX_s=dma((4,)), sX_r=dma((4, 4)), sM_s=dma((4,)), sM_r=dma((4,)), sP_s=dma((4,)), sP_r=dma((4,)),
-        sY_s=dma((4, 4)), sY_r=dma((4, 4)), sK_s=dma((4, 4)), sK_r=dma((4, 4)),
-        sN_s=dma((4, 4)), sN_r=dma((4, 4)), sT_s=dma((4, 4)), sT_r=dma((4, 4)), sG_s=dma((4, 2)), sG_r=dma((4,)),
-        sO_s=dma((8,)), sO_r=dma,
+        sQ_s=dma((2,)), sQ_r=dma((4, 2)), sX_s=dma, sX_r=dma((4, 2)), sM_s=dma, sM_r=dma((4,)), sP_s=dma, sP_r=dma((4,)),
+        sY_s=dma, sY_r=dma((4, 4)), sK_s=dma, sK_r=dma((4,)),
+        sN_s=dma, sN_r=dma((4, 4)), sT_s=dma, sT_r=dma((4, 4)), sG_s=dma, sG_r=dma((4,)),
+        sO_s=dma((4,)), sO_r=dma,
     )
     shape = jax.ShapeDtypeStruct
     feat, ing, grads, totals, affine_grad = pl.pallas_call(

time: 224 us -> 210 us (0.938)
  Pallas kernels: 223 us -> 209 us
    pallas_call x1, Pallas kernels: 218 us -> 205 us  [train_step(): pl.pallas_call(train_kernel, out_shape=(shape((1, R, D), f32), shape((1,...]
where the time goes in v4:
time: 210 us
  Pallas kernels  209 us (100%)
    pallas_call x1, Pallas kernels, train_step(): pl.pallas_call(train_kernel, out_shape=(shape((1, R, D), f32), shape((1,...  205 us
    pallas_call x1, Pallas kernels, train_step(): pl.pallas_call(lars_kernel, out_shape=(shape((1, R, D), f32), shape((1, R...  4.2 us

profile of v4, /device:TPU:0, one launch (start us, length us, event | category | flops | bytes accessed | tf_op | source)
XLA Modules:
  0.0 209.6 jit_solution(7213081398879703985)
XLA Ops:
  0.6 204.6 %shard_map.152 = (f32[1,256,512]{2,1,0:T(8,128)}, f32[1,256,512]{2,1,0:T(8,128)}, bf16[10,4,16,512]{3,2,1,0:T(8,128)(2,1)}, f32[8,512]{1,0:T(8,128)}, f32[8,512]{1,0:T(8,128)}) custom-call(bf16[4,256,512]{2,1,0:T(8,128)(2,1)} %images.1, s32[1,4]{1,0:T(1,128)} %bitcast.1, f32[1,64,512]{2,1,0:T(8,128)} %w_point.3, f32[1,9,64,512]{3,2,1,0:T(8,128)} %w_spatial.3, ...), custom_call_target="tpu_custom_call" | custom-call | tf_op jit(solution)/shard_map/pallas_call | solution.py:1429
  205.3 4.2 %shard_map.153 = (f32[1,256,512]{2,1,0:T(8,128)}, f32[1,256,512]{2,1,0:T(8,128)}, f32[1,64,512]{2,1,0:T(8,128)}, f32[1,9,64,512]{3,2,1,0:T(8,128)}, f32[1,4,512]...) custom-call(f32[1,256,512]{2,1,0:T(8,128)} %get-tuple-element.13.feat, ...), custom_call_target="tpu_custom_call" | custom-call | tf_op jit(solution)/shard_map/pallas_call | solution.py:1442

commit v5 on v4

--- a/solution.py
+++ b/solution.py
@@ -369,10 +369,10 @@
     images, crop, w_point, w_spatial, norm_in, out_grad,
     features, in_grad, grads, totals_out, affine_out,
     W, wown, F, sv, gi, abuf, Gm, caq, stage, stage_a, Hb, dzq, dz1q, pgrad, precv, gout, yrecv,
-    zs1, zrecv, gfin, aff, gaff, gsend, st_in, st_own, st_all, cnt, cntx, cown,
+    zs1, zrecv, gfin, sq_in, sq_own, sq_acc, psq, aff, gaff, gsend, st_in, st_own, st_all, cnt, cntx, cown,
     sL, sS_s, sS_r, sU_s, sU_r, sV_s, sV_r, sJ_s, sJ_r, sZ_s, sZ_r, sH_s, sH_r, sA_s, sA_r, sB_r, sD_r,
     sE_in_s, sE_in_r, sE_s, sE_r, sC_s, sC_r, sF_s, sF_r, sQ_s, sQ_r, sX_s, sX_r, sM_s, sM_r, sP_s, sP_r,
-    sY_s, sY_r, sK_s, sK_r, sN_s, sN_r, sT_s, sT_r, sG_s, sG_r, sO_s, sO_r,
+    sW_s, sW_r, sY_s, sY_r, sK_s, sK_r, sN_s, sN_r, sT_s, sT_r, sG_s, sG_r, sO_s, sO_r,
 ):
     s = lax.axis_index("section")
     bat = lax.axis_index("batch")
@@ -416,6 +416,7 @@
             spatial_squares += square(rows)
         else:
             point_squares = square(rows)
+    sq_in[...] = jnp.zeros_like(sq_in)
     with jax.named_scope("greet"):
         pl.semaphore_wait(barrier, len(greet))
 
@@ -456,6 +457,58 @@
         pltpu.make_async_copy(wown.at[split, s], W.at[s, split, bat, s], sS_r.at[s]).start()
         pltpu.make_async_copy(wown.at[whole], W.at[s, whole, bat], sU_r.at[s]).start()
 
+    @jax.named_scope("sums_start")
+    def sums_start(e, first_sum, second_sum):
+        slot = lax.rem(e, 2)
+        st_own[e] = pack(first_sum, second_sum)
+        to_core = swap_copy(st_own.at[e], st_in.at[e], sE_in_s.at[slot], sE_in_r.at[slot], s, bat ^ 1)
+
+        if not isinstance(e, int):
+
+            @pl.when(e > 1)
+            def _():
+                sums_close(e)
+
+        @pl.when(c == 0)
+        def _():
+            to_core.start()
+
+        @pl.when(c == 1)
+        def _():
+            to_core.wait_recv()
+            st_all[e, z] = st_own[e] + st_in[e]
+            for j in (7, 6, 5, 4, 3, 2, 1):
+                swap_copy(
+                    st_all.at[e, z], st_all.at[e, z], sE_s.at[slot], sE_r.at[slot], s, bat ^ j
+                ).start()
+
+    @jax.named_scope("sums_finish")
+    def sums_finish(e):
+        slot = lax.rem(e, 2)
+
+        @pl.when(c == 0)
+        def _():
+            drain(st_all.at[e], sE_r.at[slot])
+
+        @pl.when(c == 1)
+        def _():
+            drain(st_all.at[e, pl.ds(0, 3)], sE_r.at[slot])
+
+        return unpack(st_all[e, 0] + st_all[e, 1] + st_all[e, 2] + st_all[e, 3])
+
+    def sums_close(e):
+        slot = lax.rem(e, 2)
+
+        @pl.when(c == 0)
+        def _():
+            drain(st_own.at[0], sE_in_s.at[slot])
+
+        @pl.when(c == 1)
+        def _():
+            drain(cnt.at[pl.ds(0, 7)], sE_s.at[slot])
+
+    sums_start(0, point_squares, spatial_squares)
+
     half = pl.ds(HALF * c, HALF)
     first = jnp.where(c == 0, s ^ 1, s ^ 2)
     second = jnp.where(c == 0, s ^ 2, s ^ 1)
@@ -584,10 +637,6 @@
     def gather_last(b):
         other = pl.ds(HALF * (1 - c), HALF)
         drain(W.at[b, other, :, pl.ds(0, 3)], sD_r.at[b])
-
-        @pl.when(c == 1)
-        def _():
-            drain(W.at[b, whole], sJ_r.at[b])
 
     for b in range(3):
         own_quarter(b)
@@ -628,54 +677,6 @@
     drain(aff.at[pl.ds(0, 3)], sF_r)
     loads[10].wait()
     h[...] = abuf[...].astype(jnp.float32)
-
-    @jax.named_scope("sums_start")
-    def sums_start(e, first_sum, second_sum):
-        slot = lax.rem(e, 2)
-        st_own[e] = pack(first_sum, second_sum)
-        to_core = swap_copy(st_own.at[e], st_in.at[e], sE_in_s.at[slot], sE_in_r.at[slot], s, bat ^ 1)
-
-        @pl.when(e > 1)
-        def _():
-            sums_close(e)
-
-        @pl.when(c == 0)
-        def _():
-            to_core.start()
-
-        @pl.when(c == 1)
-        def _():
-            to_core.wait_recv()
-            st_all[e, z] = st_own[e] + st_in[e]
-            for j in (7, 6, 5, 4, 3, 2, 1):
-                swap_copy(
-                    st_all.at[e, z], st_all.at[e, z], sE_s.at[slot], sE_r.at[slot], s, bat ^ j
-                ).start()
-
-    @jax.named_scope("sums_finish")
-    def sums_finish(e):
-        slot = lax.rem(e, 2)
-
-        @pl.when(c == 0)
-        def _():
-            drain(st_all.at[e], sE_r.at[slot])
-
-        @pl.when(c == 1)
-        def _():
-            drain(st_all.at[e, pl.ds(0, 3)], sE_r.at[slot])
-
-        return unpack(st_all[e, 0] + st_all[e, 1] + st_all[e, 2] + st_all[e, 3])
-
-    def sums_close(e):
-        slot = lax.rem(e, 2)
-
-        @pl.when(c == 0)
-        def _():
-            drain(st_own.at[0], sE_in_s.at[slot])
-
-        @pl.when(c == 1)
-        def _():
-            drain(cnt.at[pl.ds(0, 7)], sE_s.at[slot])
 
     def moments(sums):
         center = sums[0] / row_count
@@ -734,7 +735,9 @@
 
     @jax.named_scope("forward")
     def forward(b):
-        gather_last(b)
+        @pl.when(c == 1)
+        def _():
+            drain(W.at[b, whole], sJ_r.at[b])
 
         @pl.when(b == 3)
         def _():
@@ -748,29 +751,30 @@
         z1 = zbuf[...]
         kept = valid * z1
         sums_start(
-            2 * b, jnp.sum(kept, 0, keepdims=True), jnp.sum(kept * z1, 0, keepdims=True)
+            2 * b + 1, jnp.sum(kept, 0, keepdims=True), jnp.sum(kept * z1, 0, keepdims=True)
         )
         share(b, 1, hidden)
 
         @pl.when(b == 0)
         def _():
-            gather_first(1)
-            relay_whole(1)
-            own_quarter(3)
-            start_z(3)
+            relay_z(2)
+            rest_z(1)
 
         @pl.when(b == 1)
         def _():
             relay_z(3)
             gather_first(2)
+            relay_whole(2)
+            start_whole(3)
 
         @pl.when(b == 2)
         def _():
             gather_first(3)
             relay_whole(3)
 
+        gather_second(b)
         norms = aff[b]
-        center, spread = moments(sums_finish(2 * b))
+        center, spread = moments(sums_finish(2 * b + 1))
         gi[b, 0:1] = norms[0:1] * spread
         for i in range(0, R, 64):
             xhat = (zbuf[i : i + 64] - center) * spread
@@ -779,6 +783,7 @@
             sv[b, 1, i : i + 64] = slope.astype(sv.dtype)
             abuf[i : i + 64] = value.astype(jnp.bfloat16)
         mixed = abuf[...]
+        gather_last(b)
         for k in range(9):
             Hb[:, k * D : (k + 1) * D] = jnp.dot(
                 Gm[c, pl.ds(k * R, R)], mixed, preferred_element_type=jnp.float32
@@ -789,26 +794,22 @@
         z2 = zbuf[...]
         kept = valid * z2
         sums_start(
-            2 * b + 1, jnp.sum(kept, 0, keepdims=True), jnp.sum(kept * z2, 0, keepdims=True)
+            2 * b + 2, jnp.sum(kept, 0, keepdims=True), jnp.sum(kept * z2, 0, keepdims=True)
         )
         share(b, 0, mixed.astype(jnp.float32))
 
         @pl.when(b == 0)
         def _():
-            rest_z(2)
-            start_whole(2)
+            relay_whole(1)
+            gather_first(1)
+            own_quarter(3)
+            start_z(3)
 
         @pl.when(b == 1)
         def _():
-            relay_whole(2)
             rest_z(3)
-            start_whole(3)
-
-        @pl.when(b == 2)
-        def _():
-            rest_whole(3)
-
-        center, spread = moments(sums_finish(2 * b + 1))
+
+        center, spread = moments(sums_finish(2 * b + 2))
         gi[b, 1:2] = norms[2:3] * spread
         for i in range(0, R, 64):
             xhat = (zbuf[i : i + 64] - center) * spread
@@ -824,21 +825,20 @@
     relay_z(1)
     start_whole(1)
     rest_whole(0)
-    gather_second(0)
-    relay_z(2)
-    rest_z(1)
+    psq[...] = jnp.concatenate(sums_finish(0), axis=0)
 
     @pl.loop(0, 4)
     def _(b):
         forward(b)
 
-        @pl.when(b < 2)
+        @pl.when(b == 0)
+        def _():
+            rest_z(2)
+            start_whole(2)
+
+        @pl.when(b < 3)
         def _():
             rest_whole(b + 1)
-
-        @pl.when(b < 3)
-        def _():
-            gather_second(b + 1)
 
     out_grad_rows = pltpu.make_async_copy(out_grad.at[s], abuf, sL.at[2])
     out_features = pltpu.make_async_copy(h, features.at[0], sO_s.at[0])
@@ -1071,20 +1071,42 @@
             sG_s, sG_r.at[s], section, 2 * z + core,
         ).start()
 
+    def send_squares(b):
+        def to(j):
+            return swap_copy(
+                sq_own.at[b], sq_in.at[s, bat], sW_s, sW_r, b, bat ^ j
+            )
+
+        sq_own[b] = pack(sq_acc[b, 1:2], sq_acc[b, 0:1])
+
+        @pl.when(b != s)
+        def _():
+            to(0).start()
+
+        @pl.when(b == s)
+        def _():
+            sq_in[s, bat] = sq_own[b]
+
+        for j in range(1, 8):
+            to(j).start()
+
     @jax.named_scope("finish")
     def finish(b, i):
         at, size = CHUNKS[i]
 
         def work(parts):
             drain(far_like(b, i, parts), sT_r.at[b, i])
+            squares = jnp.zeros((1, D), jnp.float32)
             for cc in parts:
                 mine = (yrecv.at[b], zs1)[cc]
                 for k in range(at, at + size):
-                    zrecv[b + cc, 0, k] = (
+                    done = (
                         zrecv[b + cc, 0, k].astype(jnp.float32)
                         + zrecv[b + cc, 2, k].astype(jnp.float32)
                         + mine[k, z].astype(jnp.float32)
                     ).astype(jnp.bfloat16)
+                    zrecv[b + cc, 0, k] = done
+                    squares += square(done.astype(jnp.float32))
 
                 @pl.when(b != s)
                 def _():
@@ -1098,12 +1120,17 @@
                     else:
                         deliver(b, i, 1, s, 1)
 
+            row = 1 if i == LAST else 0
+            sq_acc[b, row : row + 1] = squares + (0.0 if i in (0, LAST) else sq_acc[b, row : row + 1])
+            if i == LAST:
+                send_squares(b)
+
         carriers(b, work)
 
     @jax.named_scope("backward")
     def backward(bi):
         b = 3 - bi
-        e = 8 + 2 * bi
+        e = 9 + 2 * bi
         u = 2 * pairing(b)[0] + c
         first_sum = jnp.zeros((1, D), jnp.float32)
         second_sum = jnp.zeros((1, D), jnp.float32)
@@ -1171,10 +1198,12 @@
         @pl.when(bi == 2)
         def _():
             reduce_plane(3, 0)
+            reduce_near(3, 0)
 
         @pl.when(bi == 3)
         def _():
             reduce_near(3, 2)
+            reduce_far(3, 1)
             reduce_plane(2, 0)
             reduce_near(2, 0)
 
@@ -1184,13 +1213,11 @@
 
         @pl.when(bi == 2)
         def _():
-            reduce_near(3, 0)
             reduce_plane(3, 1)
 
         @pl.when(bi == 3)
         def _():
             reduce_plane(3, 3)
-            reduce_far(3, 1)
             reduce_plane(2, 1)
             reduce_near(2, 1)
 
@@ -1231,15 +1258,15 @@
     reduce_plane(2, 2)
     reduce_near(2, 2)
     grad_spatial(0)
+    reduce_far(2, 1)
     grad_point(0)
+    reduce_far(3, 3)
     pair_point(1)
-    reduce_far(2, 1)
     finish(3, 0)
     reduce_plane(2, 3)
     reduce_near(2, 3)
     reduce_plane(1, 0)
     reduce_near(1, 0)
-    reduce_far(3, 3)
     finish(3, 1)
     reduce_far(2, 2)
     finish(2, 0)
@@ -1291,22 +1318,26 @@
     grads_out = pltpu.make_async_copy(gfin, grads, sO_s.at[2])
     grads_out.start()
 
-    def lane_sum(v):
-        return jnp.sum(v, axis=1, keepdims=True)
-
-    gspatial_squares = jnp.zeros((1, D), jnp.float32)
-    for k in range(9):
-        gspatial_squares += square(gfin[k].astype(jnp.float32).reshape(64, D))
-    gpoint_squares = square(gfin[9].astype(jnp.float32).reshape(64, D))
-    lanes = lax.broadcasted_iota(jnp.int32, (1, D), 1)
-    tile = jnp.zeros((1, D), jnp.float32)
-    for i, part in enumerate((point_squares, spatial_squares, gpoint_squares, gspatial_squares)):
-        tile = jnp.where(lanes == i, lane_sum(part), tile)
-    sums_start(jnp.int32(16), tile, tile)
     drain(gaff.at[pl.ds(0, 3)], sO_r)
     affine_out[...] = gaff[0] + gaff[1] + gaff[2] + gaff[3]
-    totals, _ = sums_finish(16)
-    totals_out[...] = jnp.concatenate([totals] * 8, axis=0)
+    squares_in = sq_in.reshape(32, 8, 128)
+
+    @pl.when(s != 3)
+    def _():
+        drain(squares_in.at[pl.ds(0, 31)], sW_r)
+
+    @pl.when((s == 3) & (c == 0))
+    def _():
+        drain(squares_in.at[pl.ds(0, 15)], sW_r)
+
+    @pl.when((s == 3) & (c == 1))
+    def _():
+        drain(squares_in.at[pl.ds(0, 16)], sW_r)
+
+    gpoint_squares, gspatial_squares = unpack(jnp.sum(squares_in[...], axis=0))
+    totals_out[...] = jnp.concatenate(
+        [psq[...], gpoint_squares, gspatial_squares, jnp.zeros((4, D), jnp.float32)], axis=0
+    )
 
     with jax.named_scope("close_last"):
         sums_close(0)
@@ -1316,13 +1347,19 @@
         def _():
             drain(zrecv.at[pl.ds(0, 4), 0], sG_s)
 
+        @pl.when(c == 0)
+        def _():
+            drain(squares_in.at[pl.ds(0, 31)], sW_s)
+
         @pl.when((c == 1) & (s == 3))
         def _():
             drain(zrecv.at[pl.ds(0, 3), 0], sG_s)
+            drain(squares_in.at[pl.ds(0, 24)], sW_s)
 
         @pl.when((c == 1) & (s != 3))
         def _():
             drain(zrecv.at[pl.ds(0, 2), 0], sG_s)
+            drain(squares_in.at[pl.ds(0, 23)], sW_s)
 
     with jax.named_scope("close_outputs"):
         grads_out.wait()
@@ -1335,25 +1372,31 @@
     features, in_grad, new_point, new_spatial, new_norm, new_mom_point, new_mom_spatial, new_mom_norm,
     P, M, G, feat_rows, grad_rows, totals, affine_grad, affine, affine_mom, sem, out_sem,
 ):
+    THIRDS = 3
+    small = [
+        (totals_in, totals), (affine_in, affine_grad), (norm_in.at[0], affine), (mom_norm.at[0], affine_mom),
+        (w_point.at[0], P.at[9]), (mom_point.at[0], M.at[9]), (grads_in.at[9], G.at[9]),
+    ]
+    large = []
+    for i in range(THIRDS):
+        taps = pl.ds(3 * i, 3)
+        large += [
+            (grads_in.at[taps], G.at[taps]), (w_spatial.at[0, taps], P.at[taps]),
+            (mom_spatial.at[0, taps], M.at[taps]),
+        ]
+    rows = [(feat, feat_rows), (ing, grad_rows)]
     loads = [
-        (totals_in, totals), (affine_in, affine_grad), (norm_in.at[0], affine), (mom_norm.at[0], affine_mom),
-        (grads_in, G), (w_spatial.at[0], P.at[pl.ds(0, 9)]), (mom_spatial.at[0], M.at[pl.ds(0, 9)]),
-        (w_point.at[0], P.at[9]), (mom_point.at[0], M.at[9]),
+        pltpu.make_async_copy(a, b, sem.at[i]) for i, (a, b) in enumerate(small + large + rows)
     ]
-    loads = [pltpu.make_async_copy(a, b, sem.at[i]) for i, (a, b) in enumerate(loads)]
     for load in loads:
         load.start()
-    passed = [
-        pltpu.make_async_copy(feat, feat_rows, sem.at[9]),
-        pltpu.make_async_copy(ing, grad_rows, sem.at[10]),
-    ]
-    for copy in passed:
-        copy.start()
-    for load in loads:
+    for load in loads[: len(small)]:
         load.wait()
     D = affine.shape[1]
     rate = BASE_RATE * (STEP + 1) / WARMUP
-    point_sq, spatial_sq, gpoint_sq, gspatial_sq = [totals[0:1, i : i + 1] for i in range(4)]
+    point_sq, spatial_sq, gpoint_sq, gspatial_sq = [
+        jnp.sum(totals[i : i + 1], axis=1, keepdims=True) for i in range(4)
+    ]
     step_point = rate * TRUST_COEF * jnp.sqrt(point_sq) / (jnp.sqrt(gpoint_sq) + EPS_NORM)
     step_spatial = rate * TRUST_COEF * jnp.sqrt(spatial_sq) / (jnp.sqrt(gspatial_sq) + EPS_NORM)
     outs = []
@@ -1362,20 +1405,25 @@
         outs.append(pltpu.make_async_copy(source, target, out_sem.at[len(outs)]))
         outs[-1].start()
 
-    for k in range(10):
-        grad = G[k].astype(jnp.float32).reshape(64, D)
-        moved = MOMENTUM * M[k] + (step_point if k == 9 else step_spatial) * grad
+    def move(k, step):
+        moved = MOMENTUM * M[k] + step * G[k].astype(jnp.float32).reshape(64, D)
         M[k] = moved
         P[k] = P[k] - moved
-        if k in (2, 5, 8):
-            taps = pl.ds(k - 2, 3)
-            store(M.at[taps], new_mom_spatial.at[0, taps])
-            store(P.at[taps], new_spatial.at[0, taps])
-    for copy, rows, target in zip(passed, (feat_rows, grad_rows), (features, in_grad)):
-        copy.wait()
-        store(rows, target)
+
+    for i in range(THIRDS):
+        for load in loads[len(small) + 3 * i :][:3]:
+            load.wait()
+        for k in range(3 * i, 3 * i + 3):
+            move(k, step_spatial)
+        taps = pl.ds(3 * i, 3)
+        store(M.at[taps], new_mom_spatial.at[0, taps])
+        store(P.at[taps], new_spatial.at[0, taps])
+    move(9, step_point)
     store(M.at[9], new_mom_point.at[0])
     store(P.at[9], new_point.at[0])
+    for load, source, target in zip(loads[-2:], (feat_rows, grad_rows), (features, in_grad)):
+        load.wait()
+        store(source, target)
     grad = affine_grad[0:4]
     old = affine[...]
     affine_sq = jnp.sum(old * old, axis=1, keepdims=True)
@@ -1411,6 +1459,7 @@
         gout=V((4, 2, TAPS, 4, 16, D), bf16), yrecv=V((4, TAPS, 4, 16, D), bf16),
         zs1=V((TAPS, 4, 16, D), bf16), zrecv=V((5, 3, TAPS, 16, D), bf16),
         gfin=V((TAPS, 4, 16, D), bf16),
+        sq_in=V((4, 8, 8, 128), f32), sq_own=V((4, 8, 128), f32), sq_acc=V((4, 8, D), f32), psq=V((2, D), f32),
         aff=V((4, 8, D), f32), gaff=V((4, 8, D), f32), gsend=V((4, 8, D), f32),
         st_in=V((17, 8, 128), f32), st_own=V((17, 8, 128), f32), st_all=V((17, 4, 8, 128), f32),
         cnt=V((8, 8, 128), f32), cntx=V((6, 8, 128), f32), cown=V((8, 128), f32),
@@ -1421,6 +1470,7 @@
         sE_in_s=dma((2,)), sE_in_r=dma((2,)), sE_s=dma((2,)), sE_r=dma((2,)),
         sC_s=dma, sC_r=dma((2,)), sF_s=dma, sF_r=dma,
         sQ_s=dma((2,)), sQ_r=dma((4, 2)), sX_s=dma, sX_r=dma((4, 2)), sM_s=dma, sM_r=dma((4,)), sP_s=dma, sP_r=dma((4,)),
+        sW_s=dma, sW_r=dma,
         sY_s=dma, sY_r=dma((4, 4)), sK_s=dma, sK_r=dma((4,)),
         sN_s=dma, sN_r=dma((4, 4)), sT_s=dma, sT_r=dma((4, 4)), sG_s=dma, sG_r=dma((4,)),
         sO_s=dma((4,)), sO_r=dma,
@@ -1450,7 +1500,7 @@
         out_specs=(hbm,) * 8,
         scratch_shapes=[
             V((TAPS, 64, D), f32), V((TAPS, 64, D), f32), V((TAPS, 4, 16, D), bf16), V((1, R, D), f32),
-            V((1, R, D), f32), V((8, D), f32), V((8, D), f32), V((4, D), f32), V((4, D), f32), dma((11,)), dma((12,)),
+            V((1, R, D), f32), V((8, D), f32), V((8, D), f32), V((4, D), f32), V((4, D), f32), dma((18,)), dma((12,)),
         ],
         compiler_params=pltpu.CompilerParams(vmem_limit_bytes=64 * 1024 * 1024),
     )(feat, ing, grads, totals, affine_grad, w_point, w_spatial, norm_params, mom_point, mom_spatial, mom_norm)

time: 210 us -> 206 us (0.981)
  Pallas kernels: 209 us -> 205 us
    pallas_call x1, Pallas kernels: 205 us -> 201 us  [train_step(): pl.pallas_call(train_kernel, out_shape=(shape((1, R, D), f32), shape((1,...]
where the time goes in v5:
time: 206 us
  Pallas kernels  205 us (100%)
    pallas_call x1, Pallas kernels, train_step(): pl.pallas_call(train_kernel, out_shape=(shape((1, R, D), f32), shape((1,...  201 us

profile of v5, /device:TPU:0, one launch (start us, length us, event | category | flops | bytes accessed | tf_op | source)
XLA Modules:
  0.0 205.9 jit_solution(3219741804087539892)
XLA Ops:
  0.6 201.4 %shard_map.152 = (f32[1,256,512]{2,1,0:T(8,128)}, f32[1,256,512]{2,1,0:T(8,128)}, bf16[10,4,16,512]{3,2,1,0:T(8,128)(2,1)}, f32[8,512]{1,0:T(8,128)}, f32[8,512]{1,0:T(8,128)}) custom-call(bf16[4,256,512]{2,1,0:T(8,128)(2,1)} %images.1, s32[1,4]{1,0:T(1,128)} %bitcast.1, f32[1,64,512]{2,1,0:T(8,128)} %w_point.3, f32[1,9,64,512]{3,2,1,0:T(8,128)} %w_spatial.3, ...), custom_call_target="tpu_custom_call" | custom-call | tf_op jit(solution)/shard_map/pallas_call | solution.py:1479
  202.0 3.7 %shard_map.153 = (f32[1,256,512]{2,1,0:T(8,128)}, f32[1,256,512]{2,1,0:T(8,128)}, f32[1,64,512]{2,1,0:T(8,128)}, f32[1,9,64,512]{3,2,1,0:T(8,128)}, f32[1,4,512]...) custom-call(f32[1,256,512]{2,1,0:T(8,128)} %get-tuple-element.13.feat, ...), custom_call_target="tpu_custom_call" | custom-call | tf_op jit(solution)/shard_map/pallas_call | solution.py:1492

commit v6 on v5

--- a/solution.py
+++ b/solution.py
@@ -619,13 +619,14 @@
                 whole_to_sibling(b, z ^ j).start()
 
     @jax.named_scope("gather_first")
-    def gather_first(b):
-        for j in range(4):
+    def gather_first(b, pieces=(0, 2, 1, 3)):
+        for j in pieces:
             zz = z ^ j
             ref = pair(b, half, zz, first)
             swap_copy(ref, ref, sA_s, sA_r.at[b, zz], first, bat).wait_recv()
             along_second(b, 1, zz).start()
-        quarter_to_sibling(b, 0).start()
+        if 3 in pieces:
+            quarter_to_sibling(b, 0).start()
 
     @jax.named_scope("gather_second")
     def gather_second(b):
@@ -638,7 +639,7 @@
         other = pl.ds(HALF * (1 - c), HALF)
         drain(W.at[b, other, :, pl.ds(0, 3)], sD_r.at[b])
 
-    for b in range(3):
+    for b in range(2):
         own_quarter(b)
         if b == 0:
             start_z(0)
@@ -735,9 +736,11 @@
 
     @jax.named_scope("forward")
     def forward(b):
-        @pl.when(c == 1)
-        def _():
-            drain(W.at[b, whole], sJ_r.at[b])
+        with jax.named_scope("whole_here"):
+
+            @pl.when(c == 1)
+            def _():
+                drain(W.at[b, whole], sJ_r.at[b])
 
         @pl.when(b == 3)
         def _():
@@ -755,24 +758,27 @@
         )
         share(b, 1, hidden)
 
+        @pl.when(b == 2)
+        def _():
+            rest_z(3)
+            gather_first(3, (0, 2))
+
+        gather_second(b)
+
         @pl.when(b == 0)
         def _():
+            gather_first(1, (1, 3))
             relay_z(2)
-            rest_z(1)
 
         @pl.when(b == 1)
         def _():
-            relay_z(3)
             gather_first(2)
             relay_whole(2)
-            start_whole(3)
 
         @pl.when(b == 2)
         def _():
-            gather_first(3)
             relay_whole(3)
 
-        gather_second(b)
         norms = aff[b]
         center, spread = moments(sums_finish(2 * b + 1))
         gi[b, 0:1] = norms[0:1] * spread
@@ -801,13 +807,18 @@
         @pl.when(b == 0)
         def _():
             relay_whole(1)
-            gather_first(1)
             own_quarter(3)
+            start_whole(2)
             start_z(3)
 
         @pl.when(b == 1)
         def _():
-            rest_z(3)
+            relay_z(3)
+            start_whole(3)
+
+        @pl.when(b == 2)
+        def _():
+            gather_first(3, (1, 3))
 
         center, spread = moments(sums_finish(2 * b + 2))
         gi[b, 1:2] = norms[2:3] * spread
@@ -820,10 +831,14 @@
 
     rest_z(0)
     relay_whole(0)
+    own_quarter(2)
+    gather_first(0, (0, 2))
+    relay_z(1)
     start_z(2)
-    gather_first(0)
-    relay_z(1)
     start_whole(1)
+    gather_first(0, (1, 3))
+    gather_first(1, (0, 2))
+    rest_z(1)
     rest_whole(0)
     psq[...] = jnp.concatenate(sums_finish(0), axis=0)
 
@@ -834,7 +849,6 @@
         @pl.when(b == 0)
         def _():
             rest_z(2)
-            start_whole(2)
 
         @pl.when(b < 3)
         def _():

time: 206 us -> 203 us (0.985)
  Pallas kernels: 205 us -> 202 us
    pallas_call x1, Pallas kernels: 201 us -> 198 us  [train_step(): pl.pallas_call(train_kernel, out_shape=(shape((1, R, D), f32), shape((1,...]
where the time goes in v6:
time: 203 us
  Pallas kernels  202 us (100%)
    pallas_call x1, Pallas kernels, train_step(): pl.pallas_call(train_kernel, out_shape=(shape((1, R, D), f32), shape((1,...  198 us

profile of v6, /device:TPU:0, one launch (start us, length us, event | category | flops | bytes accessed | tf_op | source)
XLA Modules:
  0.0 202.7 jit_solution(18182112060228045539)
XLA Ops:
  0.6 198.2 %shard_map.152 = (f32[1,256,512]{2,1,0:T(8,128)}, f32[1,256,512]{2,1,0:T(8,128)}, bf16[10,4,16,512]{3,2,1,0:T(8,128)(2,1)}, f32[8,512]{1,0:T(8,128)}, f32[8,512]{1,0:T(8,128)}) custom-call(bf16[4,256,512]{2,1,0:T(8,128)(2,1)} %images.1, s32[1,4]{1,0:T(1,128)} %bitcast.1, f32[1,64,512]{2,1,0:T(8,128)} %w_point.3, f32[1,9,64,512]{3,2,1,0:T(8,128)} %w_spatial.3, ...), custom_call_target="tpu_custom_call" | custom-call | tf_op jit(solution)/shard_map/pallas_call | solution.py:1493
  198.9 3.7 %shard_map.153 = (f32[1,256,512]{2,1,0:T(8,128)}, f32[1,256,512]{2,1,0:T(8,128)}, f32[1,64,512]{2,1,0:T(8,128)}, f32[1,9,64,512]{3,2,1,0:T(8,128)}, f32[1,4,512]...) custom-call(f32[1,256,512]{2,1,0:T(8,128)} %get-tuple-element.13.feat, ...), custom_call_target="tpu_custom_call" | custom-call | tf_op jit(solution)/shard_map/pallas_call | solution.py:1506

commit v7 on v6

--- a/solution.py
+++ b/solution.py
@@ -342,6 +342,10 @@
     return jnp.concatenate(rows[:4], axis=1), jnp.concatenate(rows[4:], axis=1)
 
 
+def fold(row):
+    return sum(row[:, i * 128 : (i + 1) * 128] for i in range(4))
+
+
 def crop_codes(places, big, total_rows):
     big_area = float(BIG_SIDE * BIG_SIDE)
     small_area = float(SMALL_SIDE * SMALL_SIDE)
@@ -1091,7 +1095,7 @@
                 sq_own.at[b], sq_in.at[s, bat], sW_s, sW_r, b, bat ^ j
             )
 
-        sq_own[b] = pack(sq_acc[b, 1:2], sq_acc[b, 0:1])
+        sq_own[b] = jnp.concatenate([fold(sq_acc[b, 1:2]), fold(sq_acc[b, 0:1])], axis=0)
 
         @pl.when(b != s)
         def _():
@@ -1306,18 +1310,18 @@
     reduce_near(0, 1)
     reduce_plane(0, 2)
     reduce_near(0, 2)
+    reduce_far(0, 0)
     reduce_plane(0, 3)
     reduce_near(0, 3)
-    reduce_far(0, 0)
     finish(2, 3)
     finish(1, 1)
     reduce_far(1, 3)
     reduce_far(0, 1)
+    finish(0, 0)
     finish(1, 2)
-    finish(1, 3)
-    finish(0, 0)
     reduce_far(0, 2)
     reduce_far(0, 3)
+    finish(1, 3)
     finish(0, 1)
     close_rest()
     finish(0, 2)
@@ -1334,7 +1338,7 @@
 
     drain(gaff.at[pl.ds(0, 3)], sO_r)
     affine_out[...] = gaff[0] + gaff[1] + gaff[2] + gaff[3]
-    squares_in = sq_in.reshape(32, 8, 128)
+    squares_in = sq_in.reshape(32, 2, 128)
 
     @pl.when(s != 3)
     def _():
@@ -1348,9 +1352,8 @@
     def _():
         drain(squares_in.at[pl.ds(0, 16)], sW_r)
 
-    gpoint_squares, gspatial_squares = unpack(jnp.sum(squares_in[...], axis=0))
     totals_out[...] = jnp.concatenate(
-        [psq[...], gpoint_squares, gspatial_squares, jnp.zeros((4, D), jnp.float32)], axis=0
+        [fold(psq[...]), jnp.sum(squares_in[...], axis=0), jnp.zeros((4, 128), jnp.float32)], axis=0
     )
 
     with jax.named_scope("close_last"):
@@ -1473,7 +1476,7 @@
         gout=V((4, 2, TAPS, 4, 16, D), bf16), yrecv=V((4, TAPS, 4, 16, D), bf16),
         zs1=V((TAPS, 4, 16, D), bf16), zrecv=V((5, 3, TAPS, 16, D), bf16),
         gfin=V((TAPS, 4, 16, D), bf16),
-        sq_in=V((4, 8, 8, 128), f32), sq_own=V((4, 8, 128), f32), sq_acc=V((4, 8, D), f32), psq=V((2, D), f32),
+        sq_in=V((4, 8, 2, 128), f32), sq_own=V((4, 2, 128), f32), sq_acc=V((4, 8, D), f32), psq=V((2, D), f32),
         aff=V((4, 8, D), f32), gaff=V((4, 8, D), f32), gsend=V((4, 8, D), f32),
         st_in=V((17, 8, 128), f32), st_own=V((17, 8, 128), f32), st_all=V((17, 4, 8, 128), f32),
         cnt=V((8, 8, 128), f32), cntx=V((6, 8, 128), f32), cown=V((8, 128), f32),
@@ -1494,7 +1497,7 @@
         train_kernel,
         out_shape=(
             shape((1, R, D), f32), shape((1, R, D), f32), shape((TAPS, 4, 16, D), bf16),
-            shape((8, D), f32), shape((8, D), f32),
+            shape((8, 128), f32), shape((8, D), f32),
         ),
         in_specs=[anywhere, smem, anywhere, anywhere, vmem, anywhere],
         out_specs=(anywhere, anywhere, anywhere, vmem, vmem),
@@ -1514,7 +1517,7 @@
         out_specs=(hbm,) * 8,
         scratch_shapes=[
             V((TAPS, 64, D), f32), V((TAPS, 64, D), f32), V((TAPS, 4, 16, D), bf16), V((1, R, D), f32),
-            V((1, R, D), f32), V((8, D), f32), V((8, D), f32), V((4, D), f32), V((4, D), f32), dma((18,)), dma((12,)),
+            V((1, R, D), f32), V((8, 128), f32), V((8, D), f32), V((4, D), f32), V((4, D), f32), dma((18,)), dma((12,)),
         ],
         compiler_params=pltpu.CompilerParams(vmem_limit_bytes=64 * 1024 * 1024),
     )(feat, ing, grads, totals, affine_grad, w_point, w_spatial, norm_params, mom_point, mom_spatial, mom_norm)

time: 203 us -> 201 us (level)
  no operation moved by 1% of the time
where the time goes in v7:
time: 201 us
  Pallas kernels  200 us (100%)
    pallas_call x1, Pallas kernels, train_step(): pl.pallas_call(train_kernel, out_shape=(shape((1, R, D), f32), shape((1,...  197 us

profile of v7, /device:TPU:0, one launch (start us, length us, event | category | flops | bytes accessed | tf_op | source)
XLA Modules:
  0.0 201.0 jit_solution(14042437579087145582)
XLA Ops:
  0.6 196.6 %shard_map.152 = (f32[1,256,512]{2,1,0:T(8,128)}, f32[1,256,512]{2,1,0:T(8,128)}, bf16[10,4,16,512]{3,2,1,0:T(8,128)(2,1)}, f32[8,128]{1,0:T(8,128)}, f32[8,512]{1,0:T(8,128)}) custom-call(bf16[4,256,512]{2,1,0:T(8,128)(2,1)} %images.1, s32[1,4]{1,0:T(1,128)} %bitcast.1, f32[1,64,512]{2,1,0:T(8,128)} %w_point.3, f32[1,9,64,512]{3,2,1,0:T(8,128)} %w_spatial.3, ...), custom_call_target="tpu_custom_call" | custom-call | tf_op jit(solution)/shard_map/pallas_call | solution.py:1496
  197.2 3.7 %shard_map.153 = (f32[1,256,512]{2,1,0:T(8,128)}, f32[1,256,512]{2,1,0:T(8,128)}, f32[1,64,512]{2,1,0:T(8,128)}, f32[1,9,64,512]{3,2,1,0:T(8,128)}, f32[1,4,512]...) custom-call(f32[1,256,512]{2,1,0:T(8,128)} %get-tuple-element.13.feat, ...), custom_call_target="tpu_custom_call" | custom-call | tf_op jit(solution)/shard_map/pallas_call | solution.py:1509

commit v8 on v7

--- a/solution.py
+++ b/solution.py
@@ -910,7 +910,7 @@
             drain(zrecv.at[pl.ds(0, 3), pl.ds(0, 2)], sN_s)
             drain(zrecv.at[pl.ds(0, 3), 2], sT_s)
 
-    CHUNKS = ((0, 3), (3, 3), (6, 3), (9, 1))
+    CHUNKS = ((0, 3), (3, 4), (7, 2), (9, 1))
     LAST = len(CHUNKS) - 1
 
     def dz_copy(b, j):
@@ -974,8 +974,9 @@
                 for v in range(4)
             ]
             grad_tap(b, k, jnp.concatenate(left, axis=1), right)
-            if k % 3 == 2:
-                y_copy(b, k // 3).start()
+            for i in range(LAST):
+                if k + 1 == sum(CHUNKS[i]):
+                    y_copy(b, i).start()
 
     @jax.named_scope("grad_point")
     def grad_point(b):

time: 201 us -> 200 us (level)
  no operation moved by 1% of the time
where the time goes in v8:
time: 200 us
  Pallas kernels  199 us (100%)
    pallas_call x1, Pallas kernels, train_step(): pl.pallas_call(train_kernel, out_shape=(shape((1, R, D), f32), shape((1,...  196 us

profile of v8, /device:TPU:0, one launch (start us, length us, event | category | flops | bytes accessed | tf_op | source)
XLA Modules:
  0.0 200.1 jit_solution(17661162682964256038)
XLA Ops:
  0.6 195.7 %shard_map.152 = (f32[1,256,512]{2,1,0:T(8,128)}, f32[1,256,512]{2,1,0:T(8,128)}, bf16[10,4,16,512]{3,2,1,0:T(8,128)(2,1)}, f32[8,128]{1,0:T(8,128)}, f32[8,512]{1,0:T(8,128)}) custom-call(bf16[4,256,512]{2,1,0:T(8,128)(2,1)} %images.1, s32[1,4]{1,0:T(1,128)} %bitcast.1, f32[1,64,512]{2,1,0:T(8,128)} %w_point.3, f32[1,9,64,512]{3,2,1,0:T(8,128)} %w_spatial.3, ...), custom_call_target="tpu_custom_call" | custom-call | tf_op jit(solution)/shard_map/pallas_call | solution.py:1497
  196.3 3.7 %shard_map.153 = (f32[1,256,512]{2,1,0:T(8,128)}, f32[1,256,512]{2,1,0:T(8,128)}, f32[1,64,512]{2,1,0:T(8,128)}, f32[1,9,64,512]{3,2,1,0:T(8,128)}, f32[1,4,512]...) custom-call(f32[1,256,512]{2,1,0:T(8,128)} %get-tuple-element.13.feat, ...), custom_call_target="tpu_custom_call" | custom-call | tf_op jit(solution)/shard_map/pallas_call | solution.py:1510
